TPU v7x, 128 devices: a whole 4x4x4 slice. The times are simulated.
128 devices in a mesh: expert: 32 (over z, y, core), shard: 4 (over x).
Axes of the slice: x: 4, y: 4, z: 4, core: 2. Of those that a mesh axis runs over, the one named last changes fastest.
Arguments:
- tokens: bfloat16 [2, 16384, 1024], P(None, ('expert', 'shard')), may hold values from -6 to 6
- cotangent: bfloat16 [2, 16384, 1024], P(None, ('expert', 'shard')), may hold values from -6 to 6
- order: int32 [2, 32, 512], P(None, 'expert'), may hold values from 0 to 511, each once within a row
- lengths: int32 [2, 32, 2], P(None, 'expert'), may hold values from 1 to 448, 512 in all within a row
- routes: int32 [2, 16384, 8], P(None, ('expert', 'shard')), may hold values from 0 to 31, as said below
- gate_weights: float32 [2, 16384, 8], P(None, ('expert', 'shard')), may hold values from 0.06 to 0.2
- capacity: int32 [32], replicated, may hold values from 24 to 48, as said below
- gain_attn: bfloat16 [1024], P('shard'), may hold values from 0.25 to 1.75
- w_query: bfloat16 [1024, 1024], P('shard'), may hold values from -0.1875 to 0.1875
- w_key: bfloat16 [1024, 512], P('shard'), may hold values from -0.1875 to 0.1875
- w_value: bfloat16 [1024, 512], P('shard'), may hold values from -0.1875 to 0.1875
- w_out: bfloat16 [1024, 1024], P('shard'), may hold values from -0.75 to 0.75
- gain_ffn: bfloat16 [1024], P('shard'), may hold values from 0.25 to 1.75
- w_gate: bfloat16 [32, 1024, 512], P('expert', None, 'shard'), may hold values from -0.1875 to 0.1875
- w_up: bfloat16 [32, 1024, 512], P('expert', None, 'shard'), may hold values from -0.1875 to 0.1875
- w_down: bfloat16 [32, 1024, 512], P('expert', None, 'shard'), may hold values from -1 to 1
Outputs:
- block_out: bfloat16 [2, 16384, 1024], P(None, ('expert', 'shard'))
- grad_tokens: bfloat16 [2, 16384, 1024], P(None, ('expert', 'shard'))
- grad_gain_attn: float32 [1024], P('shard')
- grad_query: float32 [1024, 1024], P('shard')
- grad_key: float32 [1024, 512], P('shard')
- grad_value: float32 [1024, 512], P('shard')
- output_weight_gradient: float32 [1024, 1024], P('shard')
- grad_gain_ffn: float32 [1024], P('shard')
- grad_gate: float32 [32, 1024, 512], P('expert', None, 'shard')
- grad_up: float32 [32, 1024, 512], P('expert', None, 'shard')
- grad_down: float32 [32, 1024, 512], P('expert', None, 'shard')
Inputs may be any that keep to these rules, and one draw needn't show every extreme that they name: `routes`: each token names 8 different experts; one expert, drawn from the seed, is named by every token and has capacity 48. Pairs of one device beyond an expert's capacity are dropped. Each order[m, g] names every dealt position once.
All inputs are finite; a program needn't handle non-finite values.
Results may differ from a plain program's by a relative error of at most 0.03.
Values may be sent and summed in bfloat16 or wider, within the bound.
No kernel may reach another device: no remote copies, remote signals or barrier semaphores. Data moves between devices by JAX's collectives and lax.ppermute only.
A program may use at most 192 MiB of HBM per device.

v0:
```python
import jax
import jax.numpy as jnp
from jax import lax
from jax.sharding import PartitionSpec as P

D = 1024
HEADS = 16
KV_HEADS = 8
HEAD = 64
SPECIALIST_COUNT = 32
TOPK = 8
CAP = 48


eps_norm = 1e-05
masked_score = -1e30


def normed_rows(rows, gain):
    inverse_rms = lax.rsqrt(jnp.mean(rows * rows, axis=-1, keepdims=True) + eps_norm)
    return (rows * inverse_rms * gain, inverse_rms)


def normed_back(rows, gain, inverse_rms, upstream):
    gate_scaled_rows = upstream * gain
    grad_rows = inverse_rms * gate_scaled_rows - rows * inverse_rms**3 * jnp.mean(
        gate_scaled_rows * rows, axis=-1, keepdims=True
    )
    return (grad_rows, jnp.sum(upstream * rows * inverse_rms, axis=0))


def place_pairs(routes_rows, capacity):
    chosen = routes_rows.reshape(-1)
    pair_count = chosen.shape[0]
    hits = (chosen[:, None] == jnp.arange(SPECIALIST_COUNT, dtype=jnp.int32)[None, :]).astype(
        jnp.int32
    )
    ranks = jnp.sum(hits * (jnp.cumsum(hits, axis=0) - 1), axis=1)
    limits = jnp.sum(hits * capacity[None, :], axis=1)
    slots = jnp.where(ranks < limits, chosen * CAP + ranks, SPECIALIST_COUNT * CAP)
    owning_experts = (
        jnp.full((SPECIALIST_COUNT * CAP,), pair_count, jnp.int32)
        .at[slots]
        .set(jnp.arange(pair_count, dtype=jnp.int32), mode="drop")
    )
    return (slots, owning_experts)


def group_scores(queries, keys_all, same_doc):
    grouped_queries = queries.reshape(queries.shape[0], KV_HEADS, HEADS // KV_HEADS, HEAD)
    grouped_keys = keys_all.reshape(keys_all.shape[0], KV_HEADS, HEAD)
    routing_scores_raw = jnp.einsum(
        "qgrd,kgd->grqk", grouped_queries, grouped_keys, preferred_element_type=jnp.float32
    ) * HEAD ** (-0.5)
    return jnp.where(same_doc[None, None], routing_scores_raw, masked_score)


def per_device(
    tokens,
    cotangent,
    order,
    lengths,
    routes,
    gate_weights,
    capacity,
    gain_attn,
    w_query,
    w_key,
    w_value,
    w_out,
    gain_ffn,
    w_gate,
    w_up,
    w_down,
):
    micro_count = tokens.shape[0]
    piece_list = tokens.shape[1]
    group_rows = order.shape[2]
    start_row = lax.axis_index("shard") * piece_list
    share_count = HEADS // KV_HEADS
    scale = HEAD ** (-0.5)
    given_all, cot_all = (
        lax.all_gather(tokens, "shard", axis=1, tiled=True),
        lax.all_gather(cotangent, "shard", axis=1, tiled=True),
    )
    query_full, key_full, value_full, out_full, gain_attn_full, gain_ffn_full = (
        lax.all_gather(w_query, "shard", axis=0, tiled=True),
        lax.all_gather(w_key, "shard", axis=0, tiled=True),
        lax.all_gather(w_value, "shard", axis=0, tiled=True),
        lax.all_gather(w_out, "shard", axis=0, tiled=True),
        lax.all_gather(gain_attn, "shard", axis=0, tiled=True),
        lax.all_gather(gain_ffn, "shard", axis=0, tiled=True),
    )
    gate_full, up_full, down_full = (
        lax.all_gather(w_gate, "shard", axis=2, tiled=True),
        lax.all_gather(w_up, "shard", axis=2, tiled=True),
        lax.all_gather(w_down, "shard", axis=2, tiled=True),
    )
    gain_first = gain_attn_full.astype(jnp.float32)
    gain_second = gain_ffn_full.astype(jnp.float32)
    sums_query = jnp.zeros(query_full.shape, jnp.float32)
    sums_key = jnp.zeros(key_full.shape, jnp.float32)
    sums_value = jnp.zeros(value_full.shape, jnp.float32)
    sums_out = jnp.zeros(out_full.shape, jnp.float32)
    sums_gain_first = jnp.zeros((D,), jnp.float32)
    sums_gain_second = jnp.zeros((D,), jnp.float32)
    sums_gate = jnp.zeros(gate_full.shape, jnp.float32)
    accumulated_upward = jnp.zeros(up_full.shape, jnp.float32)
    sums_down = jnp.zeros(down_full.shape, jnp.float32)
    positions = jnp.arange(group_rows, dtype=jnp.int32)
    zero_row = jnp.zeros((1, D), jnp.bfloat16)
    zero_float_row = jnp.zeros((1, D), jnp.float32)
    block_rows = []
    grad_rows_all = []
    for micro_index in range(micro_count):
        order_row = order[micro_index, 0]
        dealt_index = lax.dynamic_slice_in_dim(order_row, start_row, piece_list)
        dealt = jnp.take(given_all[micro_index], dealt_index, axis=0).astype(jnp.float32)
        cot_dealt = jnp.take(cot_all[micro_index], dealt_index, axis=0).astype(jnp.float32)
        doc_ends = jnp.cumsum(lengths[micro_index, 0])
        documents_all = jnp.sum(
            (positions[:, None] >= doc_ends[None, :-1]).astype(jnp.int32), axis=1
        )
        documents_mine = lax.dynamic_slice_in_dim(documents_all, start_row, piece_list)
        same_doc = documents_mine[:, None] == documents_all[None, :]
        first_norm, first_scale = normed_rows(dealt, gain_first)
        attn_in = first_norm.astype(jnp.bfloat16)
        queries = jnp.dot(attn_in, query_full, preferred_element_type=jnp.float32).astype(
            jnp.bfloat16
        )
        keys_mine = jnp.dot(attn_in, key_full, preferred_element_type=jnp.float32).astype(
            jnp.bfloat16
        )
        values_mine = jnp.dot(attn_in, value_full, preferred_element_type=jnp.float32).astype(
            jnp.bfloat16
        )
        keys_all, values_all = (
            lax.all_gather(keys_mine, "shard", axis=0, tiled=True),
            lax.all_gather(values_mine, "shard", axis=0, tiled=True),
        )
        routing_scores_raw = group_scores(queries, keys_all, same_doc)
        highest = jnp.max(routing_scores_raw, axis=-1, keepdims=True)
        raised = jnp.exp(routing_scores_raw - highest)
        total_mass = jnp.sum(raised, axis=-1, keepdims=True)
        probs = raised / total_mass
        log_mass = highest + jnp.log(total_mass)
        grouped_values = values_all.reshape(group_rows, KV_HEADS, HEAD)
        mixed = jnp.einsum(
            "grqk,kgd->qgrd",
            probs.astype(jnp.bfloat16),
            grouped_values,
            preferred_element_type=jnp.float32,
        )
        mixed = mixed.reshape(piece_list, HEADS * HEAD).astype(jnp.bfloat16)
        middle = dealt + jnp.dot(mixed, out_full, preferred_element_type=jnp.float32)
        second_norm, second_scale = normed_rows(middle, gain_second)
        ffn_in = second_norm.astype(jnp.bfloat16)
        slots, owning_experts = place_pairs(routes[micro_index], capacity)
        owner_rows = owning_experts // TOPK
        departing_values = jnp.take(
            jnp.concatenate([ffn_in, zero_row], axis=0), owner_rows, axis=0
        ).reshape(SPECIALIST_COUNT, CAP, D)
        received = lax.all_to_all(
            departing_values, "expert", split_axis=0, concat_axis=1, tiled=True
        )
        gate_proj = jnp.einsum(
            "erd,edf->erf", received, gate_full, preferred_element_type=jnp.float32
        )
        up_proj = jnp.einsum("erd,edf->erf", received, up_full, preferred_element_type=jnp.float32)
        hidden = (jax.nn.silu(gate_proj) * up_proj).astype(jnp.bfloat16)
        expert_out = jnp.einsum(
            "erf,edf->erd", hidden, down_full, preferred_element_type=jnp.float32
        ).astype(jnp.bfloat16)
        returned = lax.all_to_all(expert_out, "expert", split_axis=1, concat_axis=0, tiled=True)
        picked = jnp.take(
            jnp.concatenate([returned.reshape(SPECIALIST_COUNT * CAP, D), zero_row], axis=0),
            slots,
            axis=0,
        ).reshape(piece_list, TOPK, D)
        gates_here = gate_weights[micro_index]
        mixture = jnp.sum(picked.astype(jnp.float32) * gates_here[:, :, None], axis=1)
        block_rows.append((middle + mixture).astype(jnp.bfloat16))
        gate_column = jnp.concatenate([gates_here.reshape(-1), jnp.zeros((1,), jnp.float32)])
        slot_gates = jnp.take(gate_column, owning_experts)
        cot_padded = jnp.concatenate([cot_dealt, zero_float_row], axis=0)
        grad_outgoing = (
            (jnp.take(cot_padded, owner_rows, axis=0) * slot_gates[:, None])
            .astype(jnp.bfloat16)
            .reshape(SPECIALIST_COUNT, CAP, D)
        )
        grad_received, rows_in = (
            lax.all_to_all(grad_outgoing, "expert", split_axis=0, concat_axis=1, tiled=True),
            lax.all_to_all(departing_values, "expert", split_axis=0, concat_axis=1, tiled=True),
        )
        gate_back = jnp.einsum(
            "erd,edf->erf", rows_in, gate_full, preferred_element_type=jnp.float32
        )
        up_back = jnp.einsum("erd,edf->erf", rows_in, up_full, preferred_element_type=jnp.float32)
        sigmoid_gate = jax.nn.sigmoid(gate_back)
        silu_gate = gate_back * sigmoid_gate
        hidden_back = (silu_gate * up_back).astype(jnp.bfloat16)
        grad_hidden = jnp.einsum(
            "erd,edf->erf", grad_received, down_full, preferred_element_type=jnp.float32
        )
        grad_gate_proj = (
            grad_hidden * up_back * sigmoid_gate * (1.0 + gate_back * (1.0 - sigmoid_gate))
        ).astype(jnp.bfloat16)
        grad_up_proj = (grad_hidden * silu_gate).astype(jnp.bfloat16)
        sums_down = sums_down + jnp.einsum(
            "erd,erf->edf", grad_received, hidden_back, preferred_element_type=jnp.float32
        )
        sums_gate = sums_gate + jnp.einsum(
            "erd,erf->edf", rows_in, grad_gate_proj, preferred_element_type=jnp.float32
        )
        accumulated_upward = accumulated_upward + jnp.einsum(
            "erd,erf->edf", rows_in, grad_up_proj, preferred_element_type=jnp.float32
        )
        grad_buffer = jnp.einsum(
            "erf,edf->erd", grad_gate_proj, gate_full, preferred_element_type=jnp.float32
        )
        grad_buffer = (
            grad_buffer
            + jnp.einsum("erf,edf->erd", grad_up_proj, up_full, preferred_element_type=jnp.float32)
        ).astype(jnp.bfloat16)
        grad_back = lax.all_to_all(grad_buffer, "expert", split_axis=1, concat_axis=0, tiled=True)
        grad_pairs = jnp.take(
            jnp.concatenate([grad_back.reshape(SPECIALIST_COUNT * CAP, D), zero_row], axis=0),
            slots,
            axis=0,
        ).reshape(piece_list, TOPK, D)
        grad_ffn_in = jnp.sum(grad_pairs.astype(jnp.float32), axis=1)
        grad_norm_second, grad_gain_second = normed_back(
            middle, gain_second, second_scale, grad_ffn_in
        )
        sums_gain_second = sums_gain_second + grad_gain_second
        grad_middle = cot_dealt + grad_norm_second
        grad_branch = grad_middle.astype(jnp.bfloat16)
        sums_out = sums_out + jnp.einsum(
            "tm,td->md", mixed, grad_branch, preferred_element_type=jnp.float32
        )
        grad_mixed = jnp.einsum(
            "td,md->tm", grad_branch, out_full, preferred_element_type=jnp.float32
        ).astype(jnp.bfloat16)
        grad_mixed = grad_mixed.reshape(piece_list, KV_HEADS, share_count, HEAD)
        scores_again = group_scores(queries, keys_all, same_doc)
        probs_again = jnp.exp(scores_again - log_mass)
        grad_probs = jnp.einsum(
            "qgrd,kgd->grqk", grad_mixed, grouped_values, preferred_element_type=jnp.float32
        )
        grad_values_part = jnp.einsum(
            "grqk,qgrd->kgd",
            probs_again.astype(jnp.bfloat16),
            grad_mixed,
            preferred_element_type=jnp.float32,
        )
        grad_scores = (
            probs_again * (grad_probs - jnp.sum(probs_again * grad_probs, axis=-1, keepdims=True))
        ).astype(jnp.bfloat16)
        grouped_queries = queries.reshape(piece_list, KV_HEADS, share_count, HEAD)
        grouped_keys = keys_all.reshape(group_rows, KV_HEADS, HEAD)
        grad_queries = (
            jnp.einsum(
                "grqk,kgd->qgrd", grad_scores, grouped_keys, preferred_element_type=jnp.float32
            )
            * scale
        )
        grad_queries = grad_queries.astype(jnp.bfloat16).reshape(piece_list, HEADS * HEAD)
        grad_keys_part = (
            jnp.einsum(
                "grqk,qgrd->kgd", grad_scores, grouped_queries, preferred_element_type=jnp.float32
            )
            * scale
        )
        grad_keys, grad_values = (
            lax.psum_scatter(
                grad_keys_part.reshape(group_rows, KV_HEADS * HEAD).astype(jnp.bfloat16),
                "shard",
                scatter_dimension=0,
                tiled=True,
            ).astype(jnp.float32),
            lax.psum_scatter(
                grad_values_part.reshape(group_rows, KV_HEADS * HEAD).astype(jnp.bfloat16),
                "shard",
                scatter_dimension=0,
                tiled=True,
            ).astype(jnp.float32),
        )
        grad_keys = grad_keys.astype(jnp.bfloat16)
        grad_values = grad_values.astype(jnp.bfloat16)
        sums_query = sums_query + jnp.einsum(
            "td,tm->dm", attn_in, grad_queries, preferred_element_type=jnp.float32
        )
        sums_key = sums_key + jnp.einsum(
            "td,tm->dm", attn_in, grad_keys, preferred_element_type=jnp.float32
        )
        sums_value = sums_value + jnp.einsum(
            "td,tm->dm", attn_in, grad_values, preferred_element_type=jnp.float32
        )
        grad_attn_in = jnp.einsum(
            "tm,dm->td", grad_queries, query_full, preferred_element_type=jnp.float32
        )
        grad_attn_in = grad_attn_in + jnp.einsum(
            "tm,dm->td", grad_keys, key_full, preferred_element_type=jnp.float32
        )
        grad_attn_in = grad_attn_in + jnp.einsum(
            "tm,dm->td", grad_values, value_full, preferred_element_type=jnp.float32
        )
        grad_norm_first, grad_gain_first = normed_back(dealt, gain_first, first_scale, grad_attn_in)
        sums_gain_first = sums_gain_first + grad_gain_first
        grad_rows_all.append((grad_middle + grad_norm_first).astype(jnp.bfloat16))
    blocks_all, grads_all = (
        lax.all_gather(jnp.stack(block_rows), "shard", axis=1, tiled=True),
        lax.all_gather(jnp.stack(grad_rows_all), "shard", axis=1, tiled=True),
    )
    given_blocks = []
    given_grads = []
    for micro_index in range(micro_count):
        inverse = jnp.zeros((group_rows,), jnp.int32).at[order[micro_index, 0]].set(positions)
        wanted = lax.dynamic_slice_in_dim(inverse, start_row, piece_list)
        given_blocks.append(jnp.take(blocks_all[micro_index], wanted, axis=0))
        given_grads.append(jnp.take(grads_all[micro_index], wanted, axis=0))
    attn_parts = (
        lax.psum_scatter(
            sums_query.astype(jnp.bfloat16), "shard", scatter_dimension=0, tiled=True
        ).astype(jnp.float32),
        lax.psum_scatter(
            sums_key.astype(jnp.bfloat16), "shard", scatter_dimension=0, tiled=True
        ).astype(jnp.float32),
        lax.psum_scatter(
            sums_value.astype(jnp.bfloat16), "shard", scatter_dimension=0, tiled=True
        ).astype(jnp.float32),
        lax.psum_scatter(
            sums_out.astype(jnp.bfloat16), "shard", scatter_dimension=0, tiled=True
        ).astype(jnp.float32),
        lax.psum_scatter(
            sums_gain_first.astype(jnp.bfloat16), "shard", scatter_dimension=0, tiled=True
        ).astype(jnp.float32),
        lax.psum_scatter(
            sums_gain_second.astype(jnp.bfloat16), "shard", scatter_dimension=0, tiled=True
        ).astype(jnp.float32),
    )
    attn_totals = (
        lax.psum(attn_parts[0].astype(jnp.bfloat16), "expert").astype(jnp.float32),
        lax.psum(attn_parts[1].astype(jnp.bfloat16), "expert").astype(jnp.float32),
        lax.psum(attn_parts[2].astype(jnp.bfloat16), "expert").astype(jnp.float32),
        lax.psum(attn_parts[3].astype(jnp.bfloat16), "expert").astype(jnp.float32),
        lax.psum(attn_parts[4].astype(jnp.bfloat16), "expert").astype(jnp.float32),
        lax.psum(attn_parts[5].astype(jnp.bfloat16), "expert").astype(jnp.float32),
    )
    expert_parts = (
        lax.psum_scatter(
            sums_gate.astype(jnp.bfloat16), "shard", scatter_dimension=2, tiled=True
        ).astype(jnp.float32),
        lax.psum_scatter(
            accumulated_upward.astype(jnp.bfloat16), "shard", scatter_dimension=2, tiled=True
        ).astype(jnp.float32),
        lax.psum_scatter(
            sums_down.astype(jnp.bfloat16), "shard", scatter_dimension=2, tiled=True
        ).astype(jnp.float32),
    )
    return (
        jnp.stack(given_blocks),
        jnp.stack(given_grads),
        attn_totals[4],
        attn_totals[0],
        attn_totals[1],
        attn_totals[2],
        attn_totals[3],
        attn_totals[5],
        expert_parts[0],
        expert_parts[1],
        expert_parts[2],
    )


def solution(mesh):
    return jax.shard_map(
        per_device,
        mesh=mesh,
        in_specs=(
            P(None, ("expert", "shard"), None),
            P(None, ("expert", "shard"), None),
            P(None, "expert", None),
            P(None, "expert", None),
            P(None, ("expert", "shard"), None),
            P(None, ("expert", "shard"), None),
            P(),
            P("shard"),
            P("shard", None),
            P("shard", None),
            P("shard", None),
            P("shard", None),
            P("shard"),
            P("expert", None, "shard"),
            P("expert", None, "shard"),
            P("expert", None, "shard"),
        ),
        out_specs=(
            P(None, ("expert", "shard"), None),
            P(None, ("expert", "shard"), None),
            P("shard"),
            P("shard", None),
            P("shard", None),
            P("shard", None),
            P("shard", None),
            P("shard"),
            P("expert", None, "shard"),
            P("expert", None, "shard"),
            P("expert", None, "shard"),
        ),
        check_vma=False,
    )
```

profile of v0, /device:TPU:1, one launch (start us, length us, event | category | flops | bytes accessed | tf_op | source)
XLA Modules:
  0.0 1272.0 jit_solution(10721992013637927414)
XLA Ops:
  59.0 17.3 %all-gather.20.cloned.1.call-done = bf16[1024,1024]{1,0:T(8,128)(2,1)} async-done(((bf16[256,1024]{1,0:T(8,128)(2,1)}), bf16[1024,1024]{1,0:T(8,128)(2,1)}) %all-gather.20.cloned.1.call-update) | async-done | bytes 2097168 | tf_op jit(solution)/shard_map/all_gather | solution.py:87
  78.6 22.5 %all-gather.18.cloned.1.call-done = bf16[1024,512]{1,0:T(8,128)(2,1)} async-done(((bf16[256,512]{1,0:T(8,128)(2,1)}), bf16[1024,512]{1,0:T(8,128)(2,1)}) %all-gather.18.cloned.1.call-update) | async-done | bytes 1048592 | tf_op jit(solution)/shard_map/all_gather | solution.py:88
  102.6 11.3 all_gather.56
  114.2 12.7 all-gather.16.cloned.1.call-done
  128.5 11.3 all_gather.54
  143.9 16.6 %all-gather.22.cloned.1.call-done = bf16[1024,1024]{1,0:T(8,128)(2,1)} async-done(((bf16[256,1024]{1,0:T(8,128)(2,1)}), bf16[1024,1024]{1,0:T(8,128)(2,1)}) %all-gather.22.cloned.1.call-update) | async-done | bytes 2097168 | tf_op jit(solution)/shard_map/all_gather | solution.py:90
  232.0 19.7 %all-gather.28.cloned.1.call-done = bf16[1,1024,512]{2,1,0:T(8,128)(2,1)} async-done(((bf16[1,1024,128]{2,1,0:T(8,128)(2,1)}), bf16[1,1024,512]{2,1,0:T(8,128)(2,1)}) %all-gather.28.cloned.1.call-update) | async-done | bytes 1048592 | tf_op jit(solution)/shard_map/all_gather | solution.py:97
  251.7 11.9 all-to-all-done.4
  269.2 11.1 all-gather.26.cloned.1.call-done
  290.9 21.6 %copy.213 = bf16[1,1536,1024]{2,0,1:T(2,128)(2,1)} copy(bf16[1,1536,1024]{2,1,0:T(8,128)(2,1)S(1)} %fusion.12) | data formatting | bytes 6291456 | tf_op jit(solution)/shard_map/convert_element_type | solution.py:173
  313.1 18.3 %reduce.1 = bf16[1536,1024]{1,0:T(8,128)(2,1)S(1)} reduce(bf16[1536,1,1024]{2,1,0:T(2,128)(2,1)} %bitcast.388, bf16[]{:T(256)} %broadcast.556), dimensions={1}, to_apply=%bitcast.379.reduce_sub_computation | reduce | bytes 6291458
  335.0 13.9 %all-to-all-start.1 = ((bf16[32,2,24576]{2,1,0:T(2,128)(2,1)}), bf16[32,2,24576]{2,1,0:T(2,128)(2,1)S(1)}, u32[]{:S(2)}, u32[]{:S(2)}) async-start(bf16[32,2,24576]{2,1,0:T(2,128)(2,1)} %reshape.996), calls=%async_computation.1 | async-start | bytes 6291456 | tf_op jit(solution)/shard_map/all_to_all | solution.py:174
  370.7 21.6 %copy.211 = bf16[1,1536,1024]{2,0,1:T(2,128)(2,1)} copy(bf16[1,1536,1024]{2,1,0:T(8,128)(2,1)S(1)} %fusion.14) | data formatting | bytes 6291456 | tf_op jit(solution)/shard_map/convert_element_type | solution.py:224
  392.3 20.0 %reduce = bf16[1536,1024]{1,0:T(8,128)(2,1)} reduce(bf16[1536,1,1024]{2,1,0:T(2,128)(2,1)} %bitcast.390, bf16[]{:T(256)} %broadcast.556), dimensions={1}, to_apply=%bitcast.377.reduce_sub_computation | reduce | bytes 6291458
  435.0 11.5 all_gather.64
  476.4 11.1 all_gather.63
  492.4 18.9 %reshape.997 = bf16[1536,1,1024]{2,1,0:T(2,128)(2,1)} reshape(bf16[32,2,24576]{2,1,0:T(2,128)(2,1)} %copy-done.14) | data formatting | bytes 6291456
  515.7 18.9 %reshape.995 = bf16[1536,1,1024]{2,1,0:T(2,128)(2,1)} reshape(bf16[32,2,24576]{2,1,0:T(2,128)(2,1)} %all-to-all-done.5) | data formatting | bytes 6291456
  582.4 33.3 %all-to-all-done.2 = bf16[32,48,1024]{2,1,0:T(8,128)(2,1)S(1)} async-done(((bf16[32,48,1024]{2,1,0:T(8,128)(2,1)}), bf16[32,48,1024]{2,1,0:T(8,128)(2,1)S(1)}, u32[]{:S(2)}, u32[]{:S(2)}) %all-to-all-start.2) | async-done | bytes 3145760 | tf_op jit(solution)/shard_map/all_to_all | solution.py:163
  626.0 21.6 %copy.212 = bf16[1,1536,1024]{2,0,1:T(2,128)(2,1)} copy(bf16[1,1536,1024]{2,1,0:T(8,128)(2,1)S(1)} %fusion.13) | data formatting | bytes 6291456 | tf_op jit(solution)/shard_map/convert_element_type | solution.py:173
  647.6 18.3 %reduce.3 = bf16[1536,1024]{1,0:T(8,128)(2,1)S(1)} reduce(bf16[1536,1,1024]{2,1,0:T(2,128)(2,1)} %bitcast.393, bf16[]{:T(256)} %broadcast.556), dimensions={1}, to_apply=%bitcast.378.reduce_sub_computation | reduce | bytes 6291458
  681.3 21.6 %copy.210 = bf16[1,1536,1024]{2,0,1:T(2,128)(2,1)} copy(bf16[1,1536,1024]{2,1,0:T(8,128)(2,1)S(1)} %fusion.15) | data formatting | bytes 6291456 | tf_op jit(solution)/shard_map/convert_element_type | solution.py:224
  703.0 18.3 %reduce.2 = bf16[1536,1024]{1,0:T(8,128)(2,1)S(1)} reduce(bf16[1536,1,1024]{2,1,0:T(2,128)(2,1)} %bitcast.389, bf16[]{:T(256)} %broadcast.556), dimensions={1}, to_apply=%bitcast.376.reduce_sub_computation | reduce | bytes 6291458
  738.4 18.9 %reshape.993 = bf16[1536,1,1024]{2,1,0:T(2,128)(2,1)} reshape(bf16[32,2,24576]{2,1,0:T(2,128)(2,1)} %all-to-all-done.3) | data formatting | bytes 6291456
  772.0 18.9 %reshape.991 = bf16[1536,1,1024]{2,1,0:T(2,128)(2,1)} reshape(bf16[32,2,24576]{2,1,0:T(2,128)(2,1)} %all-to-all-done.7) | data formatting | bytes 6291456
  916.7 23.1 %reduce-scatter.42.cloned.1.call-done = bf16[128,1024]{1,0:T(8,128)(2,1)} async-done(((bf16[512,1024]{1,0:T(8,128)(2,1)}), bf16[128,1024]{1,0:T(8,128)(2,1)}) %reduce-scatter.42.cloned.1.call-update) | async-done | bytes 262160
  942.3 23.0 %reduce-scatter.46.cloned.1.call-done = bf16[128,1024]{1,0:T(8,128)(2,1)} async-done(((bf16[512,1024]{1,0:T(8,128)(2,1)}), bf16[128,1024]{1,0:T(8,128)(2,1)}) %reduce-scatter.46.cloned.1.call-update) | async-done | bytes 262160
  974.5 66.3 %all-reduce.10 = (bf16[256]{0:T(256)(128)(2,1)S(1)}, bf16[256]{0:T(256)(128)(2,1)S(1)}) all-reduce(bf16[256]{0:T(256)(128)(2,1)S(1)} %dynamic-slice.5, bf16[256]{0:T(256)(128)(2,1)S(1)} %dynamic-slice.7), channel_id=1, replica_groups=mesh['expert'=32,'shard'=4] {'expert'}, use_global_device_ids=true, to_apply=%region_39.45 | all-reduce | flops 512 | bytes 2048 | tf_op jit(solution)/shard_map/psum | solution.py:347
  1050.3 33.3 %reduce-scatter.32.cloned.1.call-done = bf16[256,1024]{1,0:T(8,128)(2,1)} async-done(((bf16[1024,1024]{1,0:T(8,128)(2,1)}), bf16[256,1024]{1,0:T(8,128)(2,1)}) %reduce-scatter.32.cloned.1.call-update) | async-done | bytes 524304 | tf_op jit(solution)/shard_map/reduce_scatter | solution.py:332
  1083.6 31.8 %reduce-scatter.26.cloned.1.call-done = bf16[256,1024]{1,0:T(8,128)(2,1)} async-done(((bf16[1024,1024]{1,0:T(8,128)(2,1)}), bf16[256,1024]{1,0:T(8,128)(2,1)}) %reduce-scatter.26.cloned.1.call-update) | async-done | bytes 524304 | tf_op jit(solution)/shard_map/reduce_scatter | solution.py:323
  1115.4 32.8 %all-gather.34.cloned.1.call-done = bf16[2,512,1024]{2,1,0:T(8,128)(2,1)} async-done(((bf16[2,128,1024]{2,1,0:T(8,128)(2,1)}), bf16[2,512,1024]{2,1,0:T(8,128)(2,1)}) %all-gather.34.cloned.1.call-update) | async-done | bytes 2097168 | tf_op jit(solution)/shard_map/all_gather | solution.py:313
  1153.6 105.4 %all-reduce.15.cloned.1.call-done = (bf16[256,1024]{1,0:T(8,128)(2,1)}, bf16[256,512]{1,0:T(8,128)(2,1)}, bf16[256,512]{1,0:T(8,128)(2,1)}, bf16[256,1024]{1,0:T(8,128)(2,1)}) async-done(((bf16[256,1024]{1,0:T(8,128)(2,1)}, bf16[256,512]{1,0:T(8,128)(2,1)}, bf16[256,512]{1,0:T(8,128)(2,1)}, bf16[256,1024]{1,0:T(8,128)(2,1)}), (bf16[256,1024]{1,0:T(8,128)(2,1)}, bf16[256,512]{1,0:T(8,128)(2,1)}, ...) | async-done | bytes 1572880 | tf_op jit(solution)/shard_map/psum | solution.py:343
  (553 shorter events, 497.3 us)
Async XLA Ops:
  7.2 47.3 %all-gather.14.cloned.1.call-start = ((), (), s32[]{:S(2)}) async-start(), calls=%async_computation.19 | async-start | bytes 2621440 | tf_op jit(solution)/shard_map/all_gather | solution.py:83
  7.9 68.4 %all-gather.20.cloned.1.call-start = ((), (), s32[]{:S(2)}) async-start(), calls=%async_computation.22 | async-start | bytes 2621440 | tf_op jit(solution)/shard_map/all_gather | solution.py:87
  8.7 92.4 %all-gather.18.cloned.1.call-start = ((), (), s32[]{:S(2)}) async-start(), calls=%async_computation.21 | async-start | bytes 1310720 | tf_op jit(solution)/shard_map/all_gather | solution.py:88
  9.4 117.5 %all-gather.16.cloned.1.call-start = ((), (), s32[]{:S(2)}) async-start(), calls=%async_computation.20 | async-start | bytes 1310720 | tf_op jit(solution)/shard_map/all_gather | solution.py:89
  10.0 150.5 %all-gather.22.cloned.1.call-start = ((), (), s32[]{:S(2)}) async-start(), calls=%async_computation.23 | async-start | bytes 2621440 | tf_op jit(solution)/shard_map/all_gather | solution.py:90
  10.6 182.3 %all-gather.32.cloned.1.call-start = ((), (), s32[]{:S(2)}) async-start(), calls=%async_computation.28 | async-start | bytes 2621440 | tf_op jit(solution)/shard_map/all_gather | solution.py:84
  14.7 181.7 %copy-start.79 = (pred[128]{0:T(512)(128)(4,1)}, pred[128]{0:T(512)(128)(4,1)S(1)}, u32[]{:S(2)}) copy-start(pred[128]{0:T(512)(128)(4,1)S(1)} %get-tuple-element.118) | copy-start | bytes 388
  170.8 47.1 %all-to-all-start = ((bf16[32,48,1024]{2,1,0:T(8,128)(2,1)}), bf16[32,48,1024]{2,1,0:T(8,128)(2,1)}, u32[]{:S(2)}, u32[]{:S(2)}) async-start(bf16[32,48,1024]{2,1,0:T(8,128)(2,1)} %bitcast.24), calls=%async_computation | async-start | bytes 6291456 | tf_op jit(solution)/shard_map/all_to_all | solution.py:163
  178.6 47.7 %all-gather.24.cloned.1.call-start = ((), (), s32[]{:S(2)}) async-start(), calls=%async_computation.24 | async-start | bytes 1310720 | tf_op jit(solution)/shard_map/all_gather | solution.py:95
  217.9 45.8 %all-to-all-start.4 = ((bf16[32,48,1024]{2,1,0:T(8,128)(2,1)}), bf16[32,48,1024]{2,1,0:T(8,128)(2,1)S(1)}, u32[]{:S(2)}, u32[]{:S(2)}) async-start(bf16[32,48,1024]{2,1,0:T(8,128)(2,1)} %bitcast.66), calls=%async_computation.4 | async-start | bytes 6291456 | tf_op jit(solution)/shard_map/all_to_all | solution.py:192
  224.4 27.3 %all-gather.28.cloned.1.call-start = ((), (), s32[]{:S(2)}) async-start(), calls=%async_computation.26 | async-start | bytes 1310720 | tf_op jit(solution)/shard_map/all_gather | solution.py:97
  225.2 55.1 %all-gather.26.cloned.1.call-start = ((), (), s32[]{:S(2)}) async-start(), calls=%async_computation.25 | async-start | bytes 1310720 | tf_op jit(solution)/shard_map/all_gather | solution.py:96
  335.0 85.7 %all-to-all-start.1 = ((bf16[32,2,24576]{2,1,0:T(2,128)(2,1)}), bf16[32,2,24576]{2,1,0:T(2,128)(2,1)S(1)}, u32[]{:S(2)}, u32[]{:S(2)}) async-start(bf16[32,2,24576]{2,1,0:T(2,128)(2,1)} %reshape.996), calls=%async_computation.1 | async-start | bytes 6291456 | tf_op jit(solution)/shard_map/all_to_all | solution.py:174
  422.4 46.8 %all-to-all-start.5 = ((bf16[32,2,24576]{2,1,0:T(2,128)(2,1)}), bf16[32,2,24576]{2,1,0:T(2,128)(2,1)}, u32[]{:S(2)}, u32[]{:S(2)}) async-start(bf16[32,2,24576]{2,1,0:T(2,128)(2,1)} %reshape.994), calls=%async_computation.5 | async-start | bytes 6291456 | tf_op jit(solution)/shard_map/all_to_all | solution.py:225
  469.2 98.1 %all-to-all-start.6 = ((bf16[32,48,1024]{2,1,0:T(8,128)(2,1)}), bf16[32,48,1024]{2,1,0:T(8,128)(2,1)}, u32[]{:S(2)}, u32[]{:S(2)}) async-start(bf16[32,48,1024]{2,1,0:T(8,128)(2,1)} %bitcast.396), calls=%async_computation.6 | async-start | bytes 6291456 | tf_op jit(solution)/shard_map/all_to_all | solution.py:192
  567.2 48.4 %all-to-all-start.2 = ((bf16[32,48,1024]{2,1,0:T(8,128)(2,1)}), bf16[32,48,1024]{2,1,0:T(8,128)(2,1)S(1)}, u32[]{:S(2)}, u32[]{:S(2)}) async-start(bf16[32,48,1024]{2,1,0:T(8,128)(2,1)} %bitcast.53), calls=%async_computation.2 | async-start | bytes 6291456 | tf_op jit(solution)/shard_map/all_to_all | solution.py:163
  669.5 55.4 %all-to-all-start.3 = ((bf16[32,2,24576]{2,1,0:T(2,128)(2,1)}), bf16[32,2,24576]{2,1,0:T(2,128)(2,1)}, u32[]{:S(2)}, u32[]{:S(2)}) async-start(bf16[32,2,24576]{2,1,0:T(2,128)(2,1)} %reshape.992), calls=%async_computation.3 | async-start | bytes 6291456 | tf_op jit(solution)/shard_map/all_to_all | solution.py:174
  724.9 47.0 %all-to-all-start.7 = ((bf16[32,2,24576]{2,1,0:T(2,128)(2,1)}), bf16[32,2,24576]{2,1,0:T(2,128)(2,1)}, u32[]{:S(2)}, u32[]{:S(2)}) async-start(bf16[32,2,24576]{2,1,0:T(2,128)(2,1)} %reshape.990), calls=%async_computation.7 | async-start | bytes 6291456 | tf_op jit(solution)/shard_map/all_to_all | solution.py:225
  732.7 146.8 %reduce-scatter.36.cloned.1.call-start = ((), (), s32[]{:S(2)}) async-start(), calls=%async_computation.35 | async-start | bytes 655360
  738.0 144.3 %reduce-scatter.40.cloned.1.call-start = ((), (), s32[]{:S(2)}) async-start(), calls=%async_computation.37 | async-start | bytes 655360
  822.5 63.2 %reduce-scatter.34.cloned.1.call-start = ((), (), s32[]{:S(2)}) async-start(), calls=%async_computation.34 | async-start | bytes 655360
  828.7 59.8 %reduce-scatter.38.cloned.1.call-start = ((), (), s32[]{:S(2)}) async-start(), calls=%async_computation.36 | async-start | bytes 655360
  836.6 77.6 %reduce-scatter.44.cloned.1.call-start = ((), (), s32[]{:S(2)}) async-start(), calls=%async_computation.39 | async-start | bytes 1310720
  849.9 89.9 %reduce-scatter.42.cloned.1.call-start = ((), (), s32[]{:S(2)}) async-start(), calls=%async_computation.38 | async-start | bytes 1310720
  863.1 102.2 %reduce-scatter.46.cloned.1.call-start = ((), (), s32[]{:S(2)}) async-start(), calls=%async_computation.40 | async-start | bytes 1310720
  878.5 163.5 %all-gather.30.cloned.1.call-start = ((), (), s32[]{:S(2)}) async-start(), calls=%async_computation.27 | async-start | bytes 2621440 | tf_op jit(solution)/shard_map/all_gather | solution.py:312
  879.4 166.0 %reduce-scatter.30.cloned.1.call-start = ((), (), s32[]{:S(2)}) async-start(), calls=%async_computation.32 | async-start | bytes 1310720 | tf_op jit(solution)/shard_map/reduce_scatter | solution.py:329
  885.6 164.7 %reduce-scatter.28.cloned.1.call-start = ((), (), s32[]{:S(2)}) async-start(), calls=%async_computation.31 | async-start | bytes 1310720 | tf_op jit(solution)/shard_map/reduce_scatter | solution.py:326
  891.7 191.9 %reduce-scatter.32.cloned.1.call-start = ((), (), s32[]{:S(2)}) async-start(), calls=%async_computation.33 | async-start | bytes 2621440 | tf_op jit(solution)/shard_map/reduce_scatter | solution.py:332
  895.5 219.9 %reduce-scatter.26.cloned.1.call-start = ((), (), s32[]{:S(2)}) async-start(), calls=%async_computation.30 | async-start | bytes 2621440 | tf_op jit(solution)/shard_map/reduce_scatter | solution.py:323
  900.8 247.4 %all-gather.34.cloned.1.call-start = ((), (), s32[]{:S(2)}) async-start(), calls=%async_computation.29 | async-start | bytes 2621440 | tf_op jit(solution)/shard_map/all_gather | solution.py:313
  907.3 351.7 %all-reduce.15.cloned.1.call-start = ((), (), s32[]{:S(2)}) async-start(), calls=%async_computation.41 | async-start | bytes 3145728 | tf_op jit(solution)/shard_map/psum | solution.py:343
  (116 other events, 1187.1 us)
Sparse Core Ops, SparseCore 0:
  9.7 34.0 all-gather.13
  45.4 30.8 all-gather.19
  78.0 23.0 all-gather.17
  102.6 24.2 all-gather.15
  128.4 32.0 all-gather.21
  162.0 30.8 all-gather.31
  194.5 24.9 all-gather.23
  226.9 24.7 all-gather.27
  253.4 26.8 all-gather.25
  738.1 19.9 reduce-scatter.35
  822.6 17.6 reduce-scatter.39
  843.1 21.1 reduce-scatter.33
  867.2 21.1 reduce-scatter.37
  890.6 23.5 reduce-scatter.43
  916.6 23.2 reduce-scatter.41
  942.1 23.2 reduce-scatter.45
  966.9 31.9 all-gather.29
  1001.9 22.1 reduce-scatter.29
  1027.1 23.1 reduce-scatter.27
  1052.7 30.8 reduce-scatter.31
  1086.0 29.3 reduce-scatter.25
  1117.8 30.4 all-gather.33
  1152.4 106.5 all-reduce.14
where the time goes:
time: 1280 us; the launch traced here: 1270 us
  waiting for transfers between devices  436 us (34%)
  local copies, waits for them, and re-layouts  347 us (27%)
  other arithmetic  141 us (11%)
  blocking collectives  133 us (10%)
  matrix products  128 us (10%)
  starting transfers between devices  70.6 us (6%)
  between operations  17.4 us (1%)
    unnamed x268, local copies, waits for them, and re-layouts  153 us
    psum x1, waiting for transfers between devices, per_device(): lax.psum(attn_parts[0].astype(jnp.bfloat16), 'expert').astype(jnp.float32)  105 us
    unnamed x4, other arithmetic  75 us
    psum x1, blocking collectives, per_device(): lax.psum(attn_parts[4].astype(jnp.bfloat16), 'expert').astype(jnp.float32)  66.3 us
    unnamed x30, waiting for transfers between devices  52.1 us
    all_to_all x2, waiting for transfers between devices, per_device(): lax.all_to_all(departing_values, 'expert', split_axis=0, concat_axis=1, t...  44.1 us
    convert_element_type x2, local copies, waits for them, and re-layouts, per_device(): expert_out = jnp.einsum('erf,edf->erd', hidden, down_full, preferred_elem...  43.3 us
    convert_element_type x2, local copies, waits for them, and re-layouts, per_device(): grad_buffer = (grad_buffer + jnp.einsum('erf,edf->erd', grad_up_proj, up_...  43.3 us
  transfers between devices with their start and end apart: 31, of which 20 were waited for; matrix products, arithmetic and copies ran while one was open for 39% of the time, Pallas kernels for 0%

commit v1 on v0

v1 whole, which is shorter than its diff:
```python
import functools

import jax
import jax.numpy as jnp
from jax import lax
from jax.experimental import pallas as pl
from jax.experimental.pallas import tpu as pltpu
from jax.sharding import PartitionSpec as P

D = 1024
HEADS = 16
KV_HEADS = 8
HEAD = 64
F = 512
EXPERTS = 32
TOPK = 8
CAP = 48
TOK = 128
GT = 512
SHARDS = 4
SLOTS = EXPERTS * CAP
HEADS_HERE = HEADS // SHARDS
KV_HERE = KV_HEADS // SHARDS
QC = HEADS_HERE * HEAD
KC = KV_HERE * HEAD
COLS = QC + 2 * KC
ROWS_HERE = D // SHARDS

EPS = 1e-05
MASKED = -1e30
SCALE = HEAD ** (-0.5)

BF = jnp.bfloat16
F32 = jnp.float32
I32 = jnp.int32

VMEM = pl.BlockSpec(memory_space=pltpu.VMEM)
SMEM = pl.BlockSpec(memory_space=pltpu.SMEM)


def dot(a, b, ca=1, cb=0):
    return lax.dot_general(a, b, (((ca,), (cb,)), ((), ())), preferred_element_type=F32)


def shape(dims, dtype):
    return jax.ShapeDtypeStruct(dims, dtype)


def run(name, body, outs, ins, smem=(), flops=0, size=0, scratch=(), limit=56):
    return pl.pallas_call(
        body,
        out_shape=outs,
        in_specs=[SMEM if i in smem else VMEM for i in range(len(ins))],
        out_specs=[VMEM] * len(outs),
        scratch_shapes=list(scratch),
        compiler_params=pltpu.CompilerParams(vmem_limit_bytes=limit * 1024 * 1024),
        cost_estimate=pl.CostEstimate(flops=flops, bytes_accessed=size, transcendentals=0),
        name=name,
    )(*ins)


def iota(dims, axis):
    return lax.broadcasted_iota(I32, dims, axis)


def rolled_order(order_ref, x):
    rows = [(order_ref[pl.ds((x + k) & 3, 1), :] - TOK * x) & (GT - 1) for k in range(SHARDS)]
    return jnp.concatenate(rows, axis=1)


def given_by_dealt(order_ref, x, rows=GT):
    return jnp.where(iota((rows, GT), 0) == rolled_order(order_ref, x), 1.0, 0.0).astype(BF)


def stack(refs):
    return jnp.concatenate([r[...] for r in refs], axis=0)


def same_documents(x, first_length):
    across = ((iota((GT, GT), 1) + TOK * x) & (GT - 1)) >= first_length
    down = ((iota((GT, GT), 0) + TOK * x) & (GT - 1)) >= first_length
    return jnp.logical_not(jnp.logical_xor(across, down))


def pack_body(place, wq, wk, wv, ga, gf, *outs):
    x = place[0]
    gains = jnp.concatenate([ga[...], gf[...]], axis=1)
    for k in range(SHARDS):
        s = (x - k) & 3
        outs[k][0:ROWS_HERE, 0:QC] = wq[:, pl.ds(pl.multiple_of(s * QC, QC), QC)]
        outs[k][0:ROWS_HERE, QC : QC + KC] = wk[:, pl.ds(pl.multiple_of(s * KC, KC), KC)]
        outs[k][0:ROWS_HERE, QC + KC : COLS] = wv[:, pl.ds(pl.multiple_of(s * KC, KC), KC)]
        outs[k][ROWS_HERE : ROWS_HERE + 16, :] = jnp.broadcast_to(gains, (16, 2 * ROWS_HERE))


def unpack_body(place, p0, p1, p2, p3, w_out, gains_out):
    x = place[0]
    packs = (p0, p1, p2, p3)
    for k in range(SHARDS):
        s = (x + k) & 3
        w_out[pl.ds(pl.multiple_of(s * ROWS_HERE, ROWS_HERE), ROWS_HERE), :] = packs[k][
            0:ROWS_HERE, :
        ]
    rows = [p[ROWS_HERE : ROWS_HERE + 16, :].astype(F32)[0:8] for p in packs]
    for half in range(2):
        for b in range(SHARDS):
            total = jnp.zeros((8, ROWS_HERE), F32)
            for k in range(SHARDS):
                piece = rows[k][:, half * ROWS_HERE : (half + 1) * ROWS_HERE]
                total = jnp.where(((x + k) & 3) == b, piece, total)
            gains_out[half * 8 : half * 8 + 8, b * ROWS_HERE : (b + 1) * ROWS_HERE] = total


def route_body(place, order, c0, c1, c2, c3, routes, gates, cap, c01_ref, chi_ref, clo_ref, d01_ref, slot_ref, dy_ref):
    x = place[0]
    dealt_by_given = given_by_dealt(order, x)[:, 0:TOK]
    dy = dot(dealt_by_given, stack((c0, c1, c2, c3)), 0, 0).astype(BF)
    dy_ref[...] = dy
    named = iota((TOK, EXPERTS), 1)
    hits = jnp.zeros((TOK, EXPERTS), F32)
    weight = jnp.zeros((TOK, EXPERTS), F32)
    for k in range(TOPK):
        hit = routes[:, k : k + 1] == named
        hits = jnp.where(hit, 1.0, hits)
        weight = jnp.where(hit, gates[:, k : k + 1], weight)
    earlier = jnp.where(iota((TOK, TOK), 1) < iota((TOK, TOK), 0), 1.0, 0.0).astype(BF)
    ranks = dot(earlier, hits.astype(BF))
    kept = jnp.logical_and(hits > 0.0, ranks < cap[...].astype(F32))
    place_of = jnp.where(kept, ranks, -1.0).astype(BF)
    first = iota((EXPERTS, SLOTS), 0) * CAP
    slot = iota((EXPERTS, SLOTS), 1)
    spread = jnp.where(jnp.logical_and(slot >= first, slot < first + CAP), 1.0, 0.0).astype(BF)
    within = (iota((TOK, SLOTS), 1) % CAP).astype(F32)
    own = dot(place_of, spread) == within
    c01_ref[...] = jnp.where(own, 1.0, 0.0).astype(BF)
    high = weight.astype(BF)
    low = (weight - high.astype(F32)).astype(BF)
    chi_ref[...] = jnp.where(own, dot(high, spread), 0.0).astype(BF)
    clo_ref[...] = jnp.where(own, dot(low, spread), 0.0).astype(BF)
    within_t = (iota((SLOTS, TOK), 0) % CAP).astype(F32)
    own_t = dot(spread, place_of, 0, 1) == within_t
    d01 = jnp.where(own_t, 1.0, 0.0).astype(BF)
    d01_ref[...] = d01
    gate_t = jnp.where(own_t, dot(spread, high, 0, 1) + dot(spread, low, 0, 1), 0.0)
    gate_of = jnp.sum(gate_t, axis=1, keepdims=True)
    slot_ref[...] = (dot(d01, dy) * gate_of).astype(BF)


def attend_body(
    place, order, t0, t1, t2, t3, w, gains, wo, o0, o1, o2, o3, dealt_ref, xr_ref, qkv_ref, mixed_ref, mass_ref
):
    x, first_length = place[0], place[1]
    deal = given_by_dealt(order, x)
    dealt = dot(deal, stack((t0, t1, t2, t3)), 0, 0)
    dealt_ref[...] = dealt[0:TOK].astype(BF)
    scaled = dealt * lax.rsqrt(jnp.mean(dealt * dealt, axis=-1, keepdims=True) + EPS)
    xr_ref[...] = scaled.astype(BF)
    attn_in = (scaled * gains[0:1, :]).astype(BF)
    qkv = dot(attn_in, w[...]).astype(BF)
    qkv_ref[...] = qkv
    same = same_documents(x, first_length)
    heads = []
    masses = []
    for h in range(HEADS_HERE):
        g = h // (HEADS // KV_HEADS)
        q = qkv[:, h * HEAD : (h + 1) * HEAD]
        k = qkv[:, QC + g * HEAD : QC + (g + 1) * HEAD]
        v = qkv[:, QC + KC + g * HEAD : QC + KC + (g + 1) * HEAD]
        scores = jnp.where(same, dot(q, k, 1, 1) * SCALE, MASKED)
        highest = jnp.max(scores, axis=-1, keepdims=True)
        raised = jnp.exp(scores - highest)
        total = jnp.sum(raised, axis=-1, keepdims=True)
        probs = (raised * (1.0 / total)).astype(BF)
        heads.append(dot(probs, v).astype(BF))
        masses.append(jnp.broadcast_to(highest + jnp.log(total), (GT, 32)))
    mixed = jnp.concatenate(heads, axis=1)
    mixed_ref[...] = mixed
    mass_ref[...] = jnp.concatenate(masses, axis=1)
    part = dot(mixed, wo[...]).astype(BF)
    for k, out in enumerate((o0, o1, o2, o3)):
        out[...] = part[k * TOK : (k + 1) * TOK]


def leave_body(own, r1, r2, r3, dealt, gains, d01, middle_ref, rows_ref):
    middle = dealt[...].astype(F32) + (
        (own[...].astype(F32) + r1[...].astype(F32)) + (r2[...].astype(F32) + r3[...].astype(F32))
    )
    middle_ref[...] = middle
    r = lax.rsqrt(jnp.mean(middle * middle, axis=-1, keepdims=True) + EPS)
    ffn_in = (middle * r * gains[8:9, :]).astype(BF)
    rows_ref[...] = dot(d01[...], ffn_in).astype(BF)


TILE = 256


def expert_body(last, *refs):
    refs = list(refs)
    rows, grads = refs[:2]
    blocks = refs[2:6]
    refs = refs[6:]
    prev = None
    if last:
        prev, refs = refs[0], refs[1:]
    out_ref, back_ref = refs[:2]
    if last:
        own_ref, sends, (wg, wu, wd, acc) = refs[2], refs[3:6], refs[6:]
    else:
        sums_ref, (wg, wu, wd, acc) = refs[2], refs[3:]
    step = pl.program_id(0)

    @pl.when(step == 0)
    def _():
        for k in range(SHARDS):
            at = slice(k * 128, (k + 1) * 128)
            wg[:, at] = blocks[k][0]
            wu[:, at] = blocks[k][1]
            wd[:, at] = blocks[k][2]
        acc[...] = prev[...] if last else jnp.zeros(acc.shape, F32)

    row = rows[...]
    grad = grads[...]
    gate = dot(row, wg[...])
    up = dot(row, wu[...])
    sig = jax.nn.sigmoid(gate)
    silu = gate * sig
    hidden = (silu * up).astype(BF)
    out_ref[...] = dot(hidden, wd[...], 1, 1).astype(BF)
    grad_hidden = dot(grad, wd[...])
    grad_gate = (grad_hidden * up * sig * (1.0 + gate * (1.0 - sig))).astype(BF)
    grad_up = (grad_hidden * silu).astype(BF)
    back_ref[...] = (dot(grad_gate, wg[...], 1, 1) + dot(grad_up, wu[...], 1, 1)).astype(BF)
    acc[0] += dot(row, grad_gate, 0, 0)
    acc[1] += dot(row, grad_up, 0, 0)
    acc[2] += dot(grad, hidden, 0, 0)

    @pl.when(step == pl.num_programs(0) - 1)
    def _():
        if last:
            for j in range(3):
                own_ref[j] = acc[j, :, 0:128]
                for k in range(1, SHARDS):
                    sends[k - 1][j] = acc[j, :, k * 128 : (k + 1) * 128].astype(BF)
        else:
            sums_ref[...] = acc[...]


def expert_call(rows, grads, blocks, prev):
    last = prev is not None
    tiles = SLOTS // TILE
    tile = pl.BlockSpec((TILE, D), lambda i: (i, 0))

    def fixed(dims):
        return pl.BlockSpec(dims, lambda i: (0,) * len(dims), pipeline_mode=pl.Buffered(1))

    ins = [rows, grads, *blocks]
    in_specs = [tile, tile] + [fixed((3, D, 128))] * 4
    outs = [shape((SLOTS, D), BF), shape((SLOTS, D), BF)]
    out_specs = [tile, tile]
    if last:
        ins.append(prev)
        in_specs.append(fixed((3, D, F)))
        outs += [shape((3, D, 128), F32)] + [shape((3, D, 128), BF)] * 3
        out_specs += [fixed((3, D, 128))] * 4
    else:
        outs.append(shape((3, D, F), F32))
        out_specs.append(fixed((3, D, F)))
    return pl.pallas_call(
        functools.partial(expert_body, last),
        grid=(tiles,),
        in_specs=in_specs,
        out_specs=out_specs,
        out_shape=outs,
        scratch_shapes=[pltpu.VMEM((D, F), BF)] * 3 + [pltpu.VMEM((3, D, F), F32)],
        compiler_params=pltpu.CompilerParams(
            vmem_limit_bytes=56 * 1024 * 1024, dimension_semantics=("arbitrary",)
        ),
        cost_estimate=pl.CostEstimate(
            flops=18 * SLOTS * D * F, bytes_accessed=8 * SLOTS * D + 20 * D * F, transcendentals=0
        ),
        name="expert",
    )(*ins)


def returned_body(back, c01, middle, gains, dy, branch_ref, gain_ref):
    upstream = dot(c01[...], back[...])
    mid = middle[...]
    r = lax.rsqrt(jnp.mean(mid * mid, axis=-1, keepdims=True) + EPS)
    scaled = upstream * gains[8:9, :]
    grad = r * scaled - mid * (r * r * r) * jnp.mean(scaled * mid, axis=-1, keepdims=True)
    branch_ref[...] = (dy[...].astype(F32) + grad).astype(BF)
    gain_ref[...] = jnp.broadcast_to(jnp.sum(upstream * mid * r, axis=0, keepdims=True), (8, D))


def block_body(back, chi, clo, middle, out_ref):
    mixture = dot(chi[...], back[...]) + dot(clo[...], back[...])
    out_ref[...] = (middle[...] + mixture).astype(BF)


def place_body(place, order, b0, b1, b2, b3, out_ref):
    deal = given_by_dealt(order, place[0], TOK)
    out_ref[...] = dot(deal, stack((b0, b1, b2, b3))).astype(BF)


def attend_back_body(last, place, order, g0, g1, g2, g3, xr, qkv_ref, mixed, mass, w, wo, *refs):
    x, first_length = place[0], place[1]
    if last:
        prev_w, prev_o, gain0, gain1, *refs = refs
    o0, o1, o2, o3, given_ref, *refs = refs
    deal = given_by_dealt(order, x)
    branch = stack((g0, g1, g2, g3))
    given_ref[...] = dot(deal[0:TOK], branch).astype(BF)
    sum_o = dot(mixed[...], branch, 0, 0)
    grad_mixed = dot(branch, wo[...], 1, 1).astype(BF)
    qkv = qkv_ref[...]
    same = same_documents(x, first_length)
    grad_q, grad_k, grad_v = [], [], []
    for g in range(KV_HERE):
        k = qkv[:, QC + g * HEAD : QC + (g + 1) * HEAD]
        v = qkv[:, QC + KC + g * HEAD : QC + KC + (g + 1) * HEAD]
        sum_k = jnp.zeros((HEAD, GT), F32)
        sum_v = jnp.zeros((HEAD, GT), F32)
        for r in range(HEADS // KV_HEADS):
            h = g * (HEADS // KV_HEADS) + r
            q = qkv[:, h * HEAD : (h + 1) * HEAD]
            gm = grad_mixed[:, h * HEAD : (h + 1) * HEAD]
            scores = jnp.where(same, dot(q, k, 1, 1) * SCALE, MASKED)
            probs = jnp.exp(scores - mass[:, h * 32 : h * 32 + 1])
            grad_probs = dot(gm, v, 1, 1)
            sum_v += dot(gm, probs.astype(BF), 0, 0)
            weighted = probs * grad_probs
            grad_scores = weighted - probs * jnp.sum(weighted, axis=-1, keepdims=True)
            grad_scores = grad_scores.astype(BF)
            grad_q.append((dot(grad_scores, k) * SCALE).astype(BF))
            sum_k += dot(q, grad_scores, 0, 0)
        grad_k.append((sum_k * SCALE).astype(BF))
        grad_v.append(sum_v.astype(BF))
    grad_kv = jnp.concatenate(grad_k + grad_v, axis=0).astype(F32).T.astype(BF)
    grad_qkv = jnp.concatenate(grad_q + [grad_kv], axis=1)
    sum_w = dot(xr[...], grad_qkv, 0, 0)
    part = dot(grad_qkv, w[...], 1, 1).astype(BF)
    part = dot(deal, part).astype(BF)
    for k, out in enumerate((o0, o1, o2, o3)):
        out[...] = part[k * TOK : (k + 1) * TOK]
    if not last:
        sum_w_ref, sum_o_ref = refs
        sum_w_ref[...] = sum_w
        sum_o_ref[...] = sum_o
        return
    keep_ref, send_ref, all_w, all_o = refs
    c = place[2]
    all_w[...] = sum_w + prev_w[...]
    all_o[...] = sum_o + prev_o[...]
    gain = gain0[...] + gain1[...]
    for ref, half in ((keep_ref, c), (send_ref, 1 - c)):
        at = pl.ds(pl.multiple_of(half * 256, 256), 256)
        ref[0:D, :] = all_w[:, at].astype(ref.dtype)
        for j in range(2):
            at = pl.ds(pl.multiple_of(j * 512 + half * 256, 256), 256)
            ref[D + j * 256 : D + (j + 1) * 256, :] = all_o[:, at].astype(ref.dtype)
        tile = jnp.concatenate(
            [gain[0:1, b * 256 : (b + 1) * 256] for b in range(4)] + [jnp.zeros((12, 256), F32)], axis=0
        )
        for j in range(16):
            ref[6 * 256 + j * 16 : 6 * 256 + (j + 1) * 16, :] = tile.astype(ref.dtype)


def tokens_body(tokens, p0, p1, p2, p3, given, gains, out_ref):
    upstream = (p0[...].astype(F32) + p1[...].astype(F32)) + (
        p2[...].astype(F32) + p3[...].astype(F32)
    )
    v = tokens[...].astype(F32)
    r = lax.rsqrt(jnp.mean(v * v, axis=-1, keepdims=True) + EPS)
    scaled = upstream * gains[0:1, :]
    grad = r * scaled - v * (r * r * r) * jnp.mean(scaled * v, axis=-1, keepdims=True)
    out_ref[...] = (given[...].astype(F32) + grad).astype(BF)


BLOCKS = 7


def split_y_body(place, keep, got, own_ref, s1, s2, s3):
    y = place[3]
    for b in range(BLOCKS):
        for k, ref in enumerate((own_ref, s1, s2, s3)):
            at = pl.ds(pl.multiple_of(b * 256 + ((y + k) & 3) * 64, 64), 64)
            ref[b * 64 : (b + 1) * 64, :] = (keep[at, :] + got[at, :].astype(F32)).astype(ref.dtype)


def split_z_body(place, own, r1, r2, r3, own_ref, s1, s2, s3):
    z = place[4]
    for b in range(BLOCKS):
        for k, ref in enumerate((own_ref, s1, s2, s3)):
            at = pl.ds(pl.multiple_of(b * 64 + ((z + k) & 3) * 16, 16), 16)
            total = (own[at, :] + r1[at, :].astype(F32)) + (
                r2[at, :].astype(F32) + r3[at, :].astype(F32)
            )
            ref[b * 16 : (b + 1) * 16, :] = total.astype(ref.dtype)


def split_x_body(place, own, r1, r2, r3, o_ref, own_ref, s1, s2, s3):
    x = place[0]

    def total(at):
        return (own[at, :] + r1[at, :].astype(F32)) + (r2[at, :].astype(F32) + r3[at, :].astype(F32))

    gain = total(slice(96, 112))
    row = iota((16, 256), 0)
    for k, ref in enumerate((own_ref, s1, s2, s3)):
        s = (x + k) & 3
        ref[0:16, :] = total(pl.ds(pl.multiple_of(s * 16, 16), 16)).astype(ref.dtype)
        mine = jnp.sum(jnp.where(row == s, gain, 0.0), axis=0, keepdims=True)
        ref[16:32, :] = jnp.broadcast_to(mine, (16, 256)).astype(ref.dtype)
    o_ref[...] = total(slice(64, 96)).astype(BF)


def join_x_body(place, o, own, r1, r2, r3, out_ref, gain_ref):
    x = place[0]
    gain = jnp.zeros((16, 256), F32)
    for k, ref in enumerate((own, r1, r2, r3)):
        s = (x - k) & 3
        out_ref[pl.ds(pl.multiple_of(s * 16, 16), 16), :] = ref[0:16, :].astype(BF)
        gain += ref[16:32, :].astype(F32)
    out_ref[64:96, :] = o[...]
    gain_ref[...] = gain[0:8]


def join_body(index, place, own, r1, r2, r3, out_ref):
    at = place[index]
    rows = own.shape[0]
    for k, ref in enumerate((own, r1, r2, r3)):
        s = (at + k) & 3
        out_ref[pl.ds(pl.multiple_of(s * rows, rows), rows), :] = ref[...]


def weights_body(place, own, got, wq, wk, wv, gain, q_ref, k_ref, v_ref, o_ref, gain_ref):
    c = place[2]
    scale = gain[...]
    total = jnp.zeros((ROWS_HERE, 1), F32)

    def piece(ref, b):
        return jnp.concatenate(
            [ref[j * 96 + b * 16 : j * 96 + (b + 1) * 16, :] for j in range(16)], axis=0
        ).astype(F32)

    for b in range(6):
        mine, other = piece(own, b), piece(got, b)
        left = jnp.where(c == 0, mine, other)
        right = jnp.where(c == 0, other, mine)
        if b < 4:
            q_ref[:, b * QC : (b + 1) * QC] = left * scale
            k_ref[:, b * KC : (b + 1) * KC] = right[:, 0:KC] * scale
            v_ref[:, b * KC : (b + 1) * KC] = right[:, KC : 2 * KC] * scale
            total += jnp.sum(
                left * wq[:, b * QC : (b + 1) * QC].astype(F32), axis=1, keepdims=True
            )
            total += jnp.sum(
                right[:, 0:KC] * wk[:, b * KC : (b + 1) * KC].astype(F32), axis=1, keepdims=True
            )
            total += jnp.sum(
                right[:, KC : 2 * KC] * wv[:, b * KC : (b + 1) * KC].astype(F32),
                axis=1,
                keepdims=True,
            )
        else:
            o_ref[:, (b - 4) * 512 : (b - 4) * 512 + 256] = left
            o_ref[:, (b - 4) * 512 + 256 : (b - 3) * 512] = right
    gain_ref[...] = total


def from_right(v, k):
    return lax.ppermute(v, "shard", [(i, (i - k) % SHARDS) for i in range(SHARDS)])


def to_right(v, k):
    return lax.ppermute(v, "shard", [(i, (i + k) % SHARDS) for i in range(SHARDS)])


def gather_x(v):
    return [v] + [from_right(v, k) for k in (1, 2, 3)]


def scatter_x(blocks):
    return [blocks[0]] + [to_right(blocks[k], k) for k in (1, 2, 3)]


def along(v, step):
    pairs = []
    for i in range(EXPERTS):
        z, y, c = step(i // 8, (i // 2) % 4, i % 2)
        pairs.append((i, (z % 4) * 8 + (y % 4) * 2 + c % 2))
    return lax.ppermute(v, "expert", pairs)


def swap_core(v):
    return along(v, lambda z, y, c: (z, y, 1 - c))


def exchange(v):
    return lax.all_to_all(v, "expert", split_axis=0, concat_axis=0, tiled=True)


def per_device(
    tokens,
    cotangent,
    order,
    lengths,
    routes,
    gate_weights,
    capacity,
    gain_attn,
    w_query,
    w_key,
    w_value,
    w_out,
    gain_ffn,
    w_gate,
    w_up,
    w_down,
):
    micro = tokens.shape[0]
    x = lax.axis_index("shard").astype(I32)
    e = lax.axis_index("expert").astype(I32)
    places = [
        jnp.stack([x, lengths[m, 0, 0], e & 1, (e >> 1) & 3, e >> 3]) for m in range(micro)
    ]
    orders = [order[m].reshape(SHARDS, TOK) for m in range(micro)]
    cap = capacity.reshape(1, EXPERTS)

    packs = run(
        "pack",
        pack_body,
        [shape((ROWS_HERE + 16, COLS), BF)] * 4,
        [places[0], w_query, w_key, w_value, gain_attn.reshape(1, -1), gain_ffn.reshape(1, -1)],
        smem=(0,),
        size=1 << 21,
    )
    packs = [packs[0]] + [from_right_pack(packs[k], k) for k in (1, 2, 3)]
    token_rows = [gather_x(tokens[m]) for m in range(micro)]
    cot_rows = [gather_x(cotangent[m]) for m in range(micro)]
    w_qkv, gains = run(
        "unpack",
        unpack_body,
        [shape((D, COLS), BF), shape((16, D), F32)],
        [places[0], *packs],
        smem=(0,),
        size=1 << 21,
    )
    weights = jnp.concatenate([w_gate, w_up, w_down], axis=0)
    weight_blocks = gather_x(weights)

    routed, attended, left, reached = [], [], [], []
    for m in range(micro):
        routed.append(
            run(
                "route",
                route_body,
                [shape((TOK, SLOTS), BF)] * 3
                + [shape((SLOTS, TOK), BF), shape((SLOTS, D), BF), shape((TOK, D), BF)],
                [places[m], orders[m], *cot_rows[m], routes[m], gate_weights[m], cap],
                smem=(0,),
                flops=2 * SLOTS * TOK * D,
                size=6 << 20,
            )
        )
        attended.append(
            run(
                "attend",
                attend_body,
                [shape((TOK, D), BF)] * 4
                + [
                    shape((TOK, D), BF),
                    shape((GT, D), BF),
                    shape((GT, COLS), BF),
                    shape((GT, QC), BF),
                    shape((GT, 128), F32),
                ],
                [places[m], orders[m], *token_rows[m], w_qkv, gains, w_out],
                smem=(0,),
                flops=4 << 30,
                size=6 << 20,
            )
        )
    grads_in = [exchange(routed[m][4]) for m in range(micro)]
    for m in range(micro):
        parts = scatter_x(attended[m][:4])
        left.append(
            run(
                "leave",
                leave_body,
                [shape((TOK, D), F32), shape((SLOTS, D), BF)],
                [*parts, attended[m][4], gains, routed[m][3]],
                flops=2 * SLOTS * TOK * D,
                size=5 << 20,
            )
        )
        reached.append(exchange(left[m][1]))

    outs, backs, sums = [], [], None
    for m in range(micro):
        result = expert_call(reached[m], grads_in[m], weight_blocks, sums)
        outs.append(result[0])
        backs.append(exchange(result[1]))
        sums = result[2] if m < micro - 1 else result[2:]
    own = sums[0]
    others = [to_right(sums[k], k) for k in (1, 2, 3)]

    sum_w = sum_o = None
    gain_sums, grad_rows = [], []
    for m in range(micro):
        last = m == micro - 1
        branch, gain_sum = run(
            "returned",
            returned_body,
            [shape((TOK, D), BF), shape((8, D), F32)],
            [backs[m], routed[m][0], left[m][0], gains, routed[m][5]],
            flops=2 * SLOTS * TOK * D,
            size=4 << 20,
        )
        gain_sums.append(gain_sum)
        ins = [places[m], orders[m], *gather_x(branch), *attended[m][5:9], w_qkv, w_out]
        out_shapes = [shape((TOK, D), BF)] * 5
        scratch = []
        if last:
            ins += [sum_w, sum_o, *gain_sums]
            out_shapes += [shape((BLOCKS * 256, 256), F32), shape((BLOCKS * 256, 256), BF)]
            scratch = [pltpu.VMEM((D, COLS), F32), pltpu.VMEM((ROWS_HERE, D), F32)]
        else:
            out_shapes += [shape((D, COLS), F32), shape((ROWS_HERE, D), F32)]
        result = run(
            "attend_back",
            functools.partial(attend_back_body, last),
            out_shapes,
            ins,
            smem=(0,),
            flops=8 << 30,
            size=12 << 20,
            scratch=scratch,
        )
        sum_w, sum_o = result[5:7]
        parts = scatter_x(result[:4])
        grad_rows.append(
            run(
                "tokens",
                tokens_body,
                [shape((TOK, D), BF)],
                [tokens[m], *parts, result[4], gains],
                size=2 << 20,
            )[0]
        )

    place = places[0]
    four = [0, 1, 2, 3]
    got = swap_core(sum_o)
    rows = BLOCKS * 64
    pieces = run(
        "split_y",
        split_y_body,
        [shape((rows, 256), F32)] + [shape((rows, 256), BF)] * 3,
        [place, sum_w, got],
        smem=(0,),
        size=4 << 20,
    )
    pieces = [pieces[0]] + [along(pieces[k], lambda z, y, c, k=k: (z, y + k, c)) for k in four[1:]]
    rows = BLOCKS * 16
    pieces = run(
        "split_z",
        split_z_body,
        [shape((rows, 256), F32)] + [shape((rows, 256), BF)] * 3,
        [place, *pieces],
        smem=(0,),
        size=1 << 20,
    )
    pieces = [pieces[0]] + [along(pieces[k], lambda z, y, c, k=k: (z + k, y, c)) for k in four[1:]]
    o_piece, *pieces = run(
        "split_x",
        split_x_body,
        [shape((32, 256), BF), shape((32, 256), F32)] + [shape((32, 256), BF)] * 3,
        [place, *pieces],
        smem=(0,),
        size=1 << 18,
    )
    piece, gain_ffn_sum = run(
        "join_x",
        join_x_body,
        [shape((96, 256), BF), shape((8, 256), F32)],
        [place, o_piece, *scatter_x(pieces)],
        smem=(0,),
        size=1 << 18,
    )
    for name, index, step in (
        ("join_z", 4, lambda z, y, c, k: (z - k, y, c)),
        ("join_y", 3, lambda z, y, c, k: (z, y - k, c)),
    ):
        pieces = [piece] + [
            along(piece, lambda z, y, c, k=k, step=step: step(z, y, c, k)) for k in four[1:]
        ]
        piece = run(
            name,
            functools.partial(join_body, index),
            [shape((4 * piece.shape[0], 256), BF)],
            [place, *pieces],
            smem=(0,),
            size=1 << 20,
        )[0]
    grad_query, grad_key, grad_value, grad_out, grad_gain = run(
        "weights",
        weights_body,
        [
            shape(w_query.shape, F32),
            shape(w_key.shape, F32),
            shape(w_value.shape, F32),
            shape(w_out.shape, F32),
            shape((ROWS_HERE, 1), F32),
        ],
        [
            place,
            piece,
            swap_core(piece),
            w_query,
            w_key,
            w_value,
            gain_attn.astype(F32).reshape(-1, 1),
        ],
        smem=(0,),
        size=6 << 20,
    )

    blocks = []
    for m in range(micro):
        returned = exchange(outs[m])
        block = run(
            "block",
            block_body,
            [shape((TOK, D), BF)],
            [returned, routed[m][1], routed[m][2], left[m][0]],
            flops=4 * SLOTS * TOK * D,
            size=5 << 20,
        )[0]
        blocks.append(
            run(
                "place",
                place_body,
                [shape((TOK, D), BF)],
                [places[m], orders[m], *gather_x(block)],
                smem=(0,),
                size=2 << 20,
            )[0]
        )

    totals = own
    for other in others:
        totals = totals + other.astype(F32)
    return (
        jnp.stack(blocks),
        jnp.stack(grad_rows),
        grad_gain.reshape(-1),
        grad_query,
        grad_key,
        grad_value,
        grad_out,
        gain_ffn_sum[0],
        totals[0:1],
        totals[1:2],
        totals[2:3],
    )


def from_right_pack(v, k):
    return from_right(v, k)


def solution(mesh):
    return jax.shard_map(
        per_device,
        mesh=mesh,
        in_specs=(
            P(None, ("expert", "shard"), None),
            P(None, ("expert", "shard"), None),
            P(None, "expert", None),
            P(None, "expert", None),
            P(None, ("expert", "shard"), None),
            P(None, ("expert", "shard"), None),
            P(),
            P("shard"),
            P("shard", None),
            P("shard", None),
            P("shard", None),
            P("shard", None),
            P("shard"),
            P("expert", None, "shard"),
            P("expert", None, "shard"),
            P("expert", None, "shard"),
        ),
        out_specs=(
            P(None, ("expert", "shard"), None),
            P(None, ("expert", "shard"), None),
            P("shard"),
            P("shard", None),
            P("shard", None),
            P("shard", None),
            P("shard", None),
            P("shard"),
            P("expert", None, "shard"),
            P("expert", None, "shard"),
            P("expert", None, "shard"),
        ),
        check_vma=False,
    )
```

time: 1280 us -> 581 us (0.45)
  the two profiles are of different devices: /device:TPU:1 before, /device:TPU:2 now
where the time goes in v1:
time: 581 us; the launch traced here: 572 us
  starting transfers between devices  175 us (30%)
  waiting for transfers between devices  162 us (28%)
  Pallas kernels  147 us (25%)
  blocking collectives  44.8 us (8%)
  local copies, waits for them, and re-layouts  34.9 us (6%)
  other arithmetic  6.77 us (1%)
    pallas_call x25, Pallas kernels, run(): pl.pallas_call(body, out_shape=outs, in_specs=[SMEM if i in smem else VME...  98.1 us
    all_to_all x7, waiting for transfers between devices, exchange(): return lax.all_to_all(v, 'expert', split_axis=0, concat_axis=0, tiled=True)  63 us
    ppermute x30, waiting for transfers between devices, from_right(): lax.ppermute(v, 'shard', [(i, (i - k) % SHARDS) for i in range(SHARDS)])  60.5 us
    ppermute x30, starting transfers between devices, from_right(): lax.ppermute(v, 'shard', [(i, (i - k) % SHARDS) for i in range(SHARDS)])  59.6 us
    pallas_call x2, Pallas kernels, expert_call(): pl.pallas_call(functools.partial(expert_body, last), grid=(tiles,), in_sp...  49.2 us
    ppermute x18, starting transfers between devices, to_right(): lax.ppermute(v, 'shard', [(i, (i + k) % SHARDS) for i in range(SHARDS)])  47.7 us
    all_to_all x1, blocking collectives, exchange(): return lax.all_to_all(v, 'expert', split_axis=0, concat_axis=0, tiled=True)  44.8 us
    all_to_all x7, starting transfers between devices, exchange(): return lax.all_to_all(v, 'expert', split_axis=0, concat_axis=0, tiled=True)  44.1 us
  transfers between devices with their start and end apart: 69, of which 34 were waited for; matrix products, arithmetic and copies ran while one was open for 4% of the time, Pallas kernels for 24%

profile of v1, /device:TPU:2, one launch (start us, length us, event | category | flops | bytes accessed | tf_op | source)
XLA Modules:
  0.0 572.0 jit_solution(14057397412041729235)
XLA Ops:
  18.1 5.2 route.3
  23.3 8.4 %all-to-all-start.4 = ((bf16[32,48,1024]{2,1,0:T(8,128)(2,1)}), bf16[32,48,1024]{2,1,0:T(8,128)(2,1)S(1)}, u32[]{:S(2)}, u32[]{:S(2)}) async-start(bf16[32,48,1024]{2,1,0:T(8,128)(2,1)} %bitcast.52), calls=%async_computation.4 | async-start | bytes 6291456 | tf_op jit(solution)/shard_map/all_to_all | solution.py:500
  43.9 4.4 collective-permute-done.9.c1
  48.3 5.2 route.2
  53.5 20.0 %all-to-all-done.4 = bf16[32,48,1024]{2,1,0:T(8,128)(2,1)S(1)} async-done(((bf16[32,48,1024]{2,1,0:T(8,128)(2,1)}), bf16[32,48,1024]{2,1,0:T(8,128)(2,1)S(1)}, u32[]{:S(2)}, u32[]{:S(2)}) %all-to-all-start.4) | async-done | bytes 3145760 | tf_op jit(solution)/shard_map/all_to_all | solution.py:500
  75.2 4.8 all-to-all-start.1
  92.5 12.6 %collective-permute-start = (bf16[128,1024]{1,0:T(8,128)(2,1)S(1)}, bf16[128,1024]{1,0:T(8,128)(2,1)S(1)}, u32[]{:S(2)}, u32[]{:S(2)}) collective-permute-start(bf16[128,1024]{1,0:T(8,128)(2,1)S(1)} %get-tuple-element.190.t0.tokens), channel_id=1, source_target_pairs={{0,3},{1,0},{2,1},{3,2},{4,7},{5,4},{6,5},{7,6},{8,11},{9,8},{10,9... | collective-permute-start | bytes 786440 | tf_op jit(solution)/shard_map/ppermute | solution.py:472
  111.0 7.0 %attend.2 = (bf16[128,1024]{1,0:T(8,128)(2,1)}, bf16[128,1024]{1,0:T(8,128)(2,1)}, bf16[128,1024]{1,0:T(8,128)(2,1)}, bf16[128,1024]{1,0:T(8,128)(2,1)}, bf16[12...) custom-call(s32[5]{0:T(128)} %stack.44.place, ...), custom_call_target="tpu_custom_call" | custom-call | flops 4294967296 | bytes 6291456 | tf_op jit(solution)/shard_map/attend/pallas_call | solution.py:50
  135.7 4.4 leave.2
  140.1 7.4 %all-to-all-start = ((bf16[32,48,1024]{2,1,0:T(8,128)(2,1)}), bf16[32,48,1024]{2,1,0:T(8,128)(2,1)S(1)}, u32[]{:S(2)}, u32[]{:S(2)}) async-start(bf16[32,48,1024]{2,1,0:T(8,128)(2,1)} %bitcast.50), calls=%async_computation | async-start | bytes 6291456 | tf_op jit(solution)/shard_map/all_to_all | solution.py:500
  158.9 4.6 collective-permute-done.18.t1
  164.2 7.1 %attend.3 = (bf16[128,1024]{1,0:T(8,128)(2,1)}, bf16[128,1024]{1,0:T(8,128)(2,1)}, bf16[128,1024]{1,0:T(8,128)(2,1)}, bf16[128,1024]{1,0:T(8,128)(2,1)}, bf16[12...) custom-call(s32[5]{0:T(128)} %stack.46.place, ...), custom_call_target="tpu_custom_call" | custom-call | flops 4294967296 | bytes 6291456 | tf_op jit(solution)/shard_map/attend/pallas_call | solution.py:50
  171.9 4.3 collective-permute-start.22
  188.4 4.3 leave.3
  194.4 7.3 %all-to-all-start.3 = ((bf16[32,48,1024]{2,1,0:T(8,128)(2,1)}), bf16[32,48,1024]{2,1,0:T(8,128)(2,1)}, u32[]{:S(2)}, u32[]{:S(2)}) async-start(bf16[32,48,1024]{2,1,0:T(8,128)(2,1)} %bitcast.53), calls=%async_computation.3 | async-start | bytes 6291456 | tf_op jit(solution)/shard_map/all_to_all | solution.py:500
  209.7 14.5 %collective-permute-done.14.refs_5_ = bf16[3,1024,128]{2,1,0:T(8,128)(2,1)S(1)} collective-permute-done((bf16[3,1024,128]{2,1,0:T(8,128)(2,1)S(1)}, bf16[3,1024,128]{2,1,0:T(8,128)(2,1)S(1)}, u32[]{:S(2)}, u32[]{:S(2)}) %collective-permute-start.14) | collective-permute-done | bytes 786464 | tf_op jit(solution)/shard_map/ppermute | solution.py:472
  226.4 15.8 %collective-permute-done.12.refs_3_ = bf16[3,1024,128]{2,1,0:T(8,128)(2,1)S(1)} collective-permute-done((bf16[3,1024,128]{2,1,0:T(8,128)(2,1)S(1)}, bf16[3,1024,128]{2,1,0:T(8,128)(2,1)S(1)}, u32[]{:S(2)}, u32[]{:S(2)}) %collective-permute-start.12) | collective-permute-done | bytes 786464 | tf_op jit(solution)/shard_map/ppermute | solution.py:472
  243.1 23.9 %expert.2 = (bf16[1536,1024]{1,0:T(8,128)(2,1)}, bf16[1536,1024]{1,0:T(8,128)(2,1)}, f32[3,1024,512]{2,1,0:T(8,128)}) custom-call(bf16[1536,1024]{1,0:T(8,128)(2,1)} %bitcast.49, bf16[1536,1024]{1,0:T(8,128)(2,1)} %bitcast.14.refs_1_, bf16[3,1024,128]{2,1,0:T(8,128)(2,1)} %copy-done.33, bf16[3,1024,128]{2,1,0:T(8,128)(2,1)} %copy-done.47, ...), custom_call_target="tpu_custom_call" | custom-call | flops 14495514624 | bytes 23068672 | tf_op jit(solution)/shard_map/expert/pallas_call | solution.py:268
  267.0 7.3 %all-to-all-start.6 = ((bf16[32,48,1024]{2,1,0:T(8,128)(2,1)}), bf16[32,48,1024]{2,1,0:T(8,128)(2,1)S(1)}, u32[]{:S(2)}, u32[]{:S(2)}) async-start(bf16[32,48,1024]{2,1,0:T(8,128)(2,1)} %bitcast.54), calls=%async_computation.6 | async-start | bytes 6291456 | tf_op jit(solution)/shard_map/all_to_all | solution.py:500
  274.3 25.3 %expert.3 = (bf16[1536,1024]{1,0:T(8,128)(2,1)}, bf16[1536,1024]{1,0:T(8,128)(2,1)}, f32[3,1024,128]{2,1,0:T(8,128)}, bf16[3,1024,128]{2,1,0:T(8,128)(2,1)}, bf1...) custom-call(bf16[1536,1024]{1,0:T(8,128)(2,1)} %bitcast.25.refs_0_, bf16[1536,1024]{1,0:T(8,128)(2,1)} %bitcast.47, ...), custom_call_target="tpu_custom_call" | custom-call | flops 14495514624 | bytes 23068672 | tf_op jit(solution)/shard_map/expert/pallas_call | solution.py:268
  299.6 16.5 %all-to-all-done.6 = bf16[32,48,1024]{2,1,0:T(8,128)(2,1)S(1)} async-done(((bf16[32,48,1024]{2,1,0:T(8,128)(2,1)}), bf16[32,48,1024]{2,1,0:T(8,128)(2,1)S(1)}, u32[]{:S(2)}, u32[]{:S(2)}) %all-to-all-start.6) | async-done | bytes 3145760 | tf_op jit(solution)/shard_map/all_to_all | solution.py:500
  316.1 44.8 %all_to_all.88 = bf16[32,48,1024]{2,1,0:T(8,128)(2,1)} all-to-all(bf16[32,48,1024]{2,1,0:T(8,128)(2,1)} %bitcast.55), channel_id=1, replica_groups=mesh['expert'=32,'shard'=4] {'expert'}, dimensions={0} | all-to-all | bytes 6291456 | tf_op jit(solution)/shard_map/all_to_all | solution.py:500
  360.8 4.1 all-to-all-start.2
  380.2 26.5 %all-to-all-done.2 = bf16[32,48,1024]{2,1,0:T(8,128)(2,1)S(1)} async-done(((bf16[32,48,1024]{2,1,0:T(8,128)(2,1)}), bf16[32,48,1024]{2,1,0:T(8,128)(2,1)S(1)}, u32[]{:S(2)}, u32[]{:S(2)}) %all-to-all-start.2) | async-done | bytes 3145760 | tf_op jit(solution)/shard_map/all_to_all | solution.py:500
  408.4 4.8 all-to-all-start.5
  415.6 9.3 %attend_back.2 = (bf16[128,1024]{1,0:T(8,128)(2,1)}, bf16[128,1024]{1,0:T(8,128)(2,1)}, bf16[128,1024]{1,0:T(8,128)(2,1)}, bf16[128,1024]{1,0:T(8,128)(2,1)}, bf...) custom-call(s32[5]{0:T(128)} %stack.44.place, s32[4,128]{1,0:T(4,128)} %bitcast.70, ...), custom_call_target="tpu_custom_call" | custom-call | flops 8589934592 | bytes 12582912 | tf_op jit(solution)/shard_map/attend_back/pallas_call | solution.py:50
  425.6 10.9 %attend_back.3 = (bf16[128,1024]{1,0:T(8,128)(2,1)}, bf16[128,1024]{1,0:T(8,128)(2,1)}, bf16[128,1024]{1,0:T(8,128)(2,1)}, bf16[128,1024]{1,0:T(8,128)(2,1)}, bf...) custom-call(s32[5]{0:T(128)} %stack.46.place, s32[4,128]{1,0:T(4,128)} %bitcast.66, ...), custom_call_target="tpu_custom_call" | custom-call | flops 8589934592 | bytes 12582912 | tf_op jit(solution)/shard_map/attend_back/pallas_call | solution.py:50
  436.6 4.4 collective-permute-start.60
  450.6 5.1 collective-permute-done.43.r1
  458.0 4.2 collective-permute-done.44.r2
  532.3 5.3 collective-permute-start.35
  541.9 6.3 %collective-permute-start.41 = (bf16[128,1024]{1,0:T(8,128)(2,1)S(1)}, bf16[128,1024]{1,0:T(8,128)(2,1)S(1)}, u32[]{:S(2)}, u32[]{:S(2)}) collective-permute-start(bf16[128,1024]{1,0:T(8,128)(2,1)S(1)} %copy-done.49), channel_id=1, source_target_pairs={{0,3},{1,0},{2,1},{3,2},{4,7},{5,4},{6,5},{7,6},{8,11},{9,8},{10,9... | collective-permute-start | bytes 786440 | tf_op jit(solution)/shard_map/ppermute | solution.py:476
  (289 shorter events, 234.5 us)
Async XLA Ops:
  23.3 50.2 %all-to-all-start.4 = ((bf16[32,48,1024]{2,1,0:T(8,128)(2,1)}), bf16[32,48,1024]{2,1,0:T(8,128)(2,1)S(1)}, u32[]{:S(2)}, u32[]{:S(2)}) async-start(bf16[32,48,1024]{2,1,0:T(8,128)(2,1)} %bitcast.52), calls=%async_computation.4 | async-start | bytes 6291456 | tf_op jit(solution)/shard_map/all_to_all | solution.py:500
  75.2 64.9 %all-to-all-start.1 = ((bf16[32,48,1024]{2,1,0:T(8,128)(2,1)}), bf16[32,48,1024]{2,1,0:T(8,128)(2,1)}, u32[]{:S(2)}, u32[]{:S(2)}) async-start(bf16[32,48,1024]{2,1,0:T(8,128)(2,1)} %bitcast.48), calls=%async_computation.1 | async-start | bytes 6291456 | tf_op jit(solution)/shard_map/all_to_all | solution.py:500
  84.3 20.8 %collective-permute-start.4 = (bf16[272,512]{1,0:T(8,128)(2,1)}, bf16[272,512]{1,0:T(8,128)(2,1)S(1)}, u32[]{:S(2)}, u32[]{:S(2)}) collective-permute-start(bf16[272,512]{1,0:T(8,128)(2,1)} %get-tuple-element.100), channel_id=1, source_target_pairs={{0,2},{1,3},{2,0},{3,1},{4,6},{5,7},{6,4},{7,5},{8,10},{9,11},{10,... | collective-permute-start | bytes 835592 | tf_op jit(solution)/shard_map/ppermute | solution.py:472
  86.2 18.9 %collective-permute-start.5 = (bf16[272,512]{1,0:T(8,128)(2,1)}, bf16[272,512]{1,0:T(8,128)(2,1)S(1)}, u32[]{:S(2)}, u32[]{:S(2)}) collective-permute-start(bf16[272,512]{1,0:T(8,128)(2,1)} %get-tuple-element.101), channel_id=1, source_target_pairs={{0,1},{1,2},{2,3},{3,0},{4,5},{5,6},{6,7},{7,4},{8,9},{9,10},{10,1... | collective-permute-start | bytes 835592 | tf_op jit(solution)/shard_map/ppermute | solution.py:472
  89.0 19.2 %collective-permute-start.2 = (bf16[128,1024]{1,0:T(8,128)(2,1)S(1)}, bf16[128,1024]{1,0:T(8,128)(2,1)S(1)}, u32[]{:S(2)}, u32[]{:S(2)}) collective-permute-start(bf16[128,1024]{1,0:T(8,128)(2,1)S(1)} %get-tuple-element.190.t0.tokens), channel_id=1, source_target_pairs={{0,1},{1,2},{2,3},{3,0},{4,5},{5,6},{6,7},{7,4},{8,9},{9,10},{10,1... | collective-permute-start | bytes 786440 | tf_op jit(solution)/shard_map/ppermute | solution.py:472
  89.5 18.7 %collective-permute-start.1 = (bf16[128,1024]{1,0:T(8,128)(2,1)S(1)}, bf16[128,1024]{1,0:T(8,128)(2,1)S(1)}, u32[]{:S(2)}, u32[]{:S(2)}) collective-permute-start(bf16[128,1024]{1,0:T(8,128)(2,1)S(1)} %get-tuple-element.190.t0.tokens), channel_id=1, source_target_pairs={{0,2},{1,3},{2,0},{3,1},{4,6},{5,7},{6,4},{7,5},{8,10},{9,11},{10,... | collective-permute-start | bytes 786440 | tf_op jit(solution)/shard_map/ppermute | solution.py:472
  92.5 17.8 %collective-permute-start = (bf16[128,1024]{1,0:T(8,128)(2,1)S(1)}, bf16[128,1024]{1,0:T(8,128)(2,1)S(1)}, u32[]{:S(2)}, u32[]{:S(2)}) collective-permute-start(bf16[128,1024]{1,0:T(8,128)(2,1)S(1)} %get-tuple-element.190.t0.tokens), channel_id=1, source_target_pairs={{0,3},{1,0},{2,1},{3,2},{4,7},{5,4},{6,5},{7,6},{8,11},{9,8},{10,9... | collective-permute-start | bytes 786440 | tf_op jit(solution)/shard_map/ppermute | solution.py:472
  140.1 52.6 %all-to-all-start = ((bf16[32,48,1024]{2,1,0:T(8,128)(2,1)}), bf16[32,48,1024]{2,1,0:T(8,128)(2,1)S(1)}, u32[]{:S(2)}, u32[]{:S(2)}) async-start(bf16[32,48,1024]{2,1,0:T(8,128)(2,1)} %bitcast.50), calls=%async_computation | async-start | bytes 6291456 | tf_op jit(solution)/shard_map/all_to_all | solution.py:500
  194.4 72.5 %all-to-all-start.3 = ((bf16[32,48,1024]{2,1,0:T(8,128)(2,1)}), bf16[32,48,1024]{2,1,0:T(8,128)(2,1)}, u32[]{:S(2)}, u32[]{:S(2)}) async-start(bf16[32,48,1024]{2,1,0:T(8,128)(2,1)} %bitcast.53), calls=%async_computation.3 | async-start | bytes 6291456 | tf_op jit(solution)/shard_map/all_to_all | solution.py:500
  203.8 20.4 %collective-permute-start.14 = (bf16[3,1024,128]{2,1,0:T(8,128)(2,1)S(1)}, bf16[3,1024,128]{2,1,0:T(8,128)(2,1)S(1)}, u32[]{:S(2)}, u32[]{:S(2)}) collective-permute-start(bf16[3,1024,128]{2,1,0:T(8,128)(2,1)S(1)} %constant_dynamic-update-slice_fusion.refs_2_), channel_id=1, source_target_pairs={{0,1},{1,2},{2,3},{3,0},{4,5},{5,6},{6,7},{7,4},{8,9},{9,10},{10,1... | collective-permute-start | bytes 2359304 | tf_op jit(solution)/shard_map/ppermute | solution.py:472
  204.5 22.0 %collective-permute-start.13 = (bf16[3,1024,128]{2,1,0:T(8,128)(2,1)S(1)}, bf16[3,1024,128]{2,1,0:T(8,128)(2,1)S(1)}, u32[]{:S(2)}, u32[]{:S(2)}) collective-permute-start(bf16[3,1024,128]{2,1,0:T(8,128)(2,1)S(1)} %constant_dynamic-update-slice_fusion.refs_2_), channel_id=1, source_target_pairs={{0,2},{1,3},{2,0},{3,1},{4,6},{5,7},{6,4},{7,5},{8,10},{9,11},{10,... | collective-permute-start | bytes 2359304 | tf_op jit(solution)/shard_map/ppermute | solution.py:472
  207.7 34.5 %collective-permute-start.12 = (bf16[3,1024,128]{2,1,0:T(8,128)(2,1)S(1)}, bf16[3,1024,128]{2,1,0:T(8,128)(2,1)S(1)}, u32[]{:S(2)}, u32[]{:S(2)}) collective-permute-start(bf16[3,1024,128]{2,1,0:T(8,128)(2,1)S(1)} %constant_dynamic-update-slice_fusion.refs_2_), channel_id=1, source_target_pairs={{0,3},{1,0},{2,1},{3,2},{4,7},{5,4},{6,5},{7,6},{8,11},{9,8},{10,9... | collective-permute-start | bytes 2359304 | tf_op jit(solution)/shard_map/ppermute | solution.py:472
  267.0 49.0 %all-to-all-start.6 = ((bf16[32,48,1024]{2,1,0:T(8,128)(2,1)}), bf16[32,48,1024]{2,1,0:T(8,128)(2,1)S(1)}, u32[]{:S(2)}, u32[]{:S(2)}) async-start(bf16[32,48,1024]{2,1,0:T(8,128)(2,1)} %bitcast.54), calls=%async_computation.6 | async-start | bytes 6291456 | tf_op jit(solution)/shard_map/all_to_all | solution.py:500
  360.8 45.8 %all-to-all-start.2 = ((bf16[32,48,1024]{2,1,0:T(8,128)(2,1)}), bf16[32,48,1024]{2,1,0:T(8,128)(2,1)S(1)}, u32[]{:S(2)}, u32[]{:S(2)}) async-start(bf16[32,48,1024]{2,1,0:T(8,128)(2,1)} %bitcast.51), calls=%async_computation.2 | async-start | bytes 6291456 | tf_op jit(solution)/shard_map/all_to_all | solution.py:500
  368.6 44.6 %collective-permute-start.32 = (bf16[128,1024]{1,0:T(8,128)(2,1)}, bf16[128,1024]{1,0:T(8,128)(2,1)}, u32[]{:S(2)}, u32[]{:S(2)}) collective-permute-start(bf16[128,1024]{1,0:T(8,128)(2,1)} %get-tuple-element.132.g0), channel_id=1, source_target_pairs={{0,1},{1,2},{2,3},{3,0},{4,5},{5,6},{6,7},{7,4},{8,9},{9,10},{10,1... | collective-permute-start | bytes 786440 | tf_op jit(solution)/shard_map/ppermute | solution.py:472
  369.2 46.4 %collective-permute-start.31 = (bf16[128,1024]{1,0:T(8,128)(2,1)}, bf16[128,1024]{1,0:T(8,128)(2,1)}, u32[]{:S(2)}, u32[]{:S(2)}) collective-permute-start(bf16[128,1024]{1,0:T(8,128)(2,1)} %get-tuple-element.132.g0), channel_id=1, source_target_pairs={{0,2},{1,3},{2,0},{3,1},{4,6},{5,7},{6,4},{7,5},{8,10},{9,11},{10,... | collective-permute-start | bytes 786440 | tf_op jit(solution)/shard_map/ppermute | solution.py:472
  372.9 42.7 %collective-permute-start.30 = (bf16[128,1024]{1,0:T(8,128)(2,1)}, bf16[128,1024]{1,0:T(8,128)(2,1)}, u32[]{:S(2)}, u32[]{:S(2)}) collective-permute-start(bf16[128,1024]{1,0:T(8,128)(2,1)} %get-tuple-element.132.g0), channel_id=1, source_target_pairs={{0,3},{1,0},{2,1},{3,2},{4,7},{5,4},{6,5},{7,6},{8,11},{9,8},{10,9... | collective-permute-start | bytes 786440 | tf_op jit(solution)/shard_map/ppermute | solution.py:472
  378.2 46.8 %collective-permute-start.38 = (bf16[128,1024]{1,0:T(8,128)(2,1)}, bf16[128,1024]{1,0:T(8,128)(2,1)}, u32[]{:S(2)}, u32[]{:S(2)}) collective-permute-start(bf16[128,1024]{1,0:T(8,128)(2,1)} %get-tuple-element.145.g0), channel_id=1, source_target_pairs={{0,1},{1,2},{2,3},{3,0},{4,5},{5,6},{6,7},{7,4},{8,9},{9,10},{10,1... | collective-permute-start | bytes 786440 | tf_op jit(solution)/shard_map/ppermute | solution.py:472
  378.6 46.3 %collective-permute-start.37 = (bf16[128,1024]{1,0:T(8,128)(2,1)}, bf16[128,1024]{1,0:T(8,128)(2,1)}, u32[]{:S(2)}, u32[]{:S(2)}) collective-permute-start(bf16[128,1024]{1,0:T(8,128)(2,1)} %get-tuple-element.145.g0), channel_id=1, source_target_pairs={{0,2},{1,3},{2,0},{3,1},{4,6},{5,7},{6,4},{7,5},{8,10},{9,11},{10,... | collective-permute-start | bytes 786440 | tf_op jit(solution)/shard_map/ppermute | solution.py:472
  408.4 106.6 %all-to-all-start.5 = ((bf16[32,48,1024]{2,1,0:T(8,128)(2,1)}), bf16[32,48,1024]{2,1,0:T(8,128)(2,1)}, u32[]{:S(2)}, u32[]{:S(2)}) async-start(bf16[32,48,1024]{2,1,0:T(8,128)(2,1)} %bitcast.46), calls=%async_computation.5 | async-start | bytes 6291456 | tf_op jit(solution)/shard_map/all_to_all | solution.py:500
  436.5 65.8 %collective-permute-start.59 = (bf16[3,1024,128]{2,1,0:T(8,128)(2,1)S(1)}, bf16[3,1024,128]{2,1,0:T(8,128)(2,1)S(1)}, u32[]{:S(2)}, u32[]{:S(2)}) collective-permute-start(bf16[3,1024,128]{2,1,0:T(8,128)(2,1)S(1)} %copy-done.44), channel_id=1, source_target_pairs={{0,1},{1,2},{2,3},{3,0},{4,5},{5,6},{6,7},{7,4},{8,9},{9,10},{10,1... | collective-permute-start | bytes 2359304 | tf_op jit(solution)/shard_map/ppermute | solution.py:476
  436.6 72.0 %collective-permute-start.60 = (bf16[3,1024,128]{2,1,0:T(8,128)(2,1)S(1)}, bf16[3,1024,128]{2,1,0:T(8,128)(2,1)S(1)}, u32[]{:S(2)}, u32[]{:S(2)}) collective-permute-start(bf16[3,1024,128]{2,1,0:T(8,128)(2,1)S(1)} %copy-done.43), channel_id=1, source_target_pairs={{0,2},{1,3},{2,0},{3,1},{4,6},{5,7},{6,4},{7,5},{8,10},{9,11},{10,... | collective-permute-start | bytes 2359304 | tf_op jit(solution)/shard_map/ppermute | solution.py:476
  446.5 15.7 %collective-permute-start.44 = (bf16[448,256]{1,0:T(8,128)(2,1)}, bf16[448,256]{1,0:T(8,128)(2,1)S(1)}, u32[]{:S(2)}, u32[]{:S(2)}) collective-permute-start(bf16[448,256]{1,0:T(8,128)(2,1)} %get-tuple-element.163), channel_id=1, source_target_pairs={{0,16},{4,20},{8,24},{12,28},{16,0},{20,4},{24,8},{28,12},{32,48},... | collective-permute-start | bytes 688136 | tf_op jit(solution)/shard_map/ppermute | solution.py:492
  455.8 66.7 %collective-permute-start.61 = (bf16[3,1024,128]{2,1,0:T(8,128)(2,1)}, bf16[3,1024,128]{2,1,0:T(8,128)(2,1)}, u32[]{:S(2)}, u32[]{:S(2)}) collective-permute-start(bf16[3,1024,128]{2,1,0:T(8,128)(2,1)} %get-tuple-element.184), channel_id=1, source_target_pairs={{0,3},{1,0},{2,1},{3,2},{4,7},{5,4},{6,5},{7,6},{8,11},{9,8},{10,9... | collective-permute-start | bytes 2359304 | tf_op jit(solution)/shard_map/ppermute | solution.py:476
  502.3 16.7 %collective-permute-start.55 = (bf16[384,256]{1,0:T(8,128)(2,1)}, bf16[384,256]{1,0:T(8,128)(2,1)}, u32[]{:S(2)}, u32[]{:S(2)}) collective-permute-start(bf16[384,256]{1,0:T(8,128)(2,1)} %join_z.1.own), channel_id=1, source_target_pairs={{0,24},{4,28},{8,0},{12,4},{16,8},{20,12},{24,16},{28,20},{32,56},... | collective-permute-start | bytes 589832 | tf_op jit(solution)/shard_map/ppermute | solution.py:492
  508.7 15.6 %collective-permute-start.17 = (bf16[128,1024]{1,0:T(8,128)(2,1)}, bf16[128,1024]{1,0:T(8,128)(2,1)S(1)}, u32[]{:S(2)}, u32[]{:S(2)}) collective-permute-start(bf16[128,1024]{1,0:T(8,128)(2,1)} %block.2.b0), channel_id=1, source_target_pairs={{0,1},{1,2},{2,3},{3,0},{4,5},{5,6},{6,7},{7,4},{8,9},{9,10},{10,1... | collective-permute-start | bytes 786440 | tf_op jit(solution)/shard_map/ppermute | solution.py:472
  526.4 15.5 %collective-permute-start.34 = (bf16[128,1024]{1,0:T(8,128)(2,1)}, bf16[128,1024]{1,0:T(8,128)(2,1)S(1)}, u32[]{:S(2)}, u32[]{:S(2)}) collective-permute-start(bf16[128,1024]{1,0:T(8,128)(2,1)} %get-tuple-element.139), channel_id=1, source_target_pairs={{0,2},{1,3},{2,0},{3,1},{4,6},{5,7},{6,4},{7,5},{8,10},{9,11},{10,... | collective-permute-start | bytes 786440 | tf_op jit(solution)/shard_map/ppermute | solution.py:476
  530.2 35.1 %collective-permute-start.58 = (bf16[1536,256]{1,0:T(8,128)(2,1)}, bf16[1536,256]{1,0:T(8,128)(2,1)S(1)}, u32[]{:S(2)}, u32[]{:S(2)}) collective-permute-start(bf16[1536,256]{1,0:T(8,128)(2,1)} %join_y.1.own), channel_id=1, source_target_pairs={{0,4},{4,0},{8,12},{12,8},{16,20},{20,16},{24,28},{28,24},{32,36},... | collective-permute-start | bytes 2359304 | tf_op jit(solution)/shard_map/ppermute | solution.py:492
  532.3 23.4 %collective-permute-start.35 = (bf16[128,1024]{1,0:T(8,128)(2,1)S(1)}, bf16[128,1024]{1,0:T(8,128)(2,1)S(1)}, u32[]{:S(2)}, u32[]{:S(2)}) collective-permute-start(bf16[128,1024]{1,0:T(8,128)(2,1)S(1)} %copy-done.48), channel_id=1, source_target_pairs={{0,3},{1,0},{2,1},{3,2},{4,7},{5,4},{6,5},{7,6},{8,11},{9,8},{10,9... | collective-permute-start | bytes 786440 | tf_op jit(solution)/shard_map/ppermute | solution.py:476
  537.7 21.1 %collective-permute-start.39 = (bf16[128,1024]{1,0:T(8,128)(2,1)S(1)}, bf16[128,1024]{1,0:T(8,128)(2,1)S(1)}, u32[]{:S(2)}, u32[]{:S(2)}) collective-permute-start(bf16[128,1024]{1,0:T(8,128)(2,1)S(1)} %copy-done.51), channel_id=1, source_target_pairs={{0,1},{1,2},{2,3},{3,0},{4,5},{5,6},{6,7},{7,4},{8,9},{9,10},{10,1... | collective-permute-start | bytes 786440 | tf_op jit(solution)/shard_map/ppermute | solution.py:476
  538.8 20.0 %collective-permute-start.40 = (bf16[128,1024]{1,0:T(8,128)(2,1)S(1)}, bf16[128,1024]{1,0:T(8,128)(2,1)S(1)}, u32[]{:S(2)}, u32[]{:S(2)}) collective-permute-start(bf16[128,1024]{1,0:T(8,128)(2,1)S(1)} %copy-done.50), channel_id=1, source_target_pairs={{0,2},{1,3},{2,0},{3,1},{4,6},{5,7},{6,4},{7,5},{8,10},{9,11},{10,... | collective-permute-start | bytes 786440 | tf_op jit(solution)/shard_map/ppermute | solution.py:476
  541.9 16.9 %collective-permute-start.41 = (bf16[128,1024]{1,0:T(8,128)(2,1)S(1)}, bf16[128,1024]{1,0:T(8,128)(2,1)S(1)}, u32[]{:S(2)}, u32[]{:S(2)}) collective-permute-start(bf16[128,1024]{1,0:T(8,128)(2,1)S(1)} %copy-done.49), channel_id=1, source_target_pairs={{0,3},{1,0},{2,1},{3,2},{4,7},{5,4},{6,5},{7,6},{8,11},{9,8},{10,9... | collective-permute-start | bytes 786440 | tf_op jit(solution)/shard_map/ppermute | solution.py:476
  (102 other events, 929.2 us)

commit v2 on v1

v2 whole, which is shorter than its diff:
```python
import functools

import jax
import jax.numpy as jnp
from jax import lax
from jax.experimental import pallas as pl
from jax.experimental.pallas import tpu as pltpu
from jax.sharding import PartitionSpec as P

D = 1024
HEADS = 16
KV_HEADS = 8
HEAD = 64
F = 512
EXPERTS = 32
TOPK = 8
CAP = 48
TOK = 128
GT = 512
SHARDS = 4
SLOTS = EXPERTS * CAP
HEADS_HERE = HEADS // SHARDS
KV_HERE = KV_HEADS // SHARDS
QC = HEADS_HERE * HEAD
KC = KV_HERE * HEAD
COLS = QC + 2 * KC
ROWS_HERE = D // SHARDS

EPS = 1e-05
MASKED = -1e30
SCALE = HEAD ** (-0.5)

BF = jnp.bfloat16
F32 = jnp.float32
I32 = jnp.int32

VMEM = pl.BlockSpec(memory_space=pltpu.VMEM)
SMEM = pl.BlockSpec(memory_space=pltpu.SMEM)
ANY = pl.BlockSpec(memory_space=pl.ANY)


def dot(a, b, ca=1, cb=0):
    return lax.dot_general(a, b, (((ca,), (cb,)), ((), ())), preferred_element_type=F32)


def shape(dims, dtype):
    return jax.ShapeDtypeStruct(dims, dtype)


MICROSECONDS = {
    "pack": 2.5,
    "route": 4.5,
    "deal": 2.3,
    "weight_stack": 2.0,
    "attend": 7.3,
    "leave": 4.3,
    "expert": 27.0,
    "returned": 3.7,
    "attend_back": 10.0,
    "weight_sums": 3.3,
    "split_y": 2.8,
    "split_z": 2.0,
    "split_x": 1.6,
    "join_x": 1.5,
    "join_z": 1.6,
    "join_y": 2.2,
    "block": 1.2,
    "place": 2.8,
    "tokens": 3.4,
    "weights": 3.9,
}


def cost(microseconds):
    return pl.CostEstimate(
        flops=1, bytes_accessed=int(3.6e6 * microseconds) + 1, transcendentals=0
    )


def run(name, body, outs, ins, smem=(), scratch=(), limit=56, after=()):
    count = len(ins)

    def whole(*refs):
        body(*refs[:count], *refs[count + len(after) :])

    ins = [*ins, *after]
    return pl.pallas_call(
        whole,
        out_shape=outs,
        in_specs=[SMEM if i in smem else VMEM for i in range(count)] + [ANY] * len(after),
        out_specs=[VMEM] * len(outs),
        scratch_shapes=list(scratch),
        compiler_params=pltpu.CompilerParams(vmem_limit_bytes=limit * 1024 * 1024),
        cost_estimate=cost(MICROSECONDS[name]),
        name=name,
    )(*ins)


def iota(dims, axis):
    return lax.broadcasted_iota(I32, dims, axis)


def x_of(place):
    return place[0] & 3


def core_of(place):
    return (place[0] >> 2) & 1


def y_of(place):
    return (place[0] >> 3) & 3


def z_of(place):
    return place[0] >> 5


def rolled_order(order_ref, m, x):
    rows = [
        order_ref[m, :, pl.ds(pl.multiple_of(((x + k) & 3) * TOK, TOK), TOK)] for k in range(SHARDS)
    ]
    return (jnp.concatenate(rows, axis=1) - TOK * x) & (GT - 1)


def given_by_dealt(order_ref, m, x, rows=GT):
    return jnp.where(iota((rows, GT), 0) == rolled_order(order_ref, m, x), 1.0, 0.0).astype(BF)


def stack(refs):
    return jnp.concatenate([r[...] for r in refs], axis=0)


def same_documents(x, first_length):
    across = ((iota((GT, GT), 1) + TOK * x) & (GT - 1)) >= first_length
    down = ((iota((GT, GT), 0) + TOK * x) & (GT - 1)) >= first_length
    return jnp.logical_not(jnp.logical_xor(across, down))


def pack_body(place, wq, wk, wv, gains, tokens, *outs):
    x = x_of(place)
    outs[4][...] = tokens[0]
    for k in range(SHARDS):
        s = (x - k) & 3
        outs[k][0:ROWS_HERE, 0:QC] = wq[:, pl.ds(pl.multiple_of(s * QC, QC), QC)]
        outs[k][0:ROWS_HERE, QC : QC + KC] = wk[:, pl.ds(pl.multiple_of(s * KC, KC), KC)]
        outs[k][0:ROWS_HERE, QC + KC : COLS] = wv[:, pl.ds(pl.multiple_of(s * KC, KC), KC)]
        outs[k][ROWS_HERE : ROWS_HERE + 16, :] = jnp.broadcast_to(gains[...], (16, 2 * ROWS_HERE))


def unpack(x, packs, w_out, gains_out):
    for k in range(SHARDS):
        s = (x + k) & 3
        w_out[pl.ds(pl.multiple_of(s * ROWS_HERE, ROWS_HERE), ROWS_HERE), :] = packs[k][
            0:ROWS_HERE, :
        ]
    rows = [p[ROWS_HERE : ROWS_HERE + 16, :].astype(F32)[0:8] for p in packs]
    for half in range(2):
        for b in range(SHARDS):
            total = jnp.zeros((8, ROWS_HERE), F32)
            for k in range(SHARDS):
                piece = rows[k][:, half * ROWS_HERE : (half + 1) * ROWS_HERE]
                total = jnp.where(((x + k) & 3) == b, piece, total)
            gains_out[half * 8 : half * 8 + 8, b * ROWS_HERE : (b + 1) * ROWS_HERE] = total


def route_body(micro, routes, cap, tokens, cotangent, *refs):
    for m in range(1, micro):
        refs[2 * m - 2][...] = tokens[m]
        refs[2 * m - 1][...] = cotangent[m]
    outs = refs[2 * micro - 2 :]
    named = iota((EXPERTS, TOK), 0)
    earlier = jnp.where(iota((TOK, TOK), 0) < iota((TOK, TOK), 1), 1.0, 0.0).astype(BF)
    one = iota((EXPERTS, EXPERTS), 0) == iota((EXPERTS, EXPERTS), 1)
    limit = jnp.sum(jnp.where(one, cap[...], 0).astype(F32), axis=1, keepdims=True)
    first = iota((EXPERTS, SLOTS), 0) * CAP
    slot = iota((EXPERTS, SLOTS), 1)
    spread = jnp.where(jnp.logical_and(slot >= first, slot < first + CAP), 1.0, 0.0).astype(BF)
    within = (iota((TOK, SLOTS), 1) % CAP).astype(F32)
    within_t = (iota((SLOTS, TOK), 0) % CAP).astype(F32)
    for m in range(micro):
        c01_ref, d01_ref = outs[2 * m : 2 * m + 2]
        hits = jnp.zeros((EXPERTS, TOK), F32)
        for k in range(TOPK):
            hit = routes[m, k : k + 1, :] == named
            hits = jnp.where(hit, 1.0, hits)
        ranks = dot(hits.astype(BF), earlier)
        kept = jnp.logical_and(hits > 0.0, ranks < limit)
        place_of = jnp.where(kept, ranks, -1.0).astype(BF)
        own = dot(place_of, spread, 0, 0) == within
        c01_ref[...] = jnp.where(own, 1.0, 0.0).astype(BF)
        own_t = dot(spread, place_of, 0, 0) == within_t
        d01_ref[...] = jnp.where(own_t, 1.0, 0.0).astype(BF)


NOTES = 16


def deal_body(m, place, order, routes, gates, c0, c1, c2, c3, out_ref):
    deal = given_by_dealt(order, m, x_of(place))[:, 0:TOK]
    out_ref[0:TOK, :] = dot(deal, stack((c0, c1, c2, c3)), 0, 0).astype(BF)
    experts = jnp.concatenate([routes[m, k : k + 1, :] for k in range(TOPK)], axis=1).astype(F32)
    weights = jnp.concatenate([gates[m, k : k + 1, :] for k in range(TOPK)], axis=1)
    high = weights.astype(BF).astype(F32)
    row = iota((NOTES, D), 0)
    notes = jnp.where(row == 0, experts, jnp.where(row == 1, high, weights - high))
    out_ref[TOK : TOK + NOTES, :] = notes.astype(BF)


def attend_body(m, place, lengths, order, t0, t1, t2, t3, wo, *refs):
    x, first_length = x_of(place), lengths[m, 0, 0]
    if m == 0:
        packs, refs = refs[:4], refs[4:]
        o0, o1, o2, o3, dealt_ref, xr_ref, qkv_ref, mixed_ref, mass_ref, w, gains = refs
        unpack(x, packs, w, gains)
    else:
        w, gains, o0, o1, o2, o3, dealt_ref, xr_ref, qkv_ref, mixed_ref, mass_ref = refs
    deal = given_by_dealt(order, m, x)
    dealt = dot(deal, stack((t0, t1, t2, t3)), 0, 0)
    dealt_ref[...] = dealt[0:TOK].astype(BF)
    scaled = dealt * lax.rsqrt(jnp.mean(dealt * dealt, axis=-1, keepdims=True) + EPS)
    xr_ref[...] = scaled.astype(BF)
    attn_in = (scaled * gains[0:1, :]).astype(BF)
    qkv = dot(attn_in, w[...]).astype(BF)
    qkv_ref[...] = qkv
    same = same_documents(x, first_length)
    heads = []
    masses = []
    for h in range(HEADS_HERE):
        g = h // (HEADS // KV_HEADS)
        q = qkv[:, h * HEAD : (h + 1) * HEAD]
        k = qkv[:, QC + g * HEAD : QC + (g + 1) * HEAD]
        v = qkv[:, QC + KC + g * HEAD : QC + KC + (g + 1) * HEAD]
        scores = jnp.where(same, dot(q, k, 1, 1) * SCALE, MASKED)
        highest = jnp.max(scores, axis=-1, keepdims=True)
        raised = jnp.exp(scores - highest)
        total = jnp.sum(raised, axis=-1, keepdims=True)
        probs = (raised * (1.0 / total)).astype(BF)
        heads.append(dot(probs, v).astype(BF))
        masses.append(jnp.broadcast_to(highest + jnp.log(total), (GT, 32)))
    mixed = jnp.concatenate(heads, axis=1)
    mixed_ref[...] = mixed
    mass_ref[...] = jnp.concatenate(masses, axis=1)
    part = dot(mixed, wo[...]).astype(BF)
    for k, out in enumerate((o0, o1, o2, o3)):
        out[...] = part[k * TOK : (k + 1) * TOK]


def leave_body(own, r1, r2, r3, dealt, gains, d01, middle_ref, rows_ref):
    middle = dealt[...].astype(F32) + (
        (own[...].astype(F32) + r1[...].astype(F32)) + (r2[...].astype(F32) + r3[...].astype(F32))
    )
    middle_ref[...] = middle
    r = lax.rsqrt(jnp.mean(middle * middle, axis=-1, keepdims=True) + EPS)
    ffn_in = (middle * r * gains[8:9, :]).astype(BF)
    rows_ref[...] = dot(d01[...], ffn_in).astype(BF)


SOURCES = 8
TILE = SOURCES * CAP


def expert_body(m, last, waits, *refs):
    refs = list(refs[waits:])
    place, cap, rows, cotangent = refs[:4]
    blocks = refs[4:9]
    refs = refs[9:]
    prev = None
    if m > 0:
        prev, refs = refs[0], refs[1:]
    out_ref, back_ref = refs[:2]
    if last:
        own_ref, sends, (wg, wu, wd, acc) = refs[2], refs[3:6], refs[6:]
    else:
        sums_ref, (wg, wu, wd, acc) = refs[2], refs[3:]
    step = pl.program_id(0)

    @pl.when(step == 0)
    def _():
        mine, right, left, first, second = blocks
        for k, ref in enumerate((mine, right, (first, second), left)):
            at = slice(k * 128, (k + 1) * 128)
            for half in range(2):
                piece = ref[half] if k != 2 else ref[half][0]
                rows_at = slice(half * (D // 2), (half + 1) * (D // 2))
                wg[rows_at, at] = piece[0]
                wu[rows_at, at] = piece[1]
                wd[rows_at, at] = piece[2]
        acc[...] = jnp.zeros(acc.shape, F32) if prev is None else prev[...]

    expert = place[0] >> 2
    notes = cotangent[:, TOK : TOK + NOTES, :].astype(F32)
    named, high, low = (notes[:, j, :] for j in range(3))
    hits = jnp.zeros((SOURCES, TOK), F32)
    weight = jnp.zeros((SOURCES, TOK), F32)
    for k in range(TOPK):
        at = slice(k * TOK, (k + 1) * TOK)
        hit = named[:, at] == expert.astype(F32)
        hits = jnp.where(hit, 1.0, hits)
        weight = jnp.where(hit, high[:, at] + low[:, at], weight)
    earlier = jnp.where(iota((TOK, TOK), 0) < iota((TOK, TOK), 1), 1.0, 0.0).astype(BF)
    ranks = dot(hits.astype(BF), earlier)
    kept = jnp.logical_and(hits > 0.0, ranks < cap[0, expert].astype(F32))
    place_of = jnp.where(kept, ranks, -1.0)
    rank = iota((CAP, TOK), 0).astype(F32)
    picks, gates_of, grads = [], [], []
    for j in range(SOURCES):
        own = place_of[j : j + 1, :] == rank
        gate = jnp.sum(jnp.where(own, weight[j : j + 1, :], 0.0), axis=1, keepdims=True)
        pick = jnp.where(own, 1.0, 0.0).astype(BF)
        picks.append(pick)
        gates_of.append(gate)
        grads.append((dot(pick, cotangent[j, 0:TOK, :]) * gate).astype(BF))
    grad = jnp.concatenate(grads, axis=0)
    row = rows[...]
    gate_of = jnp.concatenate(gates_of, axis=0)
    gate = dot(row, wg[...])
    up = dot(row, wu[...])
    sig = jax.nn.sigmoid(gate)
    silu = gate * sig
    hidden = (silu * up).astype(BF)
    weighted = (dot(hidden, wd[...], 1, 1) * gate_of).astype(BF)
    for j in range(SOURCES):
        out_ref[j] = dot(picks[j], weighted[j * CAP : (j + 1) * CAP], 0, 0).astype(BF)
    grad_hidden = dot(grad, wd[...])
    grad_gate = (grad_hidden * up * sig * (1.0 + gate * (1.0 - sig))).astype(BF)
    grad_up = (grad_hidden * silu).astype(BF)
    back_ref[...] = (dot(grad_gate, wg[...], 1, 1) + dot(grad_up, wu[...], 1, 1)).astype(BF)
    acc[0] += dot(row, grad_gate, 0, 0)
    acc[1] += dot(row, grad_up, 0, 0)
    acc[2] += dot(grad, hidden, 0, 0)

    @pl.when(step == pl.num_programs(0) - 1)
    def _():
        if last:
            for j in range(3):
                own_ref[j] = acc[j, :, 0:128]
                for k in range(1, SHARDS):
                    sends[k - 1][j] = acc[j, :, k * 128 : (k + 1) * 128].astype(BF)
        else:
            sums_ref[...] = acc[...]


def expert_call(m, micro, place, cap, rows, cotangent, blocks, prev, after=()):
    last = m == micro - 1
    tiles = SLOTS // TILE
    tile = pl.BlockSpec((TILE, D), lambda i: (i, 0))

    def fixed(dims):
        return pl.BlockSpec(dims, lambda i: (0,) * len(dims), pipeline_mode=pl.Buffered(1))

    ins = [place, cap, rows, cotangent, *blocks]
    in_specs = [
        SMEM,
        SMEM,
        tile,
        pl.BlockSpec((SOURCES, TOK + NOTES, D), lambda i: (i, 0, 0)),
    ] + [fixed(b.shape) for b in blocks]
    ins = [*after, *ins]
    in_specs = [ANY] * len(after) + in_specs
    outs = [shape((EXPERTS, TOK, D), BF), shape((SLOTS, D), BF)]
    out_specs = [pl.BlockSpec((SOURCES, TOK, D), lambda i: (i, 0, 0)), tile]
    if m > 0:
        ins.append(prev)
        in_specs.append(fixed((3, D, F)))
    if last:
        outs += [shape((3, D, 128), F32)] + [shape((3, D, 128), BF)] * 3
        out_specs += [fixed((3, D, 128))] * 4
    else:
        outs.append(shape((3, D, F), F32))
        out_specs.append(fixed((3, D, F)))
    return pl.pallas_call(
        functools.partial(expert_body, m, last, len(after)),
        grid=(tiles,),
        in_specs=in_specs,
        out_specs=out_specs,
        out_shape=outs,
        scratch_shapes=[pltpu.VMEM((D, F), BF)] * 3 + [pltpu.VMEM((3, D, F), F32)],
        compiler_params=pltpu.CompilerParams(
            vmem_limit_bytes=56 * 1024 * 1024, dimension_semantics=("arbitrary",)
        ),
        cost_estimate=cost(MICROSECONDS["expert"]),
        name="expert",
    )(*ins)


def returned_body(back, c01, middle, gains, dy, branch_ref, gain_ref):
    upstream = dot(c01[...], back[...])
    mid = middle[...]
    r = lax.rsqrt(jnp.mean(mid * mid, axis=-1, keepdims=True) + EPS)
    scaled = upstream * gains[8:9, :]
    grad = r * scaled - mid * (r * r * r) * jnp.mean(scaled * mid, axis=-1, keepdims=True)
    branch_ref[...] = (dy[0:TOK, :].astype(F32) + grad).astype(BF)
    gain_ref[...] = jnp.broadcast_to(jnp.sum(upstream * mid * r, axis=0, keepdims=True), (8, D))


def block_body(mixture, middle, out_ref):
    out_ref[...] = (middle[...] + mixture[...].astype(F32)).astype(BF)


def place_body(micro, place, order, *refs):
    for m in range(micro):
        deal = given_by_dealt(order, m, x_of(place), TOK)
        refs[-1][m] = dot(deal, stack(refs[SHARDS * m : SHARDS * (m + 1)])).astype(BF)


def attend_back_body(m, last, place, lengths, order, g0, g1, g2, g3, xr, qkv_ref, mixed, mass, w, wo, *refs):
    x, first_length = x_of(place), lengths[m, 0, 0]
    if last:
        prev_w, prev_o, gain0, gain1, *refs = refs
    o0, o1, o2, o3, given_ref, *refs = refs
    deal = given_by_dealt(order, m, x)
    branch = stack((g0, g1, g2, g3))
    given_ref[...] = dot(deal[0:TOK], branch).astype(BF)
    sum_o = dot(mixed[...], branch, 0, 0)
    grad_mixed = dot(branch, wo[...], 1, 1).astype(BF)
    qkv = qkv_ref[...]
    same = same_documents(x, first_length)
    grad_q, grad_k, grad_v = [], [], []
    for g in range(KV_HERE):
        k = qkv[:, QC + g * HEAD : QC + (g + 1) * HEAD]
        v = qkv[:, QC + KC + g * HEAD : QC + KC + (g + 1) * HEAD]
        sum_k = jnp.zeros((HEAD, GT), F32)
        sum_v = jnp.zeros((HEAD, GT), F32)
        for r in range(HEADS // KV_HEADS):
            h = g * (HEADS // KV_HEADS) + r
            q = qkv[:, h * HEAD : (h + 1) * HEAD]
            gm = grad_mixed[:, h * HEAD : (h + 1) * HEAD]
            scores = jnp.where(same, dot(q, k, 1, 1) * SCALE, MASKED)
            probs = jnp.exp(scores - mass[:, h * 32 : h * 32 + 1])
            grad_probs = dot(gm, v, 1, 1)
            sum_v += dot(gm, probs.astype(BF), 0, 0)
            weighted = probs * grad_probs
            grad_scores = weighted - probs * jnp.sum(weighted, axis=-1, keepdims=True)
            grad_scores = grad_scores.astype(BF)
            grad_q.append((dot(grad_scores, k) * SCALE).astype(BF))
            sum_k += dot(q, grad_scores, 0, 0)
        grad_k.append((sum_k * SCALE).astype(BF))
        grad_v.append(sum_v.astype(BF))
    grad_kv = jnp.concatenate(grad_k + grad_v, axis=0).astype(F32).T.astype(BF)
    grad_qkv = jnp.concatenate(grad_q + [grad_kv], axis=1)
    sum_w = dot(xr[...], grad_qkv, 0, 0)
    part = dot(grad_qkv, w[...], 1, 1).astype(BF)
    part = dot(deal, part).astype(BF)
    for k, out in enumerate((o0, o1, o2, o3)):
        out[...] = part[k * TOK : (k + 1) * TOK]
    if not last:
        sum_w_ref, sum_o_ref = refs
        sum_w_ref[...] = sum_w
        sum_o_ref[...] = sum_o
        return
    keep_ref, send_ref, all_w, all_o = refs
    c = core_of(place)
    all_w[...] = sum_w + prev_w[...]
    all_o[...] = sum_o + prev_o[...]
    gain = gain0[...] + gain1[...]
    for ref, half in ((keep_ref, c), (send_ref, 1 - c)):
        at = pl.ds(pl.multiple_of(half * 256, 256), 256)
        ref[0:D, :] = all_w[:, at].astype(ref.dtype)
        for j in range(2):
            at = pl.ds(pl.multiple_of(j * 512 + half * 256, 256), 256)
            ref[D + j * 256 : D + (j + 1) * 256, :] = all_o[:, at].astype(ref.dtype)
        tile = jnp.concatenate(
            [gain[0:1, b * 256 : (b + 1) * 256] for b in range(4)] + [jnp.zeros((12, 256), F32)], axis=0
        )
        for j in range(16):
            ref[6 * 256 + j * 16 : 6 * 256 + (j + 1) * 16, :] = tile.astype(ref.dtype)


def tokens_body(micro, tokens, gains, *refs):
    for m in range(micro):
        p0, p1, p2, p3, given = refs[5 * m : 5 * m + 5]
        upstream = (p0[...].astype(F32) + p1[...].astype(F32)) + (
            p2[...].astype(F32) + p3[...].astype(F32)
        )
        v = tokens[m].astype(F32)
        r = lax.rsqrt(jnp.mean(v * v, axis=-1, keepdims=True) + EPS)
        scaled = upstream * gains[0:1, :]
        grad = r * scaled - v * (r * r * r) * jnp.mean(scaled * v, axis=-1, keepdims=True)
        refs[-1][m] = (given[...].astype(F32) + grad).astype(BF)


def weight_sums_body(own, r1, r2, r3, *outs):
    for j in range(3):
        outs[j][0] = (own[j] + r1[j].astype(F32)) + (r2[j].astype(F32) + r3[j].astype(F32))


def weight_stack_body(a, b, c, out_ref):
    for j, ref in enumerate((a, b, c)):
        for half in range(2):
            out_ref[half, j] = ref[0, half * (D // 2) : (half + 1) * (D // 2)]


BLOCKS = 7


def split_y_body(place, keep, got, own_ref, s1, s2, s3):
    y = y_of(place)
    for b in range(BLOCKS):
        for k, ref in enumerate((own_ref, s1, s2, s3)):
            at = pl.ds(pl.multiple_of(b * 256 + ((y + k) & 3) * 64, 64), 64)
            ref[b * 64 : (b + 1) * 64, :] = (keep[at, :] + got[at, :].astype(F32)).astype(ref.dtype)


def split_z_body(place, own, r1, r2, r3, own_ref, s1, s2, s3):
    z = z_of(place)
    for b in range(BLOCKS):
        for k, ref in enumerate((own_ref, s1, s2, s3)):
            at = pl.ds(pl.multiple_of(b * 64 + ((z + k) & 3) * 16, 16), 16)
            total = (own[at, :] + r1[at, :].astype(F32)) + (
                r2[at, :].astype(F32) + r3[at, :].astype(F32)
            )
            ref[b * 16 : (b + 1) * 16, :] = total.astype(ref.dtype)


def split_x_body(place, own, r1, r2, r3, o_ref, own_ref, s1, s2, s3):
    x = x_of(place)

    def total(at):
        return (own[at, :] + r1[at, :].astype(F32)) + (r2[at, :].astype(F32) + r3[at, :].astype(F32))

    gain = total(slice(96, 112))
    row = iota((16, 256), 0)
    for k, ref in enumerate((own_ref, s1, s2, s3)):
        s = (x + k) & 3
        ref[0:16, :] = total(pl.ds(pl.multiple_of(s * 16, 16), 16)).astype(ref.dtype)
        mine = jnp.sum(jnp.where(row == s, gain, 0.0), axis=0, keepdims=True)
        ref[16:32, :] = jnp.broadcast_to(mine, (16, 256)).astype(ref.dtype)
    o_ref[...] = total(slice(64, 96)).astype(BF)


def join_x_body(place, o, own, r1, r2, r3, out_ref, gain_ref):
    x = x_of(place)
    gain = jnp.zeros((16, 256), F32)
    for k, ref in enumerate((own, r1, r2, r3)):
        s = (x - k) & 3
        out_ref[pl.ds(pl.multiple_of(s * 16, 16), 16), :] = ref[0:16, :].astype(BF)
        gain += ref[16:32, :].astype(F32)
    out_ref[64:96, :] = o[...]
    gain_ref[...] = gain[0:1]


def join_body(index_of, place, own, r1, r2, r3, out_ref):
    at = index_of(place)
    rows = own.shape[0]
    for k, ref in enumerate((own, r1, r2, r3)):
        s = (at + k) & 3
        out_ref[pl.ds(pl.multiple_of(s * rows, rows), rows), :] = ref[...]


def weights_body(place, own, got, wq, wk, wv, gain, q_ref, k_ref, v_ref, o_ref, gain_ref):
    c = core_of(place)
    scale = gain[...]
    total = jnp.zeros((ROWS_HERE, 1), F32)

    def piece(ref, b):
        return jnp.concatenate(
            [ref[j * 96 + b * 16 : j * 96 + (b + 1) * 16, :] for j in range(16)], axis=0
        ).astype(F32)

    for b in range(6):
        mine, other = piece(own, b), piece(got, b)
        left = jnp.where(c == 0, mine, other)
        right = jnp.where(c == 0, other, mine)
        if b < 4:
            q_ref[:, b * QC : (b + 1) * QC] = left * scale
            k_ref[:, b * KC : (b + 1) * KC] = right[:, 0:KC] * scale
            v_ref[:, b * KC : (b + 1) * KC] = right[:, KC : 2 * KC] * scale
            total += jnp.sum(
                left * wq[:, b * QC : (b + 1) * QC].astype(F32), axis=1, keepdims=True
            )
            total += jnp.sum(
                right[:, 0:KC] * wk[:, b * KC : (b + 1) * KC].astype(F32), axis=1, keepdims=True
            )
            total += jnp.sum(
                right[:, KC : 2 * KC] * wv[:, b * KC : (b + 1) * KC].astype(F32),
                axis=1,
                keepdims=True,
            )
        else:
            o_ref[:, (b - 4) * 512 : (b - 4) * 512 + 256] = left
            o_ref[:, (b - 4) * 512 + 256 : (b - 3) * 512] = right
    gain_ref[...] = jnp.broadcast_to(total, (ROWS_HERE, 128)).T[0:1]


def from_right(v, k):
    return lax.ppermute(v, "shard", [(i, (i - k) % SHARDS) for i in range(SHARDS)])


def to_right(v, k):
    return lax.ppermute(v, "shard", [(i, (i + k) % SHARDS) for i in range(SHARDS)])


def gather_x(v):
    return [v] + [from_right(v, k) for k in (1, 2, 3)]


def gather_ring(v):
    half = v.shape[0] // 2
    right, left = from_right(v, 1), from_right(v, 3)
    return [v, right, left, from_right(right[:half], 1), from_right(left[half:], 3)]


def hold(arrays, *others):
    count = len(arrays)
    return pl.pallas_call(
        lambda *refs: None,
        out_shape=[shape(v.shape, v.dtype) for v in arrays],
        in_specs=[ANY] * (count + len(others)),
        out_specs=[ANY] * count,
        input_output_aliases={i: i for i in range(count)},
        cost_estimate=cost(0),
        name="hold",
    )(*arrays, *others)


def scatter_x(blocks):
    return [blocks[0]] + [to_right(blocks[k], k) for k in (1, 2, 3)]


def along(v, step):
    pairs = []
    for i in range(EXPERTS):
        z, y, c = step(i // 8, (i // 2) % 4, i % 2)
        pairs.append((i, (z % 4) * 8 + (y % 4) * 2 + c % 2))
    return lax.ppermute(v, "expert", pairs)


def swap_core(v):
    return along(v, lambda z, y, c: (z, y, 1 - c))


def sum_over_experts(v):
    return lax.psum_scatter(v, "expert", scatter_dimension=0, tiled=True)


def exchange(v):
    return lax.all_to_all(v, "expert", split_axis=0, concat_axis=0, tiled=True)


def per_device(
    tokens,
    cotangent,
    order,
    lengths,
    routes,
    gate_weights,
    capacity,
    gain_attn,
    w_query,
    w_key,
    w_value,
    w_out,
    gain_ffn,
    w_gate,
    w_up,
    w_down,
):
    micro = tokens.shape[0]
    place = lax.axis_index(("expert", "shard")).astype(I32).reshape(1)
    cap = capacity.reshape(1, EXPERTS)
    experts = jnp.swapaxes(routes, 1, 2)
    gates = jnp.swapaxes(gate_weights, 1, 2)

    cot_rows = gather_x(cotangent[0])
    *packs, tokens_first = run(
        "pack",
        pack_body,
        [shape((ROWS_HERE + 16, COLS), BF)] * 4 + [shape((TOK, D), BF)],
        [
            place,
            w_query,
            w_key,
            w_value,
            jnp.concatenate([gain_attn, gain_ffn]).reshape(1, -1),
            tokens,
        ],
        smem=(0,),
    )
    pack_done = tokens_first
    waited = hold([*packs, tokens_first], *cot_rows[1:])
    packs, tokens_first = waited[:SHARDS], waited[SHARDS]
    token_rows = gather_x(tokens_first)
    packs = [packs[0]] + [from_right(packs[k], k) for k in (1, 2, 3)]
    routed = run(
        "route",
        functools.partial(route_body, micro),
        [shape((TOK, D), BF)] * (2 * micro - 2)
        + [shape((TOK, SLOTS), BF), shape((SLOTS, TOK), BF)] * micro,
        [experts, cap, tokens, cotangent],
        after=[pack_done],
    )
    later, routed = routed[: 2 * micro - 2], routed[2 * micro - 2 :]
    routed = [routed[2 * m : 2 * m + 2] for m in range(micro)]

    attended, left, reached, dealt_cot, cot_all = [], [], [], [], []
    w_qkv = gains = weights = weight_blocks = parts = None
    for m in range(micro):
        first = m == 0
        if not first:
            cot_rows = gather_x(hold([later[2 * m - 1]], *packs[1:], *token_rows[1:])[0])
            token_rows = gather_x(hold([later[2 * m - 2]], left[-1][1])[0])
        dealt_cot.append(
            run(
                "deal",
                functools.partial(deal_body, m),
                [shape((TOK + NOTES, D), BF)],
                [place, order, experts, gates, *cot_rows],
                smem=(0,),
                after=[pack_done, routed[0][0]] if first else parts[1:2],
            )[0]
        )
        cot_all.append(lax.all_gather(dealt_cot[m], "expert", axis=0))
        if first:
            weights = run(
                "weight_stack",
                weight_stack_body,
                [shape((2, 3, D // 2, 128), BF)],
                [w_gate, w_up, w_down],
                after=dealt_cot,
            )[0]
        elif m == 1:
            weight_blocks = gather_ring(hold([weights], *parts[1:])[0])
        outs = [shape((TOK, D), BF)] * 5 + [
            shape((GT, D), BF),
            shape((GT, COLS), BF),
            shape((GT, QC), BF),
            shape((GT, 128), F32),
        ]
        if first:
            outs += [shape((D, COLS), BF), shape((16, D), F32)]
        result = run(
            "attend",
            functools.partial(attend_body, m),
            outs,
            [place, lengths, order, *token_rows, w_out, *(packs if first else (w_qkv, gains))],
            smem=(0, 1),
            after=[weights] if first else [dealt_cot[m], *weight_blocks[1:3]],
        )
        if first:
            w_qkv, gains = result[9:]
        attended.append(result[:9])
        parts = scatter_x(result[:4])
        left.append(
            run(
                "leave",
                leave_body,
                [shape((TOK, D), F32), shape((SLOTS, D), BF)],
                [*parts, result[4], gains, routed[m][1]],
                after=[] if first else weight_blocks[3:],
            )
        )
        reached.append(exchange(left[m][1]))

    backs, mixtures, sums = [], [], None
    for m in range(micro):
        result = expert_call(
            m,
            micro,
            place,
            cap,
            reached[m],
            cot_all[m],
            weight_blocks,
            sums,
            after=[left[-1][1]] if m == 0 else [],
        )
        dense, back = hold(result[:2], backs[m - 1] if m else reached[-1])
        mixtures.append(sum_over_experts(dense.reshape(-1, D)))
        backs.append(exchange(back))
        sums = result[2] if m < micro - 1 else result[2:]

    def block_of(m, after):
        return run(
            "block",
            block_body,
            [shape((TOK, D), BF)],
            [mixtures[m], left[m][0]],
            after=after,
        )[0]

    sum_w = sum_o = None
    gain_sums, grad_parts = [], []
    for m in range(micro):
        last = m == micro - 1
        branch, gain_sum = run(
            "returned",
            returned_body,
            [shape((TOK, D), BF), shape((8, D), F32)],
            [backs[m], routed[m][0], left[m][0], gains, dealt_cot[m]],
            after=() if m == 0 else (sum_w, totals[0]),
        )
        branch_rows = gather_x(branch)
        if not last:
            block_rows = gather_x(block_of(0, [branch]))
            totals = run(
                "weight_sums",
                weight_sums_body,
                [shape((1, D, 128), F32)] * 3,
                scatter_x(sums),
            )
        gain_sums.append(gain_sum)
        ins = [place, lengths, order, *branch_rows, *attended[m][5:9], w_qkv, w_out]
        out_shapes = [shape((TOK, D), BF)] * 5
        scratch = []
        if last:
            ins += [sum_w, sum_o, *gain_sums]
            out_shapes += [shape((BLOCKS * 256, 256), F32), shape((BLOCKS * 256, 256), BF)]
            scratch = [pltpu.VMEM((D, COLS), F32), pltpu.VMEM((ROWS_HERE, D), F32)]
        else:
            out_shapes += [shape((D, COLS), F32), shape((ROWS_HERE, D), F32)]
        result = run(
            "attend_back",
            functools.partial(attend_back_body, m, last),
            out_shapes,
            ins,
            smem=(0, 1),
            scratch=scratch,
        )
        sum_w, sum_o = result[5:7]
        if last:
            last_parts, last_given = result[:4], result[4]
        else:
            grad_parts += [*scatter_x(result[:4]), result[4]]
    four = [0, 1, 2, 3]
    rows = BLOCKS * 64
    split_y = run(
        "split_y",
        split_y_body,
        [shape((rows, 256), F32)] + [shape((rows, 256), BF)] * 3,
        [place, sum_w, swap_core(sum_o)],
        smem=(0,),
    )
    grad_parts += [*scatter_x(hold(last_parts, split_y[0])), last_given]
    grad_tokens = run(
        "tokens",
        functools.partial(tokens_body, micro),
        [shape(tokens.shape, BF)],
        [tokens, gains, *grad_parts],
    )[0]
    pieces = [split_y[0]] + [along(split_y[k], lambda z, y, c, k=k: (z, y + k, c)) for k in four[1:]]
    rows = BLOCKS * 16
    pieces = run(
        "split_z",
        split_z_body,
        [shape((rows, 256), F32)] + [shape((rows, 256), BF)] * 3,
        [place, *pieces],
        smem=(0,),
    )
    pieces = [pieces[0]] + [along(pieces[k], lambda z, y, c, k=k: (z + k, y, c)) for k in four[1:]]
    o_piece, *pieces = run(
        "split_x",
        split_x_body,
        [shape((32, 256), BF), shape((32, 256), F32)] + [shape((32, 256), BF)] * 3,
        [place, *pieces],
        smem=(0,),
        after=[grad_tokens],
    )
    piece, gain_ffn_sum = run(
        "join_x",
        join_x_body,
        [shape((96, 256), BF), shape((1, 256), F32)],
        [place, o_piece, *scatter_x(pieces)],
        smem=(0,),
    )
    for name, index_of, step in (
        ("join_z", z_of, lambda z, y, c, k: (z - k, y, c)),
        ("join_y", y_of, lambda z, y, c, k: (z, y - k, c)),
    ):
        pieces = [piece] + [
            along(piece, lambda z, y, c, k=k, step=step: step(z, y, c, k)) for k in four[1:]
        ]
        piece = run(
            name,
            functools.partial(join_body, index_of),
            [shape((4 * piece.shape[0], 256), BF)],
            [place, *pieces],
            smem=(0,),
        )[0]
    block_rows += gather_x(block_of(1, [piece]))
    grad_query, grad_key, grad_value, grad_out, grad_gain = run(
        "weights",
        weights_body,
        [
            shape(w_query.shape, F32),
            shape(w_key.shape, F32),
            shape(w_value.shape, F32),
            shape(w_out.shape, F32),
            shape((1, ROWS_HERE), F32),
        ],
        [
            place,
            piece,
            swap_core(piece),
            w_query,
            w_key,
            w_value,
            gain_attn.astype(F32).reshape(-1, 1),
        ],
        smem=(0,),
    )

    block_out = run(
        "place",
        functools.partial(place_body, micro),
        [shape(tokens.shape, BF)],
        [place, order, *block_rows],
        smem=(0,),
    )[0]
    return (
        block_out,
        grad_tokens,
        grad_gain.reshape(-1),
        grad_query,
        grad_key,
        grad_value,
        grad_out,
        gain_ffn_sum.reshape(-1),
        *totals,
    )


def solution(mesh):
    return jax.shard_map(
        per_device,
        mesh=mesh,
        in_specs=(
            P(None, ("expert", "shard"), None),
            P(None, ("expert", "shard"), None),
            P(None, "expert", None),
            P(None, "expert", None),
            P(None, ("expert", "shard"), None),
            P(None, ("expert", "shard"), None),
            P(),
            P("shard"),
            P("shard", None),
            P("shard", None),
            P("shard", None),
            P("shard", None),
            P("shard"),
            P("expert", None, "shard"),
            P("expert", None, "shard"),
            P("expert", None, "shard"),
        ),
        out_specs=(
            P(None, ("expert", "shard"), None),
            P(None, ("expert", "shard"), None),
            P("shard"),
            P("shard", None),
            P("shard", None),
            P("shard", None),
            P("shard", None),
            P("shard"),
            P("expert", None, "shard"),
            P("expert", None, "shard"),
            P("expert", None, "shard"),
        ),
        check_vma=False,
    )
```

time: 581 us -> 508 us (0.87)
  the two profiles are of different devices: /device:TPU:2 before, /device:TPU:1 now
where the time goes in v2:
time: 508 us; the launch traced here: 499 us
  waiting for transfers between devices  206 us (41%)
  Pallas kernels  155 us (31%)
  starting transfers between devices  98.4 us (19%)
  local copies, waits for them, and re-layouts  23.5 us (5%)
  between operations  14.9 us (3%)
    ppermute x31, waiting for transfers between devices, from_right(): lax.ppermute(v, 'shard', [(i, (i - k) % SHARDS) for i in range(SHARDS)])  93.5 us
    pallas_call x25, Pallas kernels, run(): pl.pallas_call(whole, out_shape=outs, in_specs=[SMEM if i in smem else VM...  93.3 us
    ppermute x18, waiting for transfers between devices, to_right(): lax.ppermute(v, 'shard', [(i, (i + k) % SHARDS) for i in range(SHARDS)])  69 us
    pallas_call x2, Pallas kernels, expert_call(): pl.pallas_call(functools.partial(expert_body, m, last, len(after)), grid=...  62 us
    ppermute x31, starting transfers between devices, from_right(): lax.ppermute(v, 'shard', [(i, (i - k) % SHARDS) for i in range(SHARDS)])  33.4 us
    all_to_all x4, starting transfers between devices, exchange(): return lax.all_to_all(v, 'expert', split_axis=0, concat_axis=0, tiled=True)  32 us
    ppermute x14, waiting for transfers between devices, along(): return lax.ppermute(v, 'expert', pairs)  27.6 us
    ppermute x14, starting transfers between devices, along(): return lax.ppermute(v, 'expert', pairs)  19.3 us
  transfers between devices with their start and end apart: 71, of which 43 were waited for; matrix products, arithmetic and copies ran while one was open for 1% of the time, Pallas kernels for 30%

profile of v2, /device:TPU:1, one launch (start us, length us, event | category | flops | bytes accessed | tf_op | source)
XLA Modules:
  0.0 498.7 jit_solution(12351775142775740483)
XLA Ops:
  20.0 6.9 %collective-permute-done.2.refs_7_ = bf16[128,1024]{1,0:T(8,128)(2,1)S(1)} collective-permute-done((bf16[128,1024]{1,0:T(8,128)(2,1)S(1)}, bf16[128,1024]{1,0:T(8,128)(2,1)S(1)}, u32[]{:S(2)}, u32[]{:S(2)}) %collective-permute-start.2) | collective-permute-done | bytes 262176 | tf_op jit(solution)/shard_map/ppermute | solution.py:587
  39.8 11.6 %collective-permute-done.4.refs_5_ = bf16[128,1024]{1,0:T(8,128)(2,1)S(1)} collective-permute-done((bf16[128,1024]{1,0:T(8,128)(2,1)}, bf16[128,1024]{1,0:T(8,128)(2,1)S(1)}, u32[]{:S(2)}, u32[]{:S(2)}) %collective-permute-start.4) | collective-permute-done | bytes 262176 | tf_op jit(solution)/shard_map/ppermute | solution.py:587
  51.4 7.0 %collective-permute-done.5.refs_6_ = bf16[128,1024]{1,0:T(8,128)(2,1)S(1)} collective-permute-done((bf16[128,1024]{1,0:T(8,128)(2,1)}, bf16[128,1024]{1,0:T(8,128)(2,1)S(1)}, u32[]{:S(2)}, u32[]{:S(2)}) %collective-permute-start.5) | collective-permute-done | bytes 262176 | tf_op jit(solution)/shard_map/ppermute | solution.py:587
  59.4 7.4 %attend.2 = (bf16[128,1024]{1,0:T(8,128)(2,1)}, bf16[128,1024]{1,0:T(8,128)(2,1)}, bf16[128,1024]{1,0:T(8,128)(2,1)}, bf16[128,1024]{1,0:T(8,128)(2,1)}, bf16[12...) custom-call(s32[1]{0:T(128)} %bitcast.refs_0_.refs_1_, ...), custom_call_target="tpu_custom_call" | custom-call | flops 1 | bytes 26280000 | tf_op jit(solution)/shard_map/attend/pallas_call | solution.py:87
  70.1 11.3 %collective-permute-done.9.refs_1_.refs_8_ = bf16[128,1024]{1,0:T(8,128)(2,1)S(1)} collective-permute-done((bf16[128,1024]{1,0:T(8,128)(2,1)}, bf16[128,1024]{1,0:T(8,128)(2,1)S(1)}, u32[]{:S(2)}, u32[]{:S(2)}) %collective-permute-start.9) | collective-permute-done | bytes 262176 | tf_op jit(solution)/shard_map/ppermute | solution.py:591
  81.4 5.5 %collective-permute-done.17.refs_7_ = bf16[128,1024]{1,0:T(8,128)(2,1)S(1)} collective-permute-done((bf16[128,1024]{1,0:T(8,128)(2,1)}, bf16[128,1024]{1,0:T(8,128)(2,1)S(1)}, u32[]{:S(2)}, u32[]{:S(2)}) %collective-permute-start.17) | collective-permute-done | bytes 262176 | tf_op jit(solution)/shard_map/ppermute | solution.py:587
  90.5 7.5 %collective-permute-done.10.refs_2_ = bf16[128,1024]{1,0:T(8,128)(2,1)S(1)} collective-permute-done((bf16[128,1024]{1,0:T(8,128)(2,1)S(1)}, bf16[128,1024]{1,0:T(8,128)(2,1)S(1)}, u32[]{:S(2)}, u32[]{:S(2)}) %collective-permute-start.10) | collective-permute-done | bytes 262176 | tf_op jit(solution)/shard_map/ppermute | solution.py:591
  102.0 4.3 leave.2
  106.3 9.8 %all-to-all-start = ((bf16[32,48,1024]{2,1,0:T(8,128)(2,1)}), bf16[32,48,1024]{2,1,0:T(8,128)(2,1)S(1)}, u32[]{:S(2)}, u32[]{:S(2)}) async-start(bf16[32,48,1024]{2,1,0:T(8,128)(2,1)} %bitcast.32), calls=%async_computation | async-start | bytes 6291456 | tf_op jit(solution)/shard_map/all_to_all | solution.py:638
  121.8 13.8 %collective-permute-done.18.refs_11_.refs_6_.refs_5_ = bf16[2,3,512,128]{3,2,1,0:T(8,128)(2,1)} collective-permute-done((bf16[2,3,512,128]{3,2,1,0:T(8,128)(2,1)}, bf16[2,3,512,128]{3,2,1,0:T(8,128)(2,1)}, u32[]{:S(2)}, u32[]{:S(2)}) %collective-permute-start.18) | collective-permute-done | bytes 786464 | tf_op jit(solution)/shard_map/ppermute | solution.py:587
  150.6 7.1 %attend.3 = (bf16[128,1024]{1,0:T(8,128)(2,1)}, bf16[128,1024]{1,0:T(8,128)(2,1)}, bf16[128,1024]{1,0:T(8,128)(2,1)}, bf16[128,1024]{1,0:T(8,128)(2,1)}, bf16[12...) custom-call(s32[1]{0:T(128)} %bitcast.refs_0_.refs_1_, ...), custom_call_target="tpu_custom_call" | custom-call | flops 1 | bytes 26280000 | tf_op jit(solution)/shard_map/attend/pallas_call | solution.py:87
  160.4 5.7 %collective-permute-done.20.refs_1_ = bf16[128,1024]{1,0:T(8,128)(2,1)S(1)} collective-permute-done((bf16[128,1024]{1,0:T(8,128)(2,1)}, bf16[128,1024]{1,0:T(8,128)(2,1)S(1)}, u32[]{:S(2)}, u32[]{:S(2)}) %collective-permute-start.20) | collective-permute-done | bytes 262176 | tf_op jit(solution)/shard_map/ppermute | solution.py:591
  172.9 4.3 leave.3
  178.9 9.0 %all-to-all-start.1 = ((bf16[32,48,1024]{2,1,0:T(8,128)(2,1)}), bf16[32,48,1024]{2,1,0:T(8,128)(2,1)S(1)}, u32[]{:S(2)}, u32[]{:S(2)}) async-start(bf16[32,48,1024]{2,1,0:T(8,128)(2,1)} %bitcast.29), calls=%async_computation.1 | async-start | bytes 6291456 | tf_op jit(solution)/shard_map/all_to_all | solution.py:638
  188.4 30.1 %expert.2 = (bf16[32,128,1024]{2,1,0:T(8,128)(2,1)}, bf16[1536,1024]{1,0:T(8,128)(2,1)}, f32[3,1024,512]{2,1,0:T(8,128)}) custom-call(bf16[1536,1024]{1,0:T(8,128)(2,1)} %get-tuple-element.137.refs_0_, s32[1]{0:T(128)} %bitcast.refs_0_.refs_1_, s32[1,32]{1,0:T(1,128)} %bitcast.41, bf16[1536,1024]{1,0:T(8,128)(2,1)} %bitcast.27, ...), custom_call_target="tpu_custom_call" | custom-call | flops 1 | bytes 97200000 | tf_op jit(solution)/shard_map/expert/pallas_call | solution.py:372
  218.5 8.6 %all-to-all-done.1 = bf16[32,48,1024]{2,1,0:T(8,128)(2,1)S(1)} async-done(((bf16[32,48,1024]{2,1,0:T(8,128)(2,1)}), bf16[32,48,1024]{2,1,0:T(8,128)(2,1)S(1)}, u32[]{:S(2)}, u32[]{:S(2)}) %all-to-all-start.1) | async-done | bytes 3145760 | tf_op jit(solution)/shard_map/all_to_all | solution.py:638
  228.8 6.6 %all-to-all-start.2 = ((bf16[32,48,1024]{2,1,0:T(8,128)(2,1)}), bf16[32,48,1024]{2,1,0:T(8,128)(2,1)S(1)}, u32[]{:S(2)}, u32[]{:S(2)}) async-start(bf16[32,48,1024]{2,1,0:T(8,128)(2,1)} %bitcast.31), calls=%async_computation.3 | async-start | bytes 6291456 | tf_op jit(solution)/shard_map/all_to_all | solution.py:638
  235.6 32.0 %expert.3 = (bf16[32,128,1024]{2,1,0:T(8,128)(2,1)}, bf16[1536,1024]{1,0:T(8,128)(2,1)}, f32[3,1024,128]{2,1,0:T(8,128)}, bf16[3,1024,128]{2,1,0:T(8,128)(2,1)},...) custom-call(s32[1]{0:T(128)} %bitcast.refs_0_.refs_1_, s32[1,32]{1,0:T(1,128)} %bitcast.42, ...), custom_call_target="tpu_custom_call" | custom-call | flops 1 | bytes 97200000 | tf_op jit(solution)/shard_map/expert/pallas_call | solution.py:372
  267.5 7.1 %all-to-all-done.2 = bf16[32,48,1024]{2,1,0:T(8,128)(2,1)S(1)} async-done(((bf16[32,48,1024]{2,1,0:T(8,128)(2,1)}), bf16[32,48,1024]{2,1,0:T(8,128)(2,1)S(1)}, u32[]{:S(2)}, u32[]{:S(2)}) %all-to-all-start.2) | async-done | bytes 3145760 | tf_op jit(solution)/shard_map/all_to_all | solution.py:638
  276.3 6.6 %all-to-all-start.3 = ((bf16[32,48,1024]{2,1,0:T(8,128)(2,1)}), bf16[32,48,1024]{2,1,0:T(8,128)(2,1)S(1)}, u32[]{:S(2)}, u32[]{:S(2)}) async-start(bf16[32,48,1024]{2,1,0:T(8,128)(2,1)} %bitcast.30), calls=%async_computation.5 | async-start | bytes 6291456 | tf_op jit(solution)/shard_map/all_to_all | solution.py:638
  293.4 9.9 %collective-permute-done.31.refs_1_ = bf16[3,1024,128]{2,1,0:T(8,128)(2,1)S(1)} collective-permute-done((bf16[3,1024,128]{2,1,0:T(8,128)(2,1)}, bf16[3,1024,128]{2,1,0:T(8,128)(2,1)S(1)}, u32[]{:S(2)}, u32[]{:S(2)}) %collective-permute-start.31) | collective-permute-done | bytes 786464 | tf_op jit(solution)/shard_map/ppermute | solution.py:591
  303.4 17.3 %collective-permute-done.32.refs_2_ = bf16[3,1024,128]{2,1,0:T(8,128)(2,1)S(1)} collective-permute-done((bf16[3,1024,128]{2,1,0:T(8,128)(2,1)}, bf16[3,1024,128]{2,1,0:T(8,128)(2,1)S(1)}, u32[]{:S(2)}, u32[]{:S(2)}) %collective-permute-start.32) | collective-permute-done | bytes 786464 | tf_op jit(solution)/shard_map/ppermute | solution.py:591
  326.4 6.2 %collective-permute-done.30.refs_6_ = bf16[128,1024]{1,0:T(8,128)(2,1)S(1)} collective-permute-done((bf16[128,1024]{1,0:T(8,128)(2,1)}, bf16[128,1024]{1,0:T(8,128)(2,1)S(1)}, u32[]{:S(2)}, u32[]{:S(2)}) %collective-permute-start.30) | collective-permute-done | bytes 262176 | tf_op jit(solution)/shard_map/ppermute | solution.py:587
  333.3 9.3 %attend_back.2 = (bf16[128,1024]{1,0:T(8,128)(2,1)}, bf16[128,1024]{1,0:T(8,128)(2,1)}, bf16[128,1024]{1,0:T(8,128)(2,1)}, bf16[128,1024]{1,0:T(8,128)(2,1)}, bf...) custom-call(s32[1]{0:T(128)} %bitcast.refs_0_.refs_1_, s32[2,1,2]{2,1,0:T(1,128)} %refs_1_.16, ...), custom_call_target="tpu_custom_call" | custom-call | flops 1 | bytes 36000000 | tf_op jit(solution)/shard_map/attend_back/pallas_call | solution.py:87
  350.3 5.4 %collective-permute-done.34.refs_4_ = bf16[128,1024]{1,0:T(8,128)(2,1)S(1)} collective-permute-done((bf16[128,1024]{1,0:T(8,128)(2,1)}, bf16[128,1024]{1,0:T(8,128)(2,1)S(1)}, u32[]{:S(2)}, u32[]{:S(2)}) %collective-permute-start.34) | collective-permute-done | bytes 262176 | tf_op jit(solution)/shard_map/ppermute | solution.py:587
  357.3 7.6 %collective-permute-done.36.refs_6_ = bf16[128,1024]{1,0:T(8,128)(2,1)S(1)} collective-permute-done((bf16[128,1024]{1,0:T(8,128)(2,1)}, bf16[128,1024]{1,0:T(8,128)(2,1)S(1)}, u32[]{:S(2)}, u32[]{:S(2)}) %collective-permute-start.36) | collective-permute-done | bytes 262176 | tf_op jit(solution)/shard_map/ppermute | solution.py:587
  365.6 11.7 %attend_back.3 = (bf16[128,1024]{1,0:T(8,128)(2,1)}, bf16[128,1024]{1,0:T(8,128)(2,1)}, bf16[128,1024]{1,0:T(8,128)(2,1)}, bf16[128,1024]{1,0:T(8,128)(2,1)}, bf...) custom-call(s32[1]{0:T(128)} %bitcast.refs_0_.refs_1_, s32[2,1,2]{2,1,0:T(1,128)} %refs_1_.16, ...), custom_call_target="tpu_custom_call" | custom-call | flops 1 | bytes 36000000 | tf_op jit(solution)/shard_map/attend_back/pallas_call | solution.py:87
  393.0 5.8 %collective-permute-done.39.refs_3_ = bf16[448,256]{1,0:T(8,128)(2,1)S(1)} collective-permute-done((bf16[448,256]{1,0:T(8,128)(2,1)}, bf16[448,256]{1,0:T(8,128)(2,1)S(1)}, u32[]{:S(2)}, u32[]{:S(2)}) %collective-permute-start.39) | collective-permute-done | bytes 229408 | tf_op jit(solution)/shard_map/ppermute | solution.py:626
  441.6 4.0 collective-permute-done.56.refs_2_
  446.7 7.5 %collective-permute-done.58.refs_4_ = bf16[384,256]{1,0:T(8,128)(2,1)S(1)} collective-permute-done((bf16[384,256]{1,0:T(8,128)(2,1)}, bf16[384,256]{1,0:T(8,128)(2,1)S(1)}, u32[]{:S(2)}, u32[]{:S(2)}) %collective-permute-start.58) | collective-permute-done | bytes 196640 | tf_op jit(solution)/shard_map/ppermute | solution.py:626
  473.1 4.5 collective-permute-done.27.refs_5_
  482.1 6.0 %collective-permute-done.61.refs_9_ = bf16[128,1024]{1,0:T(8,128)(2,1)S(1)} collective-permute-done((bf16[128,1024]{1,0:T(8,128)(2,1)}, bf16[128,1024]{1,0:T(8,128)(2,1)S(1)}, u32[]{:S(2)}, u32[]{:S(2)}) %collective-permute-start.61) | collective-permute-done | bytes 262176 | tf_op jit(solution)/shard_map/ppermute | solution.py:587
  (299 shorter events, 186.8 us)
Async XLA Ops:
  7.2 181.3 %all-gather.5.cloned.1.call-start = ((), (), s32[]{:S(2)}) async-start(), calls=%async_computation.8 | async-start | bytes 9732096 | tf_op jit(solution)/shard_map/all_gather | solution.py:713
  30.0 205.6 %all-gather.7.cloned.1.call-start = ((), (), s32[]{:S(2)}) async-start(), calls=%async_computation.9 | async-start | bytes 9732096 | tf_op jit(solution)/shard_map/all_gather | solution.py:713
  30.1 28.3 %collective-permute-start.6 = (bf16[272,512]{1,0:T(8,128)(2,1)}, bf16[272,512]{1,0:T(8,128)(2,1)S(1)}, u32[]{:S(2)}, u32[]{:S(2)}) collective-permute-start(bf16[272,512]{1,0:T(8,128)(2,1)} %get-tuple-element.117), channel_id=1, source_target_pairs={{0,3},{1,0},{2,1},{3,2},{4,7},{5,4},{6,5},{7,6},{8,11},{9,8},{10,9... | collective-permute-start | bytes 835592 | tf_op jit(solution)/shard_map/ppermute | solution.py:587
  30.9 27.5 %collective-permute-start.7 = (bf16[272,512]{1,0:T(8,128)(2,1)}, bf16[272,512]{1,0:T(8,128)(2,1)S(1)}, u32[]{:S(2)}, u32[]{:S(2)}) collective-permute-start(bf16[272,512]{1,0:T(8,128)(2,1)} %get-tuple-element.118), channel_id=1, source_target_pairs={{0,2},{1,3},{2,0},{3,1},{4,6},{5,7},{6,4},{7,5},{8,10},{9,11},{10,... | collective-permute-start | bytes 835592 | tf_op jit(solution)/shard_map/ppermute | solution.py:587
  33.3 25.1 %collective-permute-start.8 = (bf16[272,512]{1,0:T(8,128)(2,1)}, bf16[272,512]{1,0:T(8,128)(2,1)S(1)}, u32[]{:S(2)}, u32[]{:S(2)}) collective-permute-start(bf16[272,512]{1,0:T(8,128)(2,1)} %get-tuple-element.119), channel_id=1, source_target_pairs={{0,1},{1,2},{2,3},{3,0},{4,5},{5,6},{6,7},{7,4},{8,9},{9,10},{10,1... | collective-permute-start | bytes 835592 | tf_op jit(solution)/shard_map/ppermute | solution.py:587
  33.4 18.0 %collective-permute-start.4 = (bf16[128,1024]{1,0:T(8,128)(2,1)}, bf16[128,1024]{1,0:T(8,128)(2,1)S(1)}, u32[]{:S(2)}, u32[]{:S(2)}) collective-permute-start(bf16[128,1024]{1,0:T(8,128)(2,1)} %get-tuple-element.115.refs_3_), channel_id=1, source_target_pairs={{0,2},{1,3},{2,0},{3,1},{4,6},{5,7},{6,4},{7,5},{8,10},{9,11},{10,... | collective-permute-start | bytes 786440 | tf_op jit(solution)/shard_map/ppermute | solution.py:587
  37.7 20.7 %collective-permute-start.5 = (bf16[128,1024]{1,0:T(8,128)(2,1)}, bf16[128,1024]{1,0:T(8,128)(2,1)S(1)}, u32[]{:S(2)}, u32[]{:S(2)}) collective-permute-start(bf16[128,1024]{1,0:T(8,128)(2,1)} %get-tuple-element.115.refs_3_), channel_id=1, source_target_pairs={{0,1},{1,2},{2,3},{3,0},{4,5},{5,6},{6,7},{7,4},{8,9},{9,10},{10,1... | collective-permute-start | bytes 786440 | tf_op jit(solution)/shard_map/ppermute | solution.py:587
  69.5 17.4 %collective-permute-start.17 = (bf16[128,1024]{1,0:T(8,128)(2,1)}, bf16[128,1024]{1,0:T(8,128)(2,1)S(1)}, u32[]{:S(2)}, u32[]{:S(2)}) collective-permute-start(bf16[128,1024]{1,0:T(8,128)(2,1)} %hold.9.refs_4_), channel_id=1, source_target_pairs={{0,1},{1,2},{2,3},{3,0},{4,5},{5,6},{6,7},{7,4},{8,9},{9,10},{10,1... | collective-permute-start | bytes 786440 | tf_op jit(solution)/shard_map/ppermute | solution.py:587
  106.3 71.0 %all-to-all-start = ((bf16[32,48,1024]{2,1,0:T(8,128)(2,1)}), bf16[32,48,1024]{2,1,0:T(8,128)(2,1)S(1)}, u32[]{:S(2)}, u32[]{:S(2)}) async-start(bf16[32,48,1024]{2,1,0:T(8,128)(2,1)} %bitcast.32), calls=%async_computation | async-start | bytes 6291456 | tf_op jit(solution)/shard_map/all_to_all | solution.py:638
  116.1 19.4 %collective-permute-start.18 = (bf16[2,3,512,128]{3,2,1,0:T(8,128)(2,1)}, bf16[2,3,512,128]{3,2,1,0:T(8,128)(2,1)}, u32[]{:S(2)}, u32[]{:S(2)}) collective-permute-start(bf16[2,3,512,128]{3,2,1,0:T(8,128)(2,1)} %hold.10.refs_5_.refs_4_), channel_id=1, source_target_pairs={{0,3},{1,0},{2,1},{3,2},{4,7},{5,4},{6,5},{7,6},{8,11},{9,8},{10,9... | collective-permute-start | bytes 2359304 | tf_op jit(solution)/shard_map/ppermute | solution.py:587
  118.5 25.5 %collective-permute-start.19 = (bf16[2,3,512,128]{3,2,1,0:T(8,128)(2,1)}, bf16[2,3,512,128]{3,2,1,0:T(8,128)(2,1)}, u32[]{:S(2)}, u32[]{:S(2)}) collective-permute-start(bf16[2,3,512,128]{3,2,1,0:T(8,128)(2,1)} %hold.10.refs_5_.refs_4_), channel_id=1, source_target_pairs={{0,1},{1,2},{2,3},{3,0},{4,5},{5,6},{6,7},{7,4},{8,9},{9,10},{10,1... | collective-permute-start | bytes 2359304 | tf_op jit(solution)/shard_map/ppermute | solution.py:587
  118.5 27.6 %collective-permute-start.12 = (bf16[128,1024]{1,0:T(8,128)(2,1)}, bf16[128,1024]{1,0:T(8,128)(2,1)S(1)}, u32[]{:S(2)}, u32[]{:S(2)}) collective-permute-start(bf16[128,1024]{1,0:T(8,128)(2,1)} %hold.8.refs_3_), channel_id=1, source_target_pairs={{0,3},{1,0},{2,1},{3,2},{4,7},{5,4},{6,5},{7,6},{8,11},{9,8},{10,9... | collective-permute-start | bytes 786440 | tf_op jit(solution)/shard_map/ppermute | solution.py:587
  121.2 24.9 %collective-permute-start.13 = (bf16[128,1024]{1,0:T(8,128)(2,1)}, bf16[128,1024]{1,0:T(8,128)(2,1)S(1)}, u32[]{:S(2)}, u32[]{:S(2)}) collective-permute-start(bf16[128,1024]{1,0:T(8,128)(2,1)} %hold.8.refs_3_), channel_id=1, source_target_pairs={{0,2},{1,3},{2,0},{3,1},{4,6},{5,7},{6,4},{7,5},{8,10},{9,11},{10,... | collective-permute-start | bytes 786440 | tf_op jit(solution)/shard_map/ppermute | solution.py:587
  121.2 28.7 %collective-permute-start.14 = (bf16[128,1024]{1,0:T(8,128)(2,1)}, bf16[128,1024]{1,0:T(8,128)(2,1)S(1)}, u32[]{:S(2)}, u32[]{:S(2)}) collective-permute-start(bf16[128,1024]{1,0:T(8,128)(2,1)} %hold.8.refs_3_), channel_id=1, source_target_pairs={{0,1},{1,2},{2,3},{3,0},{4,5},{5,6},{6,7},{7,4},{8,9},{9,10},{10,1... | collective-permute-start | bytes 786440 | tf_op jit(solution)/shard_map/ppermute | solution.py:587
  136.6 35.4 %collective-permute-start.23 = (bf16[1,3,512,128]{3,2,1,0:T(8,128)(2,1)S(1)}, bf16[1,3,512,128]{3,2,1,0:T(8,128)(2,1)S(1)}, u32[]{:S(2)}, u32[]{:S(2)}) collective-permute-start(bf16[1,3,512,128]{3,2,1,0:T(8,128)(2,1)S(1)} %slice.12), channel_id=1, source_target_pairs={{0,3},{1,0},{2,1},{3,2},{4,7},{5,4},{6,5},{7,6},{8,11},{9,8},{10,9... | collective-permute-start | bytes 1179656 | tf_op jit(solution)/shard_map/ppermute | solution.py:587
  145.0 27.0 %collective-permute-start.24 = (bf16[1,3,512,128]{3,2,1,0:T(8,128)(2,1)S(1)}, bf16[1,3,512,128]{3,2,1,0:T(8,128)(2,1)S(1)}, u32[]{:S(2)}, u32[]{:S(2)}) collective-permute-start(bf16[1,3,512,128]{3,2,1,0:T(8,128)(2,1)S(1)} %slice.13), channel_id=1, source_target_pairs={{0,1},{1,2},{2,3},{3,0},{4,5},{5,6},{6,7},{7,4},{8,9},{9,10},{10,1... | collective-permute-start | bytes 1179656 | tf_op jit(solution)/shard_map/ppermute | solution.py:587
  178.9 48.2 %all-to-all-start.1 = ((bf16[32,48,1024]{2,1,0:T(8,128)(2,1)}), bf16[32,48,1024]{2,1,0:T(8,128)(2,1)S(1)}, u32[]{:S(2)}, u32[]{:S(2)}) async-start(bf16[32,48,1024]{2,1,0:T(8,128)(2,1)} %bitcast.29), calls=%async_computation.1 | async-start | bytes 6291456 | tf_op jit(solution)/shard_map/all_to_all | solution.py:638
  188.0 270.4 %reduce-scatter.3.cloned.1.call-start = ((), (), s32[]{:S(2)}) async-start(), calls=%async_computation.6 | async-start | bytes 8650752 | tf_op jit(solution)/shard_map/reduce_scatter | solution.py:634
  228.8 45.8 %all-to-all-start.2 = ((bf16[32,48,1024]{2,1,0:T(8,128)(2,1)}), bf16[32,48,1024]{2,1,0:T(8,128)(2,1)S(1)}, u32[]{:S(2)}, u32[]{:S(2)}) async-start(bf16[32,48,1024]{2,1,0:T(8,128)(2,1)} %bitcast.31), calls=%async_computation.3 | async-start | bytes 6291456 | tf_op jit(solution)/shard_map/all_to_all | solution.py:638
  235.3 227.3 %reduce-scatter.5.cloned.1.call-start = ((), (), s32[]{:S(2)}) async-start(), calls=%async_computation.7 | async-start | bytes 8650752 | tf_op jit(solution)/shard_map/reduce_scatter | solution.py:634
  276.3 66.3 %all-to-all-start.3 = ((bf16[32,48,1024]{2,1,0:T(8,128)(2,1)}), bf16[32,48,1024]{2,1,0:T(8,128)(2,1)S(1)}, u32[]{:S(2)}, u32[]{:S(2)}) async-start(bf16[32,48,1024]{2,1,0:T(8,128)(2,1)} %bitcast.30), calls=%async_computation.5 | async-start | bytes 6291456 | tf_op jit(solution)/shard_map/all_to_all | solution.py:638
  282.9 20.4 %collective-permute-start.31 = (bf16[3,1024,128]{2,1,0:T(8,128)(2,1)}, bf16[3,1024,128]{2,1,0:T(8,128)(2,1)S(1)}, u32[]{:S(2)}, u32[]{:S(2)}) collective-permute-start(bf16[3,1024,128]{2,1,0:T(8,128)(2,1)} %get-tuple-element.157), channel_id=1, source_target_pairs={{0,1},{1,2},{2,3},{3,0},{4,5},{5,6},{6,7},{7,4},{8,9},{9,10},{10,1... | collective-permute-start | bytes 2359304 | tf_op jit(solution)/shard_map/ppermute | solution.py:591
  283.0 37.8 %collective-permute-start.32 = (bf16[3,1024,128]{2,1,0:T(8,128)(2,1)}, bf16[3,1024,128]{2,1,0:T(8,128)(2,1)S(1)}, u32[]{:S(2)}, u32[]{:S(2)}) collective-permute-start(bf16[3,1024,128]{2,1,0:T(8,128)(2,1)} %get-tuple-element.158), channel_id=1, source_target_pairs={{0,2},{1,3},{2,0},{3,1},{4,6},{5,7},{6,4},{7,5},{8,10},{9,11},{10,... | collective-permute-start | bytes 2359304 | tf_op jit(solution)/shard_map/ppermute | solution.py:591
  286.3 34.4 %collective-permute-start.33 = (bf16[3,1024,128]{2,1,0:T(8,128)(2,1)}, bf16[3,1024,128]{2,1,0:T(8,128)(2,1)S(1)}, u32[]{:S(2)}, u32[]{:S(2)}) collective-permute-start(bf16[3,1024,128]{2,1,0:T(8,128)(2,1)} %get-tuple-element.159), channel_id=1, source_target_pairs={{0,3},{1,0},{2,1},{3,2},{4,7},{5,4},{6,5},{7,6},{8,11},{9,8},{10,9... | collective-permute-start | bytes 2359304 | tf_op jit(solution)/shard_map/ppermute | solution.py:591
  290.1 36.3 %collective-permute-start.28 = (bf16[128,1024]{1,0:T(8,128)(2,1)}, bf16[128,1024]{1,0:T(8,128)(2,1)S(1)}, u32[]{:S(2)}, u32[]{:S(2)}) collective-permute-start(bf16[128,1024]{1,0:T(8,128)(2,1)} %get-tuple-element.143.refs_2_.refs_3_), channel_id=1, source_target_pairs={{0,3},{1,0},{2,1},{3,2},{4,7},{5,4},{6,5},{7,6},{8,11},{9,8},{10,9... | collective-permute-start | bytes 786440 | tf_op jit(solution)/shard_map/ppermute | solution.py:587
  290.4 36.0 %collective-permute-start.29 = (bf16[128,1024]{1,0:T(8,128)(2,1)}, bf16[128,1024]{1,0:T(8,128)(2,1)S(1)}, u32[]{:S(2)}, u32[]{:S(2)}) collective-permute-start(bf16[128,1024]{1,0:T(8,128)(2,1)} %get-tuple-element.143.refs_2_.refs_3_), channel_id=1, source_target_pairs={{0,2},{1,3},{2,0},{3,1},{4,6},{5,7},{6,4},{7,5},{8,10},{9,11},{10,... | collective-permute-start | bytes 786440 | tf_op jit(solution)/shard_map/ppermute | solution.py:587
  303.2 29.4 %collective-permute-start.30 = (bf16[128,1024]{1,0:T(8,128)(2,1)}, bf16[128,1024]{1,0:T(8,128)(2,1)S(1)}, u32[]{:S(2)}, u32[]{:S(2)}) collective-permute-start(bf16[128,1024]{1,0:T(8,128)(2,1)} %get-tuple-element.143.refs_2_.refs_3_), channel_id=1, source_target_pairs={{0,1},{1,2},{2,3},{3,0},{4,5},{5,6},{6,7},{7,4},{8,9},{9,10},{10,1... | collective-permute-start | bytes 786440 | tf_op jit(solution)/shard_map/ppermute | solution.py:587
  349.5 15.4 %collective-permute-start.36 = (bf16[128,1024]{1,0:T(8,128)(2,1)}, bf16[128,1024]{1,0:T(8,128)(2,1)S(1)}, u32[]{:S(2)}, u32[]{:S(2)}) collective-permute-start(bf16[128,1024]{1,0:T(8,128)(2,1)} %get-tuple-element.161.refs_3_), channel_id=1, source_target_pairs={{0,1},{1,2},{2,3},{3,0},{4,5},{5,6},{6,7},{7,4},{8,9},{9,10},{10,1... | collective-permute-start | bytes 786440 | tf_op jit(solution)/shard_map/ppermute | solution.py:587
  401.6 15.4 %collective-permute-start.41 = (bf16[112,256]{1,0:T(8,128)(2,1)}, bf16[112,256]{1,0:T(8,128)(2,1)S(1)}, u32[]{:S(2)}, u32[]{:S(2)}) collective-permute-start(bf16[112,256]{1,0:T(8,128)(2,1)} %get-tuple-element.176), channel_id=1, source_target_pairs={{0,32},{4,36},{8,40},{12,44},{16,48},{20,52},{24,56},{28,60},{32,6... | collective-permute-start | bytes 172040 | tf_op jit(solution)/shard_map/ppermute | solution.py:626
  461.8 15.8 %collective-permute-start.27 = (bf16[128,1024]{1,0:T(8,128)(2,1)}, bf16[128,1024]{1,0:T(8,128)(2,1)S(1)}, u32[]{:S(2)}, u32[]{:S(2)}) collective-permute-start(bf16[128,1024]{1,0:T(8,128)(2,1)} %block.2.refs_2_), channel_id=1, source_target_pairs={{0,1},{1,2},{2,3},{3,0},{4,5},{5,6},{6,7},{7,4},{8,9},{9,10},{10,1... | collective-permute-start | bytes 786440 | tf_op jit(solution)/shard_map/ppermute | solution.py:587
  466.4 15.8 %collective-permute-start.60 = (bf16[128,1024]{1,0:T(8,128)(2,1)}, bf16[128,1024]{1,0:T(8,128)(2,1)S(1)}, u32[]{:S(2)}, u32[]{:S(2)}) collective-permute-start(bf16[128,1024]{1,0:T(8,128)(2,1)} %block.3.refs_6_), channel_id=1, source_target_pairs={{0,2},{1,3},{2,0},{3,1},{4,6},{5,7},{6,4},{7,5},{8,10},{9,11},{10,... | collective-permute-start | bytes 786440 | tf_op jit(solution)/shard_map/ppermute | solution.py:587
  468.4 19.7 %collective-permute-start.61 = (bf16[128,1024]{1,0:T(8,128)(2,1)}, bf16[128,1024]{1,0:T(8,128)(2,1)S(1)}, u32[]{:S(2)}, u32[]{:S(2)}) collective-permute-start(bf16[128,1024]{1,0:T(8,128)(2,1)} %block.3.refs_6_), channel_id=1, source_target_pairs={{0,1},{1,2},{2,3},{3,0},{4,5},{5,6},{6,7},{7,4},{8,9},{9,10},{10,1... | collective-permute-start | bytes 786440 | tf_op jit(solution)/shard_map/ppermute | solution.py:587
  (111 other events, 848.8 us)
Sparse Core Ops, SparseCore 0:
  30.1 55.9 all-gather.4
  90.0 84.5 all-gather.6
  228.9 123.0 reduce-scatter.2
  356.0 96.1 reduce-scatter.4

commit v3 on v2

--- a/solution.py
+++ b/solution.py
@@ -50,21 +50,21 @@
 MICROSECONDS = {
     "pack": 2.5,
     "route": 4.5,
-    "deal": 2.3,
+    "deal": 3.5,
     "weight_stack": 2.0,
     "attend": 7.3,
     "leave": 4.3,
     "expert": 27.0,
     "returned": 3.7,
-    "attend_back": 10.0,
-    "weight_sums": 3.3,
+    "attend_back": 11.0,
+    "weight_sums": 2.0,
     "split_y": 2.8,
     "split_z": 2.0,
     "split_x": 1.6,
     "join_x": 1.5,
     "join_z": 1.6,
     "join_y": 2.2,
-    "block": 1.2,
+    "block": 4.5,
     "place": 2.8,
     "tokens": 3.4,
     "weights": 3.9,
@@ -77,7 +77,7 @@
     )
 
 
-def run(name, body, outs, ins, smem=(), scratch=(), limit=56, after=()):
+def run(name, body, outs, ins, smem=(), scratch=(), limit=63, after=()):
     count = len(ins)
 
     def whole(*refs):
@@ -164,11 +164,10 @@
             gains_out[half * 8 : half * 8 + 8, b * ROWS_HERE : (b + 1) * ROWS_HERE] = total
 
 
-def route_body(micro, routes, cap, tokens, cotangent, *refs):
+def route_body(micro, routes, cap, tokens, *refs):
     for m in range(1, micro):
-        refs[2 * m - 2][...] = tokens[m]
-        refs[2 * m - 1][...] = cotangent[m]
-    outs = refs[2 * micro - 2 :]
+        refs[m - 1][...] = tokens[m]
+    outs = refs[micro - 1 :]
     named = iota((EXPERTS, TOK), 0)
     earlier = jnp.where(iota((TOK, TOK), 0) < iota((TOK, TOK), 1), 1.0, 0.0).astype(BF)
     one = iota((EXPERTS, EXPERTS), 0) == iota((EXPERTS, EXPERTS), 1)
@@ -196,15 +195,18 @@
 NOTES = 16
 
 
-def deal_body(m, place, order, routes, gates, c0, c1, c2, c3, out_ref):
-    deal = given_by_dealt(order, m, x_of(place))[:, 0:TOK]
-    out_ref[0:TOK, :] = dot(deal, stack((c0, c1, c2, c3)), 0, 0).astype(BF)
-    experts = jnp.concatenate([routes[m, k : k + 1, :] for k in range(TOPK)], axis=1).astype(F32)
-    weights = jnp.concatenate([gates[m, k : k + 1, :] for k in range(TOPK)], axis=1)
-    high = weights.astype(BF).astype(F32)
-    row = iota((NOTES, D), 0)
-    notes = jnp.where(row == 0, experts, jnp.where(row == 1, high, weights - high))
-    out_ref[TOK : TOK + NOTES, :] = notes.astype(BF)
+def deal_body(micro, place, order, routes, gates, c0, c1, c2, c3, out_ref):
+    for m in range(micro):
+        deal = given_by_dealt(order, m, x_of(place))[:, 0:TOK]
+        rows = jnp.concatenate([c[m] for c in (c0, c1, c2, c3)], axis=0)
+        out_ref[m, 0:TOK, :] = dot(deal, rows, 0, 0).astype(BF)
+        experts = jnp.concatenate([routes[m, k : k + 1, :] for k in range(TOPK)], axis=1)
+        weights = jnp.concatenate([gates[m, k : k + 1, :] for k in range(TOPK)], axis=1)
+        high = weights.astype(BF).astype(F32)
+        row = iota((NOTES, D), 0)
+        notes = jnp.where(row == 1, high, weights - high)
+        notes = jnp.where(row == 0, experts.astype(F32), notes)
+        out_ref[m, TOK : TOK + NOTES, :] = notes.astype(BF)
 
 
 def attend_body(m, place, lengths, order, t0, t1, t2, t3, wo, *refs):
@@ -270,7 +272,7 @@
         prev, refs = refs[0], refs[1:]
     out_ref, back_ref = refs[:2]
     if last:
-        own_ref, sends, (wg, wu, wd, acc) = refs[2], refs[3:6], refs[6:]
+        send_ref, (wg, wu, wd, acc) = refs[2], refs[3:]
     else:
         sums_ref, (wg, wu, wd, acc) = refs[2], refs[3:]
     step = pl.program_id(0)
@@ -289,7 +291,7 @@
         acc[...] = jnp.zeros(acc.shape, F32) if prev is None else prev[...]
 
     expert = place[0] >> 2
-    notes = cotangent[:, TOK : TOK + NOTES, :].astype(F32)
+    notes = cotangent[:, 0, TOK : TOK + NOTES, :].astype(F32)
     named, high, low = (notes[:, j, :] for j in range(3))
     hits = jnp.zeros((SOURCES, TOK), F32)
     weight = jnp.zeros((SOURCES, TOK), F32)
@@ -310,7 +312,7 @@
         pick = jnp.where(own, 1.0, 0.0).astype(BF)
         picks.append(pick)
         gates_of.append(gate)
-        grads.append((dot(pick, cotangent[j, 0:TOK, :]) * gate).astype(BF))
+        grads.append((dot(pick, cotangent[j, 0, 0:TOK, :]) * gate).astype(BF))
     grad = jnp.concatenate(grads, axis=0)
     row = rows[...]
     gate_of = jnp.concatenate(gates_of, axis=0)
@@ -320,8 +322,11 @@
     silu = gate * sig
     hidden = (silu * up).astype(BF)
     weighted = (dot(hidden, wd[...], 1, 1) * gate_of).astype(BF)
-    for j in range(SOURCES):
-        out_ref[j] = dot(picks[j], weighted[j * CAP : (j + 1) * CAP], 0, 0).astype(BF)
+    if last:
+        out_ref[...] = weighted
+    else:
+        for j in range(SOURCES):
+            out_ref[j] = dot(picks[j], weighted[j * CAP : (j + 1) * CAP], 0, 0).astype(BF)
     grad_hidden = dot(grad, wd[...])
     grad_gate = (grad_hidden * up * sig * (1.0 + gate * (1.0 - sig))).astype(BF)
     grad_up = (grad_hidden * silu).astype(BF)
@@ -333,10 +338,10 @@
     @pl.when(step == pl.num_programs(0) - 1)
     def _():
         if last:
-            for j in range(3):
-                own_ref[j] = acc[j, :, 0:128]
-                for k in range(1, SHARDS):
-                    sends[k - 1][j] = acc[j, :, k * 128 : (k + 1) * 128].astype(BF)
+            for k in range(SHARDS):
+                for j in range(3):
+                    piece = acc[j, :, k * 128 : (k + 1) * 128].astype(BF)
+                    send_ref[pl.ds((x_of(place) + k) & 3, 1), j] = piece[None]
         else:
             sums_ref[...] = acc[...]
 
@@ -354,18 +359,19 @@
         SMEM,
         SMEM,
         tile,
-        pl.BlockSpec((SOURCES, TOK + NOTES, D), lambda i: (i, 0, 0)),
+        pl.BlockSpec((SOURCES, 1, TOK + NOTES, D), lambda i: (i, m, 0, 0)),
     ] + [fixed(b.shape) for b in blocks]
     ins = [*after, *ins]
     in_specs = [ANY] * len(after) + in_specs
-    outs = [shape((EXPERTS, TOK, D), BF), shape((SLOTS, D), BF)]
-    out_specs = [pl.BlockSpec((SOURCES, TOK, D), lambda i: (i, 0, 0)), tile]
+    outs = [shape((SLOTS, D) if last else (EXPERTS, TOK, D), BF), shape((SLOTS, D), BF)]
+    dense = pl.BlockSpec((SOURCES, TOK, D), lambda i: (i, 0, 0))
+    out_specs = [tile if last else dense, tile]
     if m > 0:
         ins.append(prev)
         in_specs.append(fixed((3, D, F)))
     if last:
-        outs += [shape((3, D, 128), F32)] + [shape((3, D, 128), BF)] * 3
-        out_specs += [fixed((3, D, 128))] * 4
+        outs.append(shape((SHARDS, 3, D, 128), BF))
+        out_specs.append(fixed((SHARDS, 3, D, 128)))
     else:
         outs.append(shape((3, D, F), F32))
         out_specs.append(fixed((3, D, F)))
@@ -377,37 +383,42 @@
         out_shape=outs,
         scratch_shapes=[pltpu.VMEM((D, F), BF)] * 3 + [pltpu.VMEM((3, D, F), F32)],
         compiler_params=pltpu.CompilerParams(
-            vmem_limit_bytes=56 * 1024 * 1024, dimension_semantics=("arbitrary",)
+            vmem_limit_bytes=63 * 1024 * 1024, dimension_semantics=("arbitrary",)
         ),
         cost_estimate=cost(MICROSECONDS["expert"]),
         name="expert",
     )(*ins)
 
 
-def returned_body(back, c01, middle, gains, dy, branch_ref, gain_ref):
+def returned_body(m, back, c01, middle, gains, dy, branch_ref, gain_ref):
     upstream = dot(c01[...], back[...])
     mid = middle[...]
     r = lax.rsqrt(jnp.mean(mid * mid, axis=-1, keepdims=True) + EPS)
     scaled = upstream * gains[8:9, :]
     grad = r * scaled - mid * (r * r * r) * jnp.mean(scaled * mid, axis=-1, keepdims=True)
-    branch_ref[...] = (dy[0:TOK, :].astype(F32) + grad).astype(BF)
+    branch_ref[...] = (dy[m, 0:TOK, :].astype(F32) + grad).astype(BF)
     gain_ref[...] = jnp.broadcast_to(jnp.sum(upstream * mid * r, axis=0, keepdims=True), (8, D))
 
 
-def block_body(mixture, middle, out_ref):
-    out_ref[...] = (middle[...] + mixture[...].astype(F32)).astype(BF)
-
-
-def place_body(micro, place, order, *refs):
+def block_body(micro, mixture, slots, c01, *refs):
+    for m in range(micro - 1):
+        refs[-1][m] = (refs[m][...] + mixture[...].astype(F32)).astype(BF)
+    refs[-1][micro - 1] = (refs[micro - 1][...] + dot(c01[...], slots[...])).astype(BF)
+
+
+def place_body(micro, place, order, rows, out_ref):
+    given = iota((TOK, GT), 0) + TOK * x_of(place)
     for m in range(micro):
-        deal = given_by_dealt(order, m, x_of(place), TOK)
-        refs[-1][m] = dot(deal, stack(refs[SHARDS * m : SHARDS * (m + 1)])).astype(BF)
+        deal = jnp.where(given == order[m], 1.0, 0.0).astype(BF)
+        dealt = jnp.concatenate([rows[s, m] for s in range(SHARDS)], axis=0)
+        out_ref[m] = dot(deal, dealt).astype(BF)
 
 
 def attend_back_body(m, last, place, lengths, order, g0, g1, g2, g3, xr, qkv_ref, mixed, mass, w, wo, *refs):
     x, first_length = x_of(place), lengths[m, 0, 0]
     if last:
         prev_w, prev_o, gain0, gain1, *refs = refs
+        before, refs = refs[:4], refs[4:]
     o0, o1, o2, o3, given_ref, *refs = refs
     deal = given_by_dealt(order, m, x)
     branch = stack((g0, g1, g2, g3))
@@ -443,7 +454,11 @@
     part = dot(grad_qkv, w[...], 1, 1).astype(BF)
     part = dot(deal, part).astype(BF)
     for k, out in enumerate((o0, o1, o2, o3)):
-        out[...] = part[k * TOK : (k + 1) * TOK]
+        if last:
+            out[0] = before[k][...]
+            out[1] = part[k * TOK : (k + 1) * TOK]
+        else:
+            out[...] = part[k * TOK : (k + 1) * TOK]
     if not last:
         sum_w_ref, sum_o_ref = refs
         sum_w_ref[...] = sum_w
@@ -467,22 +482,21 @@
             ref[6 * 256 + j * 16 : 6 * 256 + (j + 1) * 16, :] = tile.astype(ref.dtype)
 
 
-def tokens_body(micro, tokens, gains, *refs):
+def tokens_body(micro, tokens, gains, p0, p1, p2, p3, *refs):
     for m in range(micro):
-        p0, p1, p2, p3, given = refs[5 * m : 5 * m + 5]
-        upstream = (p0[...].astype(F32) + p1[...].astype(F32)) + (
-            p2[...].astype(F32) + p3[...].astype(F32)
+        upstream = (p0[m].astype(F32) + p1[m].astype(F32)) + (
+            p2[m].astype(F32) + p3[m].astype(F32)
         )
         v = tokens[m].astype(F32)
         r = lax.rsqrt(jnp.mean(v * v, axis=-1, keepdims=True) + EPS)
         scaled = upstream * gains[0:1, :]
         grad = r * scaled - v * (r * r * r) * jnp.mean(scaled * v, axis=-1, keepdims=True)
-        refs[-1][m] = (given[...].astype(F32) + grad).astype(BF)
-
-
-def weight_sums_body(own, r1, r2, r3, *outs):
+        refs[-1][m] = (refs[m][...].astype(F32) + grad).astype(BF)
+
+
+def weight_sums_body(sums, *outs):
     for j in range(3):
-        outs[j][0] = (own[j] + r1[j].astype(F32)) + (r2[j].astype(F32) + r3[j].astype(F32))
+        outs[j][0] = sums[j].astype(F32)
 
 
 def weight_stack_body(a, b, c, out_ref):
@@ -662,7 +676,7 @@
     experts = jnp.swapaxes(routes, 1, 2)
     gates = jnp.swapaxes(gate_weights, 1, 2)
 
-    cot_rows = gather_x(cotangent[0])
+    cot_rows = gather_x(cotangent)
     *packs, tokens_first = run(
         "pack",
         pack_body,
@@ -685,42 +699,38 @@
     routed = run(
         "route",
         functools.partial(route_body, micro),
-        [shape((TOK, D), BF)] * (2 * micro - 2)
+        [shape((TOK, D), BF)] * (micro - 1)
         + [shape((TOK, SLOTS), BF), shape((SLOTS, TOK), BF)] * micro,
-        [experts, cap, tokens, cotangent],
+        [experts, cap, tokens],
         after=[pack_done],
     )
-    later, routed = routed[: 2 * micro - 2], routed[2 * micro - 2 :]
+    token_copies, routed = routed[: micro - 1], routed[micro - 1 :]
     routed = [routed[2 * m : 2 * m + 2] for m in range(micro)]
 
-    attended, left, reached, dealt_cot, cot_all = [], [], [], [], []
-    w_qkv = gains = weights = weight_blocks = parts = None
+    weights = run(
+        "weight_stack",
+        weight_stack_body,
+        [shape((2, 3, D // 2, 128), BF)],
+        [w_gate, w_up, w_down],
+        after=routed[0][:1],
+    )[0]
+    attended, left, reached = [], [], []
+    w_qkv = gains = weight_blocks = None
+
+    dealt_cot = run(
+        "deal",
+        functools.partial(deal_body, micro),
+        [shape((micro, TOK + NOTES, D), BF)],
+        [place, order, experts, gates, *cot_rows],
+        smem=(0,),
+        after=[pack_done, routed[0][0]],
+    )[0]
+    cot_all = lax.all_gather(dealt_cot, "expert", axis=0)
     for m in range(micro):
         first = m == 0
         if not first:
-            cot_rows = gather_x(hold([later[2 * m - 1]], *packs[1:], *token_rows[1:])[0])
-            token_rows = gather_x(hold([later[2 * m - 2]], left[-1][1])[0])
-        dealt_cot.append(
-            run(
-                "deal",
-                functools.partial(deal_body, m),
-                [shape((TOK + NOTES, D), BF)],
-                [place, order, experts, gates, *cot_rows],
-                smem=(0,),
-                after=[pack_done, routed[0][0]] if first else parts[1:2],
-            )[0]
-        )
-        cot_all.append(lax.all_gather(dealt_cot[m], "expert", axis=0))
-        if first:
-            weights = run(
-                "weight_stack",
-                weight_stack_body,
-                [shape((2, 3, D // 2, 128), BF)],
-                [w_gate, w_up, w_down],
-                after=dealt_cot,
-            )[0]
-        elif m == 1:
-            weight_blocks = gather_ring(hold([weights], *parts[1:])[0])
+            token_rows = gather_x(hold([token_copies[m - 1]], left[-1][1])[0])
+            weight_blocks = gather_ring(hold([weights], *token_rows[1:])[0])
         outs = [shape((TOK, D), BF)] * 5 + [
             shape((GT, D), BF),
             shape((GT, COLS), BF),
@@ -735,7 +745,7 @@
             outs,
             [place, lengths, order, *token_rows, w_out, *(packs if first else (w_qkv, gains))],
             smem=(0, 1),
-            after=[weights] if first else [dealt_cot[m], *weight_blocks[1:3]],
+            after=[dealt_cot] if first else [],
         )
         if first:
             w_qkv, gains = result[9:]
@@ -747,7 +757,7 @@
                 leave_body,
                 [shape((TOK, D), F32), shape((SLOTS, D), BF)],
                 [*parts, result[4], gains, routed[m][1]],
-                after=[] if first else weight_blocks[3:],
+                after=[weights] if first else weight_blocks[1:3],
             )
         )
         reached.append(exchange(left[m][1]))
@@ -760,51 +770,50 @@
             place,
             cap,
             reached[m],
-            cot_all[m],
+            cot_all,
             weight_blocks,
             sums,
             after=[left[-1][1]] if m == 0 else [],
         )
-        dense, back = hold(result[:2], backs[m - 1] if m else reached[-1])
-        mixtures.append(sum_over_experts(dense.reshape(-1, D)))
+        if m < micro - 1:
+            dense, back = hold(result[:2], reached[-1])
+            mixtures.append(sum_over_experts(dense.reshape(-1, D)))
+        else:
+            last_out, back = result[0], hold([result[1]], backs[m - 1])[0]
         backs.append(exchange(back))
-        sums = result[2] if m < micro - 1 else result[2:]
-
-    def block_of(m, after):
-        return run(
-            "block",
-            block_body,
-            [shape((TOK, D), BF)],
-            [mixtures[m], left[m][0]],
-            after=after,
-        )[0]
+        sums = result[2]
 
     sum_w = sum_o = None
-    gain_sums, grad_parts = [], []
+    gain_sums, givens = [], []
     for m in range(micro):
         last = m == micro - 1
         branch, gain_sum = run(
             "returned",
-            returned_body,
+            functools.partial(returned_body, m),
             [shape((TOK, D), BF), shape((8, D), F32)],
-            [backs[m], routed[m][0], left[m][0], gains, dealt_cot[m]],
-            after=() if m == 0 else (sum_w, totals[0]),
+            [backs[m], routed[m][0], left[m][0], gains, dealt_cot],
+            after=() if m == 0 else (sum_w,),
         )
         branch_rows = gather_x(branch)
-        if not last:
-            block_rows = gather_x(block_of(0, [branch]))
+        if last:
+            mixtures.append(exchange(hold([last_out], branch)[0]))
+        else:
+            sums = lax.psum_scatter(
+                sums.reshape(-1, 128), "shard", scatter_dimension=0, tiled=True
+            )
             totals = run(
                 "weight_sums",
                 weight_sums_body,
                 [shape((1, D, 128), F32)] * 3,
-                scatter_x(sums),
+                [sums.reshape(3, D, 128)],
             )
         gain_sums.append(gain_sum)
         ins = [place, lengths, order, *branch_rows, *attended[m][5:9], w_qkv, w_out]
         out_shapes = [shape((TOK, D), BF)] * 5
         scratch = []
         if last:
-            ins += [sum_w, sum_o, *gain_sums]
+            ins += [sum_w, sum_o, *gain_sums, *parts]
+            out_shapes = [shape((micro, TOK, D), BF)] * 4 + out_shapes[4:]
             out_shapes += [shape((BLOCKS * 256, 256), F32), shape((BLOCKS * 256, 256), BF)]
             scratch = [pltpu.VMEM((D, COLS), F32), pltpu.VMEM((ROWS_HERE, D), F32)]
         else:
@@ -818,10 +827,9 @@
             scratch=scratch,
         )
         sum_w, sum_o = result[5:7]
-        if last:
-            last_parts, last_given = result[:4], result[4]
-        else:
-            grad_parts += [*scatter_x(result[:4]), result[4]]
+        parts = result[:4]
+        givens.append(result[4])
+
     four = [0, 1, 2, 3]
     rows = BLOCKS * 64
     split_y = run(
@@ -831,30 +839,39 @@
         [place, sum_w, swap_core(sum_o)],
         smem=(0,),
     )
-    grad_parts += [*scatter_x(hold(last_parts, split_y[0])), last_given]
-    grad_tokens = run(
-        "tokens",
-        functools.partial(tokens_body, micro),
-        [shape(tokens.shape, BF)],
-        [tokens, gains, *grad_parts],
-    )[0]
     pieces = [split_y[0]] + [along(split_y[k], lambda z, y, c, k=k: (z, y + k, c)) for k in four[1:]]
     rows = BLOCKS * 16
-    pieces = run(
+    split_z, *pieces = run(
         "split_z",
         split_z_body,
         [shape((rows, 256), F32)] + [shape((rows, 256), BF)] * 3,
         [place, *pieces],
         smem=(0,),
     )
-    pieces = [pieces[0]] + [along(pieces[k], lambda z, y, c, k=k: (z + k, y, c)) for k in four[1:]]
+    pieces = [split_z] + [
+        along(pieces[k - 1], lambda z, y, c, k=k: (z + k, y, c)) for k in four[1:]
+    ]
+    blocks = run(
+        "block",
+        functools.partial(block_body, micro),
+        [shape((micro, TOK, D), BF)],
+        [*mixtures, routed[-1][0], *[left[m][0] for m in range(micro)]],
+        after=[split_z],
+    )[0]
+    block_out = run(
+        "place",
+        functools.partial(place_body, micro),
+        [shape(tokens.shape, BF)],
+        [place, order, lax.all_gather(blocks, "shard", axis=0)],
+        smem=(0,),
+    )[0]
     o_piece, *pieces = run(
         "split_x",
         split_x_body,
         [shape((32, 256), BF), shape((32, 256), F32)] + [shape((32, 256), BF)] * 3,
         [place, *pieces],
         smem=(0,),
-        after=[grad_tokens],
+        after=[blocks],
     )
     piece, gain_ffn_sum = run(
         "join_x",
@@ -863,6 +880,12 @@
         [place, o_piece, *scatter_x(pieces)],
         smem=(0,),
     )
+    grad_tokens = run(
+        "tokens",
+        functools.partial(tokens_body, micro),
+        [shape(tokens.shape, BF)],
+        [tokens, gains, *scatter_x(hold(parts, piece)), *givens],
+    )[0]
     for name, index_of, step in (
         ("join_z", z_of, lambda z, y, c, k: (z - k, y, c)),
         ("join_y", y_of, lambda z, y, c, k: (z, y - k, c)),
@@ -876,8 +899,8 @@
             [shape((4 * piece.shape[0], 256), BF)],
             [place, *pieces],
             smem=(0,),
+            after=[grad_tokens] if name == "join_y" else [],
         )[0]
-    block_rows += gather_x(block_of(1, [piece]))
     grad_query, grad_key, grad_value, grad_out, grad_gain = run(
         "weights",
         weights_body,
@@ -900,13 +923,6 @@
         smem=(0,),
     )
 
-    block_out = run(
-        "place",
-        functools.partial(place_body, micro),
-        [shape(tokens.shape, BF)],
-        [place, order, *block_rows],
-        smem=(0,),
-    )[0]
     return (
         block_out,
         grad_tokens,

time: 508 us -> 484 us (0.953)
  waiting for transfers between devices: 206 us -> 180 us
  starting transfers between devices: 98.4 us -> 115 us
  local copies, waits for them, and re-layouts: 23.5 us -> 14.6 us
    ppermute x18 -> x12, waiting for transfers between devices: 69 us -> 50.9 us  [to_right(): lax.ppermute(v, 'shard', [(i, (i + k) % SHARDS) for i in range(SHARDS)])]
    all_to_all x4 -> x5, waiting for transfers between devices: 15.7 us -> 32 us  [exchange(): return lax.all_to_all(v, 'expert', split_axis=0, concat_axis=0, tiled=True)]
    ppermute x31 -> x22, waiting for transfers between devices: 93.5 us -> 77.5 us  [from_right(): lax.ppermute(v, 'shard', [(i, (i - k) % SHARDS) for i in range(SHARDS)])]
    all_to_all x4 -> x5, starting transfers between devices: 32 us -> 42.1 us  [exchange(): return lax.all_to_all(v, 'expert', split_axis=0, concat_axis=0, tiled=True)]
    ppermute x14, waiting for transfers between devices: 27.6 us -> 19.1 us  [along(): return lax.ppermute(v, 'expert', pairs)]
    unnamed x144 -> x96, local copies, waits for them, and re-layouts: 19.1 us -> 12.2 us
    ppermute x14, starting transfers between devices: 19.3 us -> 25 us  [along(): return lax.ppermute(v, 'expert', pairs)]
    ppermute x18 -> x12, starting transfers between devices: 12.9 us -> 15.5 us  [to_right(): lax.ppermute(v, 'shard', [(i, (i + k) % SHARDS) for i in range(SHARDS)])]
  transfers between devices with their start and end apart: 71 -> 57, of which waited for: 43 -> 31; matrix products, arithmetic and copies ran while one was open for 1% -> 1% of each run, Pallas kernels for 30% -> 30%
where the time goes in v3:
time: 484 us; the launch traced here: 474 us
  waiting for transfers between devices  180 us (37%)
  Pallas kernels  150 us (31%)
  starting transfers between devices  115 us (24%)
  local copies, waits for them, and re-layouts  14.6 us (3%)
  between operations  14.6 us (3%)
    pallas_call x23, Pallas kernels, run(): pl.pallas_call(whole, out_shape=outs, in_specs=[SMEM if i in smem else VM...  90.7 us
    ppermute x22, waiting for transfers between devices, from_right(): lax.ppermute(v, 'shard', [(i, (i - k) % SHARDS) for i in range(SHARDS)])  77.5 us
    pallas_call x2, Pallas kernels, expert_call(): pl.pallas_call(functools.partial(expert_body, m, last, len(after)), grid=...  58.9 us
    ppermute x12, waiting for transfers between devices, to_right(): lax.ppermute(v, 'shard', [(i, (i + k) % SHARDS) for i in range(SHARDS)])  50.9 us
    all_to_all x5, starting transfers between devices, exchange(): return lax.all_to_all(v, 'expert', split_axis=0, concat_axis=0, tiled=True)  42.1 us
    ppermute x22, starting transfers between devices, from_right(): lax.ppermute(v, 'shard', [(i, (i - k) % SHARDS) for i in range(SHARDS)])  32.2 us
    all_to_all x5, waiting for transfers between devices, exchange(): return lax.all_to_all(v, 'expert', split_axis=0, concat_axis=0, tiled=True)  32 us
    ppermute x14, starting transfers between devices, along(): return lax.ppermute(v, 'expert', pairs)  25 us
  transfers between devices with their start and end apart: 57, of which 31 were waited for; matrix products, arithmetic and copies ran while one was open for 1% of the time, Pallas kernels for 30%

profile of v3, /device:TPU:1, one launch (start us, length us, event | category | flops | bytes accessed | tf_op | source)
XLA Modules:
  0.0 474.1 jit_solution(18193149765200263532)
XLA Ops:
  22.3 11.8 %collective-permute-done.refs_5_ = bf16[2,128,1024]{2,1,0:T(8,128)(2,1)} collective-permute-done((bf16[2,128,1024]{2,1,0:T(8,128)(2,1)}, bf16[2,128,1024]{2,1,0:T(8,128)(2,1)}, u32[]{:S(2)}, u32[]{:S(2)}) %collective-permute-start) | collective-permute-done | bytes 524320 | tf_op jit(solution)/shard_map/ppermute | solution.py:601
  48.1 17.3 %collective-permute-done.4.refs_5_ = bf16[128,1024]{1,0:T(8,128)(2,1)S(1)} collective-permute-done((bf16[128,1024]{1,0:T(8,128)(2,1)}, bf16[128,1024]{1,0:T(8,128)(2,1)S(1)}, u32[]{:S(2)}, u32[]{:S(2)}) %collective-permute-start.4) | collective-permute-done | bytes 262176 | tf_op jit(solution)/shard_map/ppermute | solution.py:601
  66.9 7.4 %attend.2 = (bf16[128,1024]{1,0:T(8,128)(2,1)}, bf16[128,1024]{1,0:T(8,128)(2,1)}, bf16[128,1024]{1,0:T(8,128)(2,1)}, bf16[128,1024]{1,0:T(8,128)(2,1)}, bf16[12...) custom-call(s32[1]{0:T(128)} %bitcast.refs_0_.refs_1_, ...), custom_call_target="tpu_custom_call" | custom-call | flops 1 | bytes 26280000 | tf_op jit(solution)/shard_map/attend/pallas_call | solution.py:87
  82.0 7.9 %collective-permute-done.10.refs_2_ = bf16[128,1024]{1,0:T(8,128)(2,1)S(1)} collective-permute-done((bf16[128,1024]{1,0:T(8,128)(2,1)}, bf16[128,1024]{1,0:T(8,128)(2,1)S(1)}, u32[]{:S(2)}, u32[]{:S(2)}) %collective-permute-start.10) | collective-permute-done | bytes 262176 | tf_op jit(solution)/shard_map/ppermute | solution.py:605
  90.8 4.5 leave.2
  95.3 9.4 %all-to-all-start = ((bf16[32,48,1024]{2,1,0:T(8,128)(2,1)}), bf16[32,48,1024]{2,1,0:T(8,128)(2,1)}, u32[]{:S(2)}, u32[]{:S(2)}) async-start(bf16[32,48,1024]{2,1,0:T(8,128)(2,1)} %bitcast.25), calls=%async_computation | async-start | bytes 6291456 | tf_op jit(solution)/shard_map/all_to_all | solution.py:652
  108.3 5.9 %collective-permute-done.14.refs_6_.refs_3_ = bf16[128,1024]{1,0:T(8,128)(2,1)S(1)} collective-permute-done((bf16[128,1024]{1,0:T(8,128)(2,1)}, bf16[128,1024]{1,0:T(8,128)(2,1)S(1)}, u32[]{:S(2)}, u32[]{:S(2)}) %collective-permute-start.14) | collective-permute-done | bytes 262176 | tf_op jit(solution)/shard_map/ppermute | solution.py:601
  114.2 6.2 %collective-permute-done.13.refs_5_.refs_2_ = bf16[128,1024]{1,0:T(8,128)(2,1)S(1)} collective-permute-done((bf16[128,1024]{1,0:T(8,128)(2,1)}, bf16[128,1024]{1,0:T(8,128)(2,1)S(1)}, u32[]{:S(2)}, u32[]{:S(2)}) %collective-permute-start.13) | collective-permute-done | bytes 262176 | tf_op jit(solution)/shard_map/ppermute | solution.py:601
  124.4 7.1 %attend.3 = (bf16[128,1024]{1,0:T(8,128)(2,1)}, bf16[128,1024]{1,0:T(8,128)(2,1)}, bf16[128,1024]{1,0:T(8,128)(2,1)}, bf16[128,1024]{1,0:T(8,128)(2,1)}, bf16[12...) custom-call(s32[1]{0:T(128)} %bitcast.refs_0_.refs_1_, ...), custom_call_target="tpu_custom_call" | custom-call | flops 1 | bytes 26280000 | tf_op jit(solution)/shard_map/attend/pallas_call | solution.py:87
  134.5 12.5 %collective-permute-done.15.refs_1_ = bf16[128,1024]{1,0:T(8,128)(2,1)S(1)} collective-permute-done((bf16[128,1024]{1,0:T(8,128)(2,1)}, bf16[128,1024]{1,0:T(8,128)(2,1)S(1)}, u32[]{:S(2)}, u32[]{:S(2)}) %collective-permute-start.15) | collective-permute-done | bytes 262176 | tf_op jit(solution)/shard_map/ppermute | solution.py:605
  146.9 7.1 %collective-permute-done.16.refs_2_ = bf16[128,1024]{1,0:T(8,128)(2,1)S(1)} collective-permute-done((bf16[128,1024]{1,0:T(8,128)(2,1)}, bf16[128,1024]{1,0:T(8,128)(2,1)S(1)}, u32[]{:S(2)}, u32[]{:S(2)}) %collective-permute-start.16) | collective-permute-done | bytes 262176 | tf_op jit(solution)/shard_map/ppermute | solution.py:605
  155.1 4.3 leave.3
  159.3 8.4 %all-to-all-start.1 = ((bf16[32,48,1024]{2,1,0:T(8,128)(2,1)}), bf16[32,48,1024]{2,1,0:T(8,128)(2,1)}, u32[]{:S(2)}, u32[]{:S(2)}) async-start(bf16[32,48,1024]{2,1,0:T(8,128)(2,1)} %bitcast.28), calls=%async_computation.1 | async-start | bytes 6291456 | tf_op jit(solution)/shard_map/all_to_all | solution.py:652
  172.1 7.6 %collective-permute-done.21.refs_9_.refs_8_ = bf16[1,3,512,128]{3,2,1,0:T(8,128)(2,1)S(1)} collective-permute-done((bf16[1,3,512,128]{3,2,1,0:T(8,128)(2,1)S(1)}, bf16[1,3,512,128]{3,2,1,0:T(8,128)(2,1)S(1)}, u32[]{:S(2)}, u32[]{:S(2)}) %collective-permute-start.21) | collective-permute-done | bytes 393248 | tf_op jit(solution)/shard_map/ppermute | solution.py:601
  180.7 29.9 %expert.2 = (bf16[32,128,1024]{2,1,0:T(8,128)(2,1)}, bf16[1536,1024]{1,0:T(8,128)(2,1)}, f32[3,1024,512]{2,1,0:T(8,128)}) custom-call(bf16[1536,1024]{1,0:T(8,128)(2,1)} %get-tuple-element.130.refs_0_, s32[1]{0:T(128)} %bitcast.refs_0_.refs_1_, s32[1,32]{1,0:T(1,128)} %bitcast.36, bf16[1536,1024]{1,0:T(8,128)(2,1)} %bitcast.5.refs_3_, ...), custom_call_target="tpu_custom_call" | custom-call | flops 1 | bytes 97200000 | tf_op jit(solution)/shard_map/expert/pallas_call | solution.py:378
  210.7 8.5 %all-to-all-start.2 = ((bf16[32,48,1024]{2,1,0:T(8,128)(2,1)}), bf16[32,48,1024]{2,1,0:T(8,128)(2,1)}, u32[]{:S(2)}, u32[]{:S(2)}) async-start(bf16[32,48,1024]{2,1,0:T(8,128)(2,1)} %bitcast.10), calls=%async_computation.3 | async-start | bytes 6291456 | tf_op jit(solution)/shard_map/all_to_all | solution.py:652
  219.3 29.0 %expert.3 = (bf16[1536,1024]{1,0:T(8,128)(2,1)}, bf16[1536,1024]{1,0:T(8,128)(2,1)}, bf16[4,3,1024,128]{3,2,1,0:T(8,128)(2,1)}) custom-call(s32[1]{0:T(128)} %bitcast.refs_0_.refs_1_, s32[1,32]{1,0:T(1,128)} %bitcast.37, bf16[1536,1024]{1,0:T(8,128)(2,1)} %bitcast.8.refs_2_, bf16[32,2,144,1024]{3,2,1,0:T(8,128)(2,1)} %bitcast.23, ...), custom_call_target="tpu_custom_call" | custom-call | flops 1 | bytes 97200000 | tf_op jit(solution)/shard_map/expert/pallas_call | solution.py:378
  248.3 10.2 %all-to-all-done.2 = bf16[32,48,1024]{2,1,0:T(8,128)(2,1)} async-done(((bf16[32,48,1024]{2,1,0:T(8,128)(2,1)}), bf16[32,48,1024]{2,1,0:T(8,128)(2,1)}, u32[]{:S(2)}, u32[]{:S(2)}) %all-to-all-start.2) | async-done | bytes 3145760 | tf_op jit(solution)/shard_map/all_to_all | solution.py:652
  258.5 7.5 %all-to-all-start.3 = ((bf16[32,48,1024]{2,1,0:T(8,128)(2,1)}), bf16[32,48,1024]{2,1,0:T(8,128)(2,1)}, u32[]{:S(2)}, u32[]{:S(2)}) async-start(bf16[32,48,1024]{2,1,0:T(8,128)(2,1)} %bitcast.27), calls=%async_computation.4 | async-start | bytes 6291456 | tf_op jit(solution)/shard_map/all_to_all | solution.py:652
  270.4 4.0 collective-permute-start.23
  274.3 5.5 %collective-permute-done.24.refs_6_ = bf16[128,1024]{1,0:T(8,128)(2,1)S(1)} collective-permute-done((bf16[128,1024]{1,0:T(8,128)(2,1)}, bf16[128,1024]{1,0:T(8,128)(2,1)S(1)}, u32[]{:S(2)}, u32[]{:S(2)}) %collective-permute-start.24) | collective-permute-done | bytes 262176 | tf_op jit(solution)/shard_map/ppermute | solution.py:601
  279.8 6.5 %collective-permute-done.23.refs_5_ = bf16[128,1024]{1,0:T(8,128)(2,1)S(1)} collective-permute-done((bf16[128,1024]{1,0:T(8,128)(2,1)}, bf16[128,1024]{1,0:T(8,128)(2,1)S(1)}, u32[]{:S(2)}, u32[]{:S(2)}) %collective-permute-start.23) | collective-permute-done | bytes 262176 | tf_op jit(solution)/shard_map/ppermute | solution.py:601
  287.1 9.3 %attend_back.2 = (bf16[128,1024]{1,0:T(8,128)(2,1)}, bf16[128,1024]{1,0:T(8,128)(2,1)}, bf16[128,1024]{1,0:T(8,128)(2,1)}, bf16[128,1024]{1,0:T(8,128)(2,1)}, bf...) custom-call(s32[1]{0:T(128)} %bitcast.refs_0_.refs_1_, s32[2,1,2]{2,1,0:T(1,128)} %refs_1_.14, ...), custom_call_target="tpu_custom_call" | custom-call | flops 1 | bytes 39600000 | tf_op jit(solution)/shard_map/attend_back/pallas_call | solution.py:87
  296.4 21.8 %all-to-all-done.3 = bf16[32,48,1024]{2,1,0:T(8,128)(2,1)} async-done(((bf16[32,48,1024]{2,1,0:T(8,128)(2,1)}), bf16[32,48,1024]{2,1,0:T(8,128)(2,1)}, u32[]{:S(2)}, u32[]{:S(2)}) %all-to-all-start.3) | async-done | bytes 3145760 | tf_op jit(solution)/shard_map/all_to_all | solution.py:652
  322.0 8.3 %all-to-all-start.4 = ((bf16[32,48,1024]{2,1,0:T(8,128)(2,1)}), bf16[32,48,1024]{2,1,0:T(8,128)(2,1)}, u32[]{:S(2)}, u32[]{:S(2)}) async-start(bf16[32,48,1024]{2,1,0:T(8,128)(2,1)} %bitcast.26), calls=%async_computation.5 | async-start | bytes 6291456 | tf_op jit(solution)/shard_map/all_to_all | solution.py:652
  335.0 4.2 collective-permute-done.27.refs_6_
  339.2 6.6 %collective-permute-done.26.refs_5_ = bf16[128,1024]{1,0:T(8,128)(2,1)S(1)} collective-permute-done((bf16[128,1024]{1,0:T(8,128)(2,1)S(1)}, bf16[128,1024]{1,0:T(8,128)(2,1)S(1)}, u32[]{:S(2)}, u32[]{:S(2)}) %collective-permute-start.26) | collective-permute-done | bytes 262176 | tf_op jit(solution)/shard_map/ppermute | solution.py:601
  346.6 12.2 %attend_back.3 = (bf16[2,128,1024]{2,1,0:T(8,128)(2,1)}, bf16[2,128,1024]{2,1,0:T(8,128)(2,1)}, bf16[2,128,1024]{2,1,0:T(8,128)(2,1)}, bf16[2,128,1024]{2,1,0:T(...) custom-call(s32[1]{0:T(128)} %bitcast.refs_0_.refs_1_, ...), custom_call_target="tpu_custom_call" | custom-call | flops 1 | bytes 39600000 | tf_op jit(solution)/shard_map/attend_back/pallas_call | solution.py:87
  371.0 4.3 collective-permute-done.29.refs_2_
  375.3 5.5 %collective-permute-done.30.refs_3_ = bf16[448,256]{1,0:T(8,128)(2,1)S(1)} collective-permute-done((bf16[448,256]{1,0:T(8,128)(2,1)}, bf16[448,256]{1,0:T(8,128)(2,1)S(1)}, u32[]{:S(2)}, u32[]{:S(2)}) %collective-permute-start.30) | collective-permute-done | bytes 229408 | tf_op jit(solution)/shard_map/ppermute | solution.py:640
  422.8 20.3 %collective-permute-done.39.refs_4_ = bf16[2,128,1024]{2,1,0:T(8,128)(2,1)} collective-permute-done((bf16[2,128,1024]{2,1,0:T(8,128)(2,1)}, bf16[2,128,1024]{2,1,0:T(8,128)(2,1)}, u32[]{:S(2)}, u32[]{:S(2)}) %collective-permute-start.39) | collective-permute-done | bytes 524320 | tf_op jit(solution)/shard_map/ppermute | solution.py:605
  449.3 7.1 %collective-permute-start.47 = (bf16[1536,256]{1,0:T(8,128)(2,1)}, bf16[1536,256]{1,0:T(8,128)(2,1)S(1)}, u32[]{:S(2)}, u32[]{:S(2)}) collective-permute-start(bf16[1536,256]{1,0:T(8,128)(2,1)} %join_y.1.refs_1_), channel_id=1, source_target_pairs={{0,4},{4,0},{8,12},{12,8},{16,20},{20,16},{24,28},{28,24},{32,36},... | collective-permute-start | bytes 2359304 | tf_op jit(solution)/shard_map/ppermute | solution.py:640
  (220 shorter events, 141.7 us)
Async XLA Ops:
  7.2 172.8 %all-gather.5.cloned.1.call-start = ((), (), s32[]{:S(2)}) async-start(), calls=%async_computation.9 | async-start | bytes 19464192 | tf_op jit(solution)/shard_map/all_gather | solution.py:728
  7.2 15.1 %collective-permute-start.1 = (bf16[2,128,1024]{2,1,0:T(8,128)(2,1)}, bf16[2,128,1024]{2,1,0:T(8,128)(2,1)S(1)}, u32[]{:S(2)}, u32[]{:S(2)}) collective-permute-start(bf16[2,128,1024]{2,1,0:T(8,128)(2,1)} %refs_4_.2), channel_id=1, source_target_pairs={{0,2},{1,3},{2,0},{3,1},{4,6},{5,7},{6,4},{7,5},{8,10},{9,11},{10,... | collective-permute-start | bytes 1572872 | tf_op jit(solution)/shard_map/ppermute | solution.py:601
  10.9 23.2 %collective-permute-start = (bf16[2,128,1024]{2,1,0:T(8,128)(2,1)}, bf16[2,128,1024]{2,1,0:T(8,128)(2,1)}, u32[]{:S(2)}, u32[]{:S(2)}) collective-permute-start(bf16[2,128,1024]{2,1,0:T(8,128)(2,1)} %refs_4_.2), channel_id=1, source_target_pairs={{0,3},{1,0},{2,1},{3,2},{4,7},{5,4},{6,5},{7,6},{8,11},{9,8},{10,9... | collective-permute-start | bytes 1572872 | tf_op jit(solution)/shard_map/ppermute | solution.py:601
  11.7 23.1 %collective-permute-start.2 = (bf16[2,128,1024]{2,1,0:T(8,128)(2,1)}, bf16[2,128,1024]{2,1,0:T(8,128)(2,1)}, u32[]{:S(2)}, u32[]{:S(2)}) collective-permute-start(bf16[2,128,1024]{2,1,0:T(8,128)(2,1)} %refs_4_.2), channel_id=1, source_target_pairs={{0,1},{1,2},{2,3},{3,0},{4,5},{5,6},{6,7},{7,4},{8,9},{9,10},{10,1... | collective-permute-start | bytes 1572872 | tf_op jit(solution)/shard_map/ppermute | solution.py:601
  39.2 26.2 %collective-permute-start.6 = (bf16[272,512]{1,0:T(8,128)(2,1)}, bf16[272,512]{1,0:T(8,128)(2,1)S(1)}, u32[]{:S(2)}, u32[]{:S(2)}) collective-permute-start(bf16[272,512]{1,0:T(8,128)(2,1)} %get-tuple-element.111), channel_id=1, source_target_pairs={{0,3},{1,0},{2,1},{3,2},{4,7},{5,4},{6,5},{7,6},{8,11},{9,8},{10,9... | collective-permute-start | bytes 835592 | tf_op jit(solution)/shard_map/ppermute | solution.py:601
  40.6 24.9 %collective-permute-start.7 = (bf16[272,512]{1,0:T(8,128)(2,1)}, bf16[272,512]{1,0:T(8,128)(2,1)S(1)}, u32[]{:S(2)}, u32[]{:S(2)}) collective-permute-start(bf16[272,512]{1,0:T(8,128)(2,1)} %get-tuple-element.112), channel_id=1, source_target_pairs={{0,2},{1,3},{2,0},{3,1},{4,6},{5,7},{6,4},{7,5},{8,10},{9,11},{10,... | collective-permute-start | bytes 835592 | tf_op jit(solution)/shard_map/ppermute | solution.py:601
  42.2 23.2 %collective-permute-start.8 = (bf16[272,512]{1,0:T(8,128)(2,1)}, bf16[272,512]{1,0:T(8,128)(2,1)S(1)}, u32[]{:S(2)}, u32[]{:S(2)}) collective-permute-start(bf16[272,512]{1,0:T(8,128)(2,1)} %get-tuple-element.113), channel_id=1, source_target_pairs={{0,1},{1,2},{2,3},{3,0},{4,5},{5,6},{6,7},{7,4},{8,9},{9,10},{10,1... | collective-permute-start | bytes 835592 | tf_op jit(solution)/shard_map/ppermute | solution.py:601
  42.5 22.9 %collective-permute-start.4 = (bf16[128,1024]{1,0:T(8,128)(2,1)}, bf16[128,1024]{1,0:T(8,128)(2,1)S(1)}, u32[]{:S(2)}, u32[]{:S(2)}) collective-permute-start(bf16[128,1024]{1,0:T(8,128)(2,1)} %get-tuple-element.109.refs_3_), channel_id=1, source_target_pairs={{0,2},{1,3},{2,0},{3,1},{4,6},{5,7},{6,4},{7,5},{8,10},{9,11},{10,... | collective-permute-start | bytes 786440 | tf_op jit(solution)/shard_map/ppermute | solution.py:601
  46.3 19.1 %collective-permute-start.3 = (bf16[128,1024]{1,0:T(8,128)(2,1)}, bf16[128,1024]{1,0:T(8,128)(2,1)S(1)}, u32[]{:S(2)}, u32[]{:S(2)}) collective-permute-start(bf16[128,1024]{1,0:T(8,128)(2,1)} %get-tuple-element.109.refs_3_), channel_id=1, source_target_pairs={{0,3},{1,0},{2,1},{3,2},{4,7},{5,4},{6,5},{7,6},{8,11},{9,8},{10,9... | collective-permute-start | bytes 786440 | tf_op jit(solution)/shard_map/ppermute | solution.py:601
  74.7 15.3 %collective-permute-start.10 = (bf16[128,1024]{1,0:T(8,128)(2,1)}, bf16[128,1024]{1,0:T(8,128)(2,1)S(1)}, u32[]{:S(2)}, u32[]{:S(2)}) collective-permute-start(bf16[128,1024]{1,0:T(8,128)(2,1)} %get-tuple-element.117), channel_id=1, source_target_pairs={{0,2},{1,3},{2,0},{3,1},{4,6},{5,7},{6,4},{7,5},{8,10},{9,11},{10,... | collective-permute-start | bytes 786440 | tf_op jit(solution)/shard_map/ppermute | solution.py:605
  95.3 64.1 %all-to-all-start = ((bf16[32,48,1024]{2,1,0:T(8,128)(2,1)}), bf16[32,48,1024]{2,1,0:T(8,128)(2,1)}, u32[]{:S(2)}, u32[]{:S(2)}) async-start(bf16[32,48,1024]{2,1,0:T(8,128)(2,1)} %bitcast.25), calls=%async_computation | async-start | bytes 6291456 | tf_op jit(solution)/shard_map/all_to_all | solution.py:652
  105.0 15.3 %collective-permute-start.13 = (bf16[128,1024]{1,0:T(8,128)(2,1)}, bf16[128,1024]{1,0:T(8,128)(2,1)S(1)}, u32[]{:S(2)}, u32[]{:S(2)}) collective-permute-start(bf16[128,1024]{1,0:T(8,128)(2,1)} %hold.8.refs_3_), channel_id=1, source_target_pairs={{0,2},{1,3},{2,0},{3,1},{4,6},{5,7},{6,4},{7,5},{8,10},{9,11},{10,... | collective-permute-start | bytes 786440 | tf_op jit(solution)/shard_map/ppermute | solution.py:601
  121.8 32.2 %collective-permute-start.19 = (bf16[2,3,512,128]{3,2,1,0:T(8,128)(2,1)}, bf16[2,3,512,128]{3,2,1,0:T(8,128)(2,1)S(1)}, u32[]{:S(2)}, u32[]{:S(2)}) collective-permute-start(bf16[2,3,512,128]{3,2,1,0:T(8,128)(2,1)} %hold.9.refs_5_.refs_4_), channel_id=1, source_target_pairs={{0,1},{1,2},{2,3},{3,0},{4,5},{5,6},{6,7},{7,4},{8,9},{9,10},{10,1... | collective-permute-start | bytes 2359304 | tf_op jit(solution)/shard_map/ppermute | solution.py:601
  121.8 32.3 %collective-permute-start.18 = (bf16[2,3,512,128]{3,2,1,0:T(8,128)(2,1)}, bf16[2,3,512,128]{3,2,1,0:T(8,128)(2,1)}, u32[]{:S(2)}, u32[]{:S(2)}) collective-permute-start(bf16[2,3,512,128]{3,2,1,0:T(8,128)(2,1)} %hold.9.refs_5_.refs_4_), channel_id=1, source_target_pairs={{0,3},{1,0},{2,1},{3,2},{4,7},{5,4},{6,5},{7,6},{8,11},{9,8},{10,9... | collective-permute-start | bytes 2359304 | tf_op jit(solution)/shard_map/ppermute | solution.py:601
  131.5 15.4 %collective-permute-start.15 = (bf16[128,1024]{1,0:T(8,128)(2,1)}, bf16[128,1024]{1,0:T(8,128)(2,1)S(1)}, u32[]{:S(2)}, u32[]{:S(2)}) collective-permute-start(bf16[128,1024]{1,0:T(8,128)(2,1)} %get-tuple-element.125), channel_id=1, source_target_pairs={{0,1},{1,2},{2,3},{3,0},{4,5},{5,6},{6,7},{7,4},{8,9},{9,10},{10,1... | collective-permute-start | bytes 786440 | tf_op jit(solution)/shard_map/ppermute | solution.py:605
  131.6 22.4 %collective-permute-start.16 = (bf16[128,1024]{1,0:T(8,128)(2,1)}, bf16[128,1024]{1,0:T(8,128)(2,1)S(1)}, u32[]{:S(2)}, u32[]{:S(2)}) collective-permute-start(bf16[128,1024]{1,0:T(8,128)(2,1)} %get-tuple-element.126), channel_id=1, source_target_pairs={{0,2},{1,3},{2,0},{3,1},{4,6},{5,7},{6,4},{7,5},{8,10},{9,11},{10,... | collective-permute-start | bytes 786440 | tf_op jit(solution)/shard_map/ppermute | solution.py:605
  133.8 20.1 %collective-permute-start.17 = (bf16[128,1024]{1,0:T(8,128)(2,1)}, bf16[128,1024]{1,0:T(8,128)(2,1)S(1)}, u32[]{:S(2)}, u32[]{:S(2)}) collective-permute-start(bf16[128,1024]{1,0:T(8,128)(2,1)} %get-tuple-element.127), channel_id=1, source_target_pairs={{0,3},{1,0},{2,1},{3,2},{4,7},{5,4},{6,5},{7,6},{8,11},{9,8},{10,9... | collective-permute-start | bytes 786440 | tf_op jit(solution)/shard_map/ppermute | solution.py:605
  159.3 51.4 %all-to-all-start.1 = ((bf16[32,48,1024]{2,1,0:T(8,128)(2,1)}), bf16[32,48,1024]{2,1,0:T(8,128)(2,1)}, u32[]{:S(2)}, u32[]{:S(2)}) async-start(bf16[32,48,1024]{2,1,0:T(8,128)(2,1)} %bitcast.28), calls=%async_computation.1 | async-start | bytes 6291456 | tf_op jit(solution)/shard_map/all_to_all | solution.py:652
  167.8 216.0 %reduce-scatter.3.cloned.1.call-start = ((), (), s32[]{:S(2)}) async-start(), calls=%async_computation.7 | async-start | bytes 8650752 | tf_op jit(solution)/shard_map/reduce_scatter | solution.py:648
  210.7 47.8 %all-to-all-start.2 = ((bf16[32,48,1024]{2,1,0:T(8,128)(2,1)}), bf16[32,48,1024]{2,1,0:T(8,128)(2,1)}, u32[]{:S(2)}, u32[]{:S(2)}) async-start(bf16[32,48,1024]{2,1,0:T(8,128)(2,1)} %bitcast.10), calls=%async_computation.3 | async-start | bytes 6291456 | tf_op jit(solution)/shard_map/all_to_all | solution.py:652
  219.3 237.9 %reduce-scatter.5.cloned.1.call-start = ((), (), s32[]{:S(2)}) async-start(), calls=%async_computation.8 | async-start | bytes 3932160 | tf_op jit(solution)/shard_map/reduce_scatter | solution.py:801
  258.5 59.7 %all-to-all-start.3 = ((bf16[32,48,1024]{2,1,0:T(8,128)(2,1)}), bf16[32,48,1024]{2,1,0:T(8,128)(2,1)}, u32[]{:S(2)}, u32[]{:S(2)}) async-start(bf16[32,48,1024]{2,1,0:T(8,128)(2,1)} %bitcast.27), calls=%async_computation.4 | async-start | bytes 6291456 | tf_op jit(solution)/shard_map/all_to_all | solution.py:652
  270.4 15.9 %collective-permute-start.23 = (bf16[128,1024]{1,0:T(8,128)(2,1)}, bf16[128,1024]{1,0:T(8,128)(2,1)S(1)}, u32[]{:S(2)}, u32[]{:S(2)}) collective-permute-start(bf16[128,1024]{1,0:T(8,128)(2,1)} %get-tuple-element.141.refs_3_), channel_id=1, source_target_pairs={{0,2},{1,3},{2,0},{3,1},{4,6},{5,7},{6,4},{7,5},{8,10},{9,11},{10,... | collective-permute-start | bytes 786440 | tf_op jit(solution)/shard_map/ppermute | solution.py:601
  322.0 61.7 %all-to-all-start.4 = ((bf16[32,48,1024]{2,1,0:T(8,128)(2,1)}), bf16[32,48,1024]{2,1,0:T(8,128)(2,1)}, u32[]{:S(2)}, u32[]{:S(2)}) async-start(bf16[32,48,1024]{2,1,0:T(8,128)(2,1)} %bitcast.26), calls=%async_computation.5 | async-start | bytes 6291456 | tf_op jit(solution)/shard_map/all_to_all | solution.py:652
  330.3 134.0 %all-gather.7.cloned.1.call-start = ((), (), s32[]{:S(2)}) async-start(), calls=%async_computation.10 | async-start | bytes 2621440 | tf_op jit(solution)/shard_map/all_gather | solution.py:865
  331.1 14.6 %collective-permute-start.26 = (bf16[128,1024]{1,0:T(8,128)(2,1)S(1)}, bf16[128,1024]{1,0:T(8,128)(2,1)S(1)}, u32[]{:S(2)}, u32[]{:S(2)}) collective-permute-start(bf16[128,1024]{1,0:T(8,128)(2,1)S(1)} %copy-done.5), channel_id=1, source_target_pairs={{0,2},{1,3},{2,0},{3,1},{4,6},{5,7},{6,4},{7,5},{8,10},{9,11},{10,... | collective-permute-start | bytes 786440 | tf_op jit(solution)/shard_map/ppermute | solution.py:601
  404.8 17.6 %collective-permute-start.38 = (bf16[2,128,1024]{2,1,0:T(8,128)(2,1)}, bf16[2,128,1024]{2,1,0:T(8,128)(2,1)S(1)}, u32[]{:S(2)}, u32[]{:S(2)}) collective-permute-start(bf16[2,128,1024]{2,1,0:T(8,128)(2,1)} %get-tuple-element.180), channel_id=1, source_target_pairs={{0,1},{1,2},{2,3},{3,0},{4,5},{5,6},{6,7},{7,4},{8,9},{9,10},{10,1... | collective-permute-start | bytes 1572872 | tf_op jit(solution)/shard_map/ppermute | solution.py:605
  405.6 37.5 %collective-permute-start.39 = (bf16[2,128,1024]{2,1,0:T(8,128)(2,1)}, bf16[2,128,1024]{2,1,0:T(8,128)(2,1)}, u32[]{:S(2)}, u32[]{:S(2)}) collective-permute-start(bf16[2,128,1024]{2,1,0:T(8,128)(2,1)} %get-tuple-element.181), channel_id=1, source_target_pairs={{0,2},{1,3},{2,0},{3,1},{4,6},{5,7},{6,4},{7,5},{8,10},{9,11},{10,... | collective-permute-start | bytes 1572872 | tf_op jit(solution)/shard_map/ppermute | solution.py:605
  408.9 34.2 %collective-permute-start.40 = (bf16[2,128,1024]{2,1,0:T(8,128)(2,1)}, bf16[2,128,1024]{2,1,0:T(8,128)(2,1)}, u32[]{:S(2)}, u32[]{:S(2)}) collective-permute-start(bf16[2,128,1024]{2,1,0:T(8,128)(2,1)} %get-tuple-element.182), channel_id=1, source_target_pairs={{0,3},{1,0},{2,1},{3,2},{4,7},{5,4},{6,5},{7,6},{8,11},{9,8},{10,9... | collective-permute-start | bytes 1572872 | tf_op jit(solution)/shard_map/ppermute | solution.py:605
  419.3 27.1 %collective-permute-start.46 = (bf16[384,256]{1,0:T(8,128)(2,1)}, bf16[384,256]{1,0:T(8,128)(2,1)S(1)}, u32[]{:S(2)}, u32[]{:S(2)}) collective-permute-start(bf16[384,256]{1,0:T(8,128)(2,1)} %join_z.1.refs_1_), channel_id=1, source_target_pairs={{0,8},{4,12},{8,16},{12,20},{16,24},{20,28},{24,0},{28,4},{32,40},... | collective-permute-start | bytes 589832 | tf_op jit(solution)/shard_map/ppermute | solution.py:640
  419.7 26.7 %collective-permute-start.45 = (bf16[384,256]{1,0:T(8,128)(2,1)}, bf16[384,256]{1,0:T(8,128)(2,1)S(1)}, u32[]{:S(2)}, u32[]{:S(2)}) collective-permute-start(bf16[384,256]{1,0:T(8,128)(2,1)} %join_z.1.refs_1_), channel_id=1, source_target_pairs={{0,16},{4,20},{8,24},{12,28},{16,0},{20,4},{24,8},{28,12},{32,48},... | collective-permute-start | bytes 589832 | tf_op jit(solution)/shard_map/ppermute | solution.py:640
  422.4 24.1 %collective-permute-start.44 = (bf16[384,256]{1,0:T(8,128)(2,1)}, bf16[384,256]{1,0:T(8,128)(2,1)}, u32[]{:S(2)}, u32[]{:S(2)}) collective-permute-start(bf16[384,256]{1,0:T(8,128)(2,1)} %join_z.1.refs_1_), channel_id=1, source_target_pairs={{0,24},{4,28},{8,0},{12,4},{16,8},{20,12},{24,16},{28,20},{32,56},... | collective-permute-start | bytes 589832 | tf_op jit(solution)/shard_map/ppermute | solution.py:640
  (73 other events, 410.9 us)
Sparse Core Ops, SparseCore 0:
  37.8 106.3 all-gather.4
  210.9 141.8 reduce-scatter.2
  355.3 44.0 reduce-scatter.4
  401.1 47.3 all-gather.6

commit v4 on v3

--- a/solution.py
+++ b/solution.py
@@ -59,10 +59,9 @@
     "attend_back": 11.0,
     "weight_sums": 2.0,
     "split_y": 2.8,
-    "split_z": 2.0,
-    "split_x": 1.6,
+    "sum_y": 2.0,
+    "split_x": 2.4,
     "join_x": 1.5,
-    "join_z": 1.6,
     "join_y": 2.2,
     "block": 4.5,
     "place": 2.8,
@@ -418,7 +417,6 @@
     x, first_length = x_of(place), lengths[m, 0, 0]
     if last:
         prev_w, prev_o, gain0, gain1, *refs = refs
-        before, refs = refs[:4], refs[4:]
     o0, o1, o2, o3, given_ref, *refs = refs
     deal = given_by_dealt(order, m, x)
     branch = stack((g0, g1, g2, g3))
@@ -454,11 +452,7 @@
     part = dot(grad_qkv, w[...], 1, 1).astype(BF)
     part = dot(deal, part).astype(BF)
     for k, out in enumerate((o0, o1, o2, o3)):
-        if last:
-            out[0] = before[k][...]
-            out[1] = part[k * TOK : (k + 1) * TOK]
-        else:
-            out[...] = part[k * TOK : (k + 1) * TOK]
+        out[...] = part[k * TOK : (k + 1) * TOK]
     if not last:
         sum_w_ref, sum_o_ref = refs
         sum_w_ref[...] = sum_w
@@ -482,16 +476,17 @@
             ref[6 * 256 + j * 16 : 6 * 256 + (j + 1) * 16, :] = tile.astype(ref.dtype)
 
 
-def tokens_body(micro, tokens, gains, p0, p1, p2, p3, *refs):
+def tokens_body(micro, tokens, gains, *refs):
     for m in range(micro):
-        upstream = (p0[m].astype(F32) + p1[m].astype(F32)) + (
-            p2[m].astype(F32) + p3[m].astype(F32)
+        p0, p1, p2, p3, given = refs[5 * m : 5 * m + 5]
+        upstream = (p0[...].astype(F32) + p1[...].astype(F32)) + (
+            p2[...].astype(F32) + p3[...].astype(F32)
         )
         v = tokens[m].astype(F32)
         r = lax.rsqrt(jnp.mean(v * v, axis=-1, keepdims=True) + EPS)
         scaled = upstream * gains[0:1, :]
         grad = r * scaled - v * (r * r * r) * jnp.mean(scaled * v, axis=-1, keepdims=True)
-        refs[-1][m] = (refs[m][...].astype(F32) + grad).astype(BF)
+        refs[-1][m] = (given[...].astype(F32) + grad).astype(BF)
 
 
 def weight_sums_body(sums, *outs):
@@ -516,31 +511,29 @@
             ref[b * 64 : (b + 1) * 64, :] = (keep[at, :] + got[at, :].astype(F32)).astype(ref.dtype)
 
 
-def split_z_body(place, own, r1, r2, r3, own_ref, s1, s2, s3):
-    z = z_of(place)
-    for b in range(BLOCKS):
-        for k, ref in enumerate((own_ref, s1, s2, s3)):
-            at = pl.ds(pl.multiple_of(b * 64 + ((z + k) & 3) * 16, 16), 16)
-            total = (own[at, :] + r1[at, :].astype(F32)) + (
-                r2[at, :].astype(F32) + r3[at, :].astype(F32)
-            )
-            ref[b * 16 : (b + 1) * 16, :] = total.astype(ref.dtype)
-
-
-def split_x_body(place, own, r1, r2, r3, o_ref, own_ref, s1, s2, s3):
-    x = x_of(place)
+def sum_y_body(own, r1, r2, r3, out_ref):
+    total = (own[...] + r1[...].astype(F32)) + (r2[...].astype(F32) + r3[...].astype(F32))
+    out_ref[...] = total.astype(BF)
+
+
+def split_x_body(place, own, r1, r2, r3, o_ref, own_ref, s1, s2, s3, held):
+    x, z = x_of(place), z_of(place)
+    for k, ref in enumerate((own, r1, r2, r3)):
+        held[pl.ds((z - k) & 3, 1)] = ref[...][None]
 
     def total(at):
-        return (own[at, :] + r1[at, :].astype(F32)) + (r2[at, :].astype(F32) + r3[at, :].astype(F32))
-
-    gain = total(slice(96, 112))
+        return (held[0, at, :].astype(F32) + held[1, at, :].astype(F32)) + (
+            held[2, at, :].astype(F32) + held[3, at, :].astype(F32)
+        )
+
+    gain = total(slice(384, 400))
     row = iota((16, 256), 0)
     for k, ref in enumerate((own_ref, s1, s2, s3)):
         s = (x + k) & 3
-        ref[0:16, :] = total(pl.ds(pl.multiple_of(s * 16, 16), 16)).astype(ref.dtype)
+        ref[0:64, :] = total(pl.ds(pl.multiple_of(s * 64, 64), 64)).astype(BF)
         mine = jnp.sum(jnp.where(row == s, gain, 0.0), axis=0, keepdims=True)
-        ref[16:32, :] = jnp.broadcast_to(mine, (16, 256)).astype(ref.dtype)
-    o_ref[...] = total(slice(64, 96)).astype(BF)
+        ref[64:80, :] = jnp.broadcast_to(mine, (16, 256)).astype(BF)
+    o_ref[...] = total(slice(256, 384)).astype(BF)
 
 
 def join_x_body(place, o, own, r1, r2, r3, out_ref, gain_ref):
@@ -548,17 +541,16 @@
     gain = jnp.zeros((16, 256), F32)
     for k, ref in enumerate((own, r1, r2, r3)):
         s = (x - k) & 3
-        out_ref[pl.ds(pl.multiple_of(s * 16, 16), 16), :] = ref[0:16, :].astype(BF)
-        gain += ref[16:32, :].astype(F32)
-    out_ref[64:96, :] = o[...]
+        out_ref[pl.ds(pl.multiple_of(s * 64, 64), 64), :] = ref[0:64, :]
+        gain += ref[64:80, :].astype(F32)
+    out_ref[256:384, :] = o[...]
     gain_ref[...] = gain[0:1]
 
 
-def join_body(index_of, place, own, r1, r2, r3, out_ref):
-    at = index_of(place)
+def join_y_body(place, own, r1, r2, r3, out_ref):
     rows = own.shape[0]
     for k, ref in enumerate((own, r1, r2, r3)):
-        s = (at + k) & 3
+        s = (y_of(place) + k) & 3
         out_ref[pl.ds(pl.multiple_of(s * rows, rows), rows), :] = ref[...]
 
 
@@ -569,7 +561,7 @@
 
     def piece(ref, b):
         return jnp.concatenate(
-            [ref[j * 96 + b * 16 : j * 96 + (b + 1) * 16, :] for j in range(16)], axis=0
+            [ref[j * 384 + b * 64 : j * 384 + (b + 1) * 64, :] for j in range(4)], axis=0
         ).astype(F32)
 
     for b in range(6):
@@ -729,7 +721,7 @@
     for m in range(micro):
         first = m == 0
         if not first:
-            token_rows = gather_x(hold([token_copies[m - 1]], left[-1][1])[0])
+            token_rows = later_rows
             weight_blocks = gather_ring(hold([weights], *token_rows[1:])[0])
         outs = [shape((TOK, D), BF)] * 5 + [
             shape((GT, D), BF),
@@ -751,13 +743,15 @@
             w_qkv, gains = result[9:]
         attended.append(result[:9])
         parts = scatter_x(result[:4])
+        if first:
+            later_rows = gather_x(hold([token_copies[m]], parts[1])[0])
         left.append(
             run(
                 "leave",
                 leave_body,
                 [shape((TOK, D), F32), shape((SLOTS, D), BF)],
                 [*parts, result[4], gains, routed[m][1]],
-                after=[weights] if first else weight_blocks[1:3],
+                after=[weights, *later_rows[1:]] if first else weight_blocks[1:3],
             )
         )
         reached.append(exchange(left[m][1]))
@@ -784,7 +778,7 @@
         sums = result[2]
 
     sum_w = sum_o = None
-    gain_sums, givens = [], []
+    gain_sums, grad_parts = [], []
     for m in range(micro):
         last = m == micro - 1
         branch, gain_sum = run(
@@ -792,7 +786,7 @@
             functools.partial(returned_body, m),
             [shape((TOK, D), BF), shape((8, D), F32)],
             [backs[m], routed[m][0], left[m][0], gains, dealt_cot],
-            after=() if m == 0 else (sum_w,),
+            after=() if m == 0 else (sum_w, *grad_parts[1:4]),
         )
         branch_rows = gather_x(branch)
         if last:
@@ -812,8 +806,7 @@
         out_shapes = [shape((TOK, D), BF)] * 5
         scratch = []
         if last:
-            ins += [sum_w, sum_o, *gain_sums, *parts]
-            out_shapes = [shape((micro, TOK, D), BF)] * 4 + out_shapes[4:]
+            ins += [sum_w, sum_o, *gain_sums]
             out_shapes += [shape((BLOCKS * 256, 256), F32), shape((BLOCKS * 256, 256), BF)]
             scratch = [pltpu.VMEM((D, COLS), F32), pltpu.VMEM((ROWS_HERE, D), F32)]
         else:
@@ -827,8 +820,10 @@
             scratch=scratch,
         )
         sum_w, sum_o = result[5:7]
-        parts = result[:4]
-        givens.append(result[4])
+        if last:
+            last_parts = result[:5]
+        else:
+            grad_parts += [*scatter_x(result[:4]), result[4]]
 
     four = [0, 1, 2, 3]
     rows = BLOCKS * 64
@@ -840,23 +835,17 @@
         smem=(0,),
     )
     pieces = [split_y[0]] + [along(split_y[k], lambda z, y, c, k=k: (z, y + k, c)) for k in four[1:]]
-    rows = BLOCKS * 16
-    split_z, *pieces = run(
-        "split_z",
-        split_z_body,
-        [shape((rows, 256), F32)] + [shape((rows, 256), BF)] * 3,
-        [place, *pieces],
-        smem=(0,),
-    )
-    pieces = [split_z] + [
-        along(pieces[k - 1], lambda z, y, c, k=k: (z + k, y, c)) for k in four[1:]
-    ]
+    last_parts = [*scatter_x(last_parts[:4]), last_parts[4]]
+    sum_y = run(
+        "sum_y", sum_y_body, [shape((rows, 256), BF)], pieces, after=last_parts[1:4]
+    )[0]
+    pieces = [sum_y] + [along(sum_y, lambda z, y, c, k=k: (z + k, y, c)) for k in four[1:]]
     blocks = run(
         "block",
         functools.partial(block_body, micro),
         [shape((micro, TOK, D), BF)],
         [*mixtures, routed[-1][0], *[left[m][0] for m in range(micro)]],
-        after=[split_z],
+        after=[sum_y],
     )[0]
     block_out = run(
         "place",
@@ -868,39 +857,35 @@
     o_piece, *pieces = run(
         "split_x",
         split_x_body,
-        [shape((32, 256), BF), shape((32, 256), F32)] + [shape((32, 256), BF)] * 3,
+        [shape((128, 256), BF)] + [shape((80, 256), BF)] * 4,
         [place, *pieces],
         smem=(0,),
+        scratch=[pltpu.VMEM((4, rows, 256), BF)],
         after=[blocks],
     )
+    x_pieces = scatter_x(pieces)
     piece, gain_ffn_sum = run(
         "join_x",
         join_x_body,
-        [shape((96, 256), BF), shape((1, 256), F32)],
-        [place, o_piece, *scatter_x(pieces)],
+        [shape((384, 256), BF), shape((1, 256), F32)],
+        [place, o_piece, *x_pieces],
         smem=(0,),
     )
     grad_tokens = run(
         "tokens",
         functools.partial(tokens_body, micro),
         [shape(tokens.shape, BF)],
-        [tokens, gains, *scatter_x(hold(parts, piece)), *givens],
+        [tokens, gains, *grad_parts, *last_parts],
     )[0]
-    for name, index_of, step in (
-        ("join_z", z_of, lambda z, y, c, k: (z - k, y, c)),
-        ("join_y", y_of, lambda z, y, c, k: (z, y - k, c)),
-    ):
-        pieces = [piece] + [
-            along(piece, lambda z, y, c, k=k, step=step: step(z, y, c, k)) for k in four[1:]
-        ]
-        piece = run(
-            name,
-            functools.partial(join_body, index_of),
-            [shape((4 * piece.shape[0], 256), BF)],
-            [place, *pieces],
-            smem=(0,),
-            after=[grad_tokens] if name == "join_y" else [],
-        )[0]
+    pieces = [piece] + [along(piece, lambda z, y, c, k=k: (z, y - k, c)) for k in four[1:]]
+    piece = run(
+        "join_y",
+        join_y_body,
+        [shape((1536, 256), BF)],
+        [place, *pieces],
+        smem=(0,),
+        after=[grad_tokens, totals[0]],
+    )[0]
     grad_query, grad_key, grad_value, grad_out, grad_gain = run(
         "weights",
         weights_body,
@@ -921,6 +906,7 @@
             gain_attn.astype(F32).reshape(-1, 1),
         ],
         smem=(0,),
+        after=[block_out],
     )
 
     return (

time: 484 us -> 454 us (0.938)
  waiting for transfers between devices: 180 us -> 157 us
    all_to_all x5, waiting for transfers between devices: 32 us -> 18.1 us  [exchange(): return lax.all_to_all(v, 'expert', split_axis=0, concat_axis=0, tiled=True)]
    ppermute x14 -> x11, starting transfers between devices: 25 us -> 17.6 us  [along(): return lax.ppermute(v, 'expert', pairs)]
    ppermute x14 -> x11, waiting for transfers between devices: 19.1 us -> 13.6 us  [along(): return lax.ppermute(v, 'expert', pairs)]
    ppermute x12 -> x15, starting transfers between devices: 15.5 us -> 19.8 us  [to_right(): lax.ppermute(v, 'shard', [(i, (i + k) % SHARDS) for i in range(SHARDS)])]
    ppermute x12 -> x15, waiting for transfers between devices: 50.9 us -> 48.1 us  [to_right(): lax.ppermute(v, 'shard', [(i, (i + k) % SHARDS) for i in range(SHARDS)])]
    unnamed x96 -> x88, local copies, waits for them, and re-layouts: 12.2 us -> 10 us
    pallas_call x23 -> x22, Pallas kernels: 90.7 us -> 88.8 us  [run(): pl.pallas_call(whole, out_shape=outs, in_specs=[SMEM if i in smem else VM...]
  transfers between devices with their start and end apart: 57 -> 57, of which waited for: 31 -> 33; matrix products, arithmetic and copies ran while one was open for 1% -> 1% of each run, Pallas kernels for 30% -> 32%
where the time goes in v4:
time: 454 us; the launch traced here: 445 us
  waiting for transfers between devices  157 us (35%)
  Pallas kernels  148 us (33%)
  starting transfers between devices  112 us (25%)
  between operations  14.6 us (3%)
  local copies, waits for them, and re-layouts  12.4 us (3%)
    pallas_call x22, Pallas kernels, run(): pl.pallas_call(whole, out_shape=outs, in_specs=[SMEM if i in smem else VM...  88.8 us
    ppermute x22, waiting for transfers between devices, from_right(): lax.ppermute(v, 'shard', [(i, (i - k) % SHARDS) for i in range(SHARDS)])  75 us
    pallas_call x2, Pallas kernels, expert_call(): pl.pallas_call(functools.partial(expert_body, m, last, len(after)), grid=...  58.9 us
    ppermute x15, waiting for transfers between devices, to_right(): lax.ppermute(v, 'shard', [(i, (i + k) % SHARDS) for i in range(SHARDS)])  48.1 us
    all_to_all x5, starting transfers between devices, exchange(): return lax.all_to_all(v, 'expert', split_axis=0, concat_axis=0, tiled=True)  41.5 us
    ppermute x22, starting transfers between devices, from_right(): lax.ppermute(v, 'shard', [(i, (i - k) % SHARDS) for i in range(SHARDS)])  33.3 us
    ppermute x15, starting transfers between devices, to_right(): lax.ppermute(v, 'shard', [(i, (i + k) % SHARDS) for i in range(SHARDS)])  19.8 us
    all_to_all x5, waiting for transfers between devices, exchange(): return lax.all_to_all(v, 'expert', split_axis=0, concat_axis=0, tiled=True)  18.1 us
  transfers between devices with their start and end apart: 57, of which 33 were waited for; matrix products, arithmetic and copies ran while one was open for 1% of the time, Pallas kernels for 32%

profile of v4, /device:TPU:1, one launch (start us, length us, event | category | flops | bytes accessed | tf_op | source)
XLA Modules:
  0.0 445.0 jit_solution(9910588799003149262)
XLA Ops:
  22.3 11.8 %collective-permute-done.refs_5_ = bf16[2,128,1024]{2,1,0:T(8,128)(2,1)} collective-permute-done((bf16[2,128,1024]{2,1,0:T(8,128)(2,1)}, bf16[2,128,1024]{2,1,0:T(8,128)(2,1)}, u32[]{:S(2)}, u32[]{:S(2)}) %collective-permute-start) | collective-permute-done | bytes 524320 | tf_op jit(solution)/shard_map/ppermute | solution.py:593
  48.1 17.3 %collective-permute-done.4.refs_5_ = bf16[128,1024]{1,0:T(8,128)(2,1)S(1)} collective-permute-done((bf16[128,1024]{1,0:T(8,128)(2,1)}, bf16[128,1024]{1,0:T(8,128)(2,1)S(1)}, u32[]{:S(2)}, u32[]{:S(2)}) %collective-permute-start.4) | collective-permute-done | bytes 262176 | tf_op jit(solution)/shard_map/ppermute | solution.py:593
  66.9 7.4 %attend.2 = (bf16[128,1024]{1,0:T(8,128)(2,1)}, bf16[128,1024]{1,0:T(8,128)(2,1)}, bf16[128,1024]{1,0:T(8,128)(2,1)}, bf16[128,1024]{1,0:T(8,128)(2,1)}, bf16[12...) custom-call(s32[1]{0:T(128)} %bitcast.refs_0_.refs_1_, ...), custom_call_target="tpu_custom_call" | custom-call | flops 1 | bytes 26280000 | tf_op jit(solution)/shard_map/attend/pallas_call | solution.py:86
  78.0 4.0 collective-permute-done.9.refs_1_
  82.7 3.9 collective-permute-start.11
  91.1 5.8 %collective-permute-done.12.refs_6_.refs_3_.refs_10_ = bf16[128,1024]{1,0:T(8,128)(2,1)S(1)} collective-permute-done((bf16[128,1024]{1,0:T(8,128)(2,1)}, bf16[128,1024]{1,0:T(8,128)(2,1)S(1)}, u32[]{:S(2)}, u32[]{:S(2)}) %collective-permute-start.12) | collective-permute-done | bytes 262176 | tf_op jit(solution)/shard_map/ppermute | solution.py:593
  96.9 4.4 collective-permute-done.11.refs_5_.refs_2_.refs_9_
  102.1 4.3 leave.3
  106.4 9.7 %all-to-all-start = ((bf16[32,48,1024]{2,1,0:T(8,128)(2,1)}), bf16[32,48,1024]{2,1,0:T(8,128)(2,1)}, u32[]{:S(2)}, u32[]{:S(2)}) async-start(bf16[32,48,1024]{2,1,0:T(8,128)(2,1)} %bitcast.29), calls=%async_computation | async-start | bytes 6291456 | tf_op jit(solution)/shard_map/all_to_all | solution.py:644
  118.8 7.0 %attend.3 = (bf16[128,1024]{1,0:T(8,128)(2,1)}, bf16[128,1024]{1,0:T(8,128)(2,1)}, bf16[128,1024]{1,0:T(8,128)(2,1)}, bf16[128,1024]{1,0:T(8,128)(2,1)}, bf16[12...) custom-call(s32[1]{0:T(128)} %bitcast.refs_0_.refs_1_, ...), custom_call_target="tpu_custom_call" | custom-call | flops 1 | bytes 26280000 | tf_op jit(solution)/shard_map/attend/pallas_call | solution.py:86
  128.6 13.6 %collective-permute-done.13.refs_1_ = bf16[128,1024]{1,0:T(8,128)(2,1)S(1)} collective-permute-done((bf16[128,1024]{1,0:T(8,128)(2,1)}, bf16[128,1024]{1,0:T(8,128)(2,1)S(1)}, u32[]{:S(2)}, u32[]{:S(2)}) %collective-permute-start.13) | collective-permute-done | bytes 262176 | tf_op jit(solution)/shard_map/ppermute | solution.py:597
  142.1 6.1 %collective-permute-done.14.refs_2_ = bf16[128,1024]{1,0:T(8,128)(2,1)S(1)} collective-permute-done((bf16[128,1024]{1,0:T(8,128)(2,1)}, bf16[128,1024]{1,0:T(8,128)(2,1)S(1)}, u32[]{:S(2)}, u32[]{:S(2)}) %collective-permute-start.14) | collective-permute-done | bytes 262176 | tf_op jit(solution)/shard_map/ppermute | solution.py:597
  149.2 4.3 leave.2
  155.3 7.4 %all-to-all-start.1 = ((bf16[32,48,1024]{2,1,0:T(8,128)(2,1)}), bf16[32,48,1024]{2,1,0:T(8,128)(2,1)}, u32[]{:S(2)}, u32[]{:S(2)}) async-start(bf16[32,48,1024]{2,1,0:T(8,128)(2,1)} %bitcast.27), calls=%async_computation.1 | async-start | bytes 6291456 | tf_op jit(solution)/shard_map/all_to_all | solution.py:644
  167.0 7.4 %collective-permute-done.21.refs_9_.refs_8_ = bf16[1,3,512,128]{3,2,1,0:T(8,128)(2,1)S(1)} collective-permute-done((bf16[1,3,512,128]{3,2,1,0:T(8,128)(2,1)S(1)}, bf16[1,3,512,128]{3,2,1,0:T(8,128)(2,1)S(1)}, u32[]{:S(2)}, u32[]{:S(2)}) %collective-permute-start.21) | collective-permute-done | bytes 393248 | tf_op jit(solution)/shard_map/ppermute | solution.py:593
  175.5 30.0 %expert.2 = (bf16[32,128,1024]{2,1,0:T(8,128)(2,1)}, bf16[1536,1024]{1,0:T(8,128)(2,1)}, f32[3,1024,512]{2,1,0:T(8,128)}) custom-call(bf16[1536,1024]{1,0:T(8,128)(2,1)} %get-tuple-element.116.refs_0_, s32[1]{0:T(128)} %bitcast.refs_0_.refs_1_, s32[1,32]{1,0:T(1,128)} %bitcast.36, bf16[1536,1024]{1,0:T(8,128)(2,1)} %bitcast.5.refs_3_, ...), custom_call_target="tpu_custom_call" | custom-call | flops 1 | bytes 97200000 | tf_op jit(solution)/shard_map/expert/pallas_call | solution.py:377
  205.5 8.8 %all-to-all-start.2 = ((bf16[32,48,1024]{2,1,0:T(8,128)(2,1)}), bf16[32,48,1024]{2,1,0:T(8,128)(2,1)}, u32[]{:S(2)}, u32[]{:S(2)}) async-start(bf16[32,48,1024]{2,1,0:T(8,128)(2,1)} %bitcast.10), calls=%async_computation.3 | async-start | bytes 6291456 | tf_op jit(solution)/shard_map/all_to_all | solution.py:644
  214.3 29.0 %expert.3 = (bf16[1536,1024]{1,0:T(8,128)(2,1)}, bf16[1536,1024]{1,0:T(8,128)(2,1)}, bf16[4,3,1024,128]{3,2,1,0:T(8,128)(2,1)}) custom-call(s32[1]{0:T(128)} %bitcast.refs_0_.refs_1_, s32[1,32]{1,0:T(1,128)} %bitcast.37, bf16[1536,1024]{1,0:T(8,128)(2,1)} %bitcast.8.refs_2_, bf16[32,2,144,1024]{3,2,1,0:T(8,128)(2,1)} %bitcast.23, ...), custom_call_target="tpu_custom_call" | custom-call | flops 1 | bytes 97200000 | tf_op jit(solution)/shard_map/expert/pallas_call | solution.py:377
  243.3 10.2 %all-to-all-done.2 = bf16[32,48,1024]{2,1,0:T(8,128)(2,1)} async-done(((bf16[32,48,1024]{2,1,0:T(8,128)(2,1)}), bf16[32,48,1024]{2,1,0:T(8,128)(2,1)}, u32[]{:S(2)}, u32[]{:S(2)}) %all-to-all-start.2) | async-done | bytes 3145760 | tf_op jit(solution)/shard_map/all_to_all | solution.py:644
  253.5 7.4 %all-to-all-start.3 = ((bf16[32,48,1024]{2,1,0:T(8,128)(2,1)}), bf16[32,48,1024]{2,1,0:T(8,128)(2,1)}, u32[]{:S(2)}, u32[]{:S(2)}) async-start(bf16[32,48,1024]{2,1,0:T(8,128)(2,1)} %bitcast.26), calls=%async_computation.4 | async-start | bytes 6291456 | tf_op jit(solution)/shard_map/all_to_all | solution.py:644
  269.5 5.3 %collective-permute-done.24.refs_6_ = bf16[128,1024]{1,0:T(8,128)(2,1)S(1)} collective-permute-done((bf16[128,1024]{1,0:T(8,128)(2,1)}, bf16[128,1024]{1,0:T(8,128)(2,1)S(1)}, u32[]{:S(2)}, u32[]{:S(2)}) %collective-permute-start.24) | collective-permute-done | bytes 262176 | tf_op jit(solution)/shard_map/ppermute | solution.py:593
  274.9 6.5 %collective-permute-done.23.refs_5_ = bf16[128,1024]{1,0:T(8,128)(2,1)S(1)} collective-permute-done((bf16[128,1024]{1,0:T(8,128)(2,1)}, bf16[128,1024]{1,0:T(8,128)(2,1)S(1)}, u32[]{:S(2)}, u32[]{:S(2)}) %collective-permute-start.23) | collective-permute-done | bytes 262176 | tf_op jit(solution)/shard_map/ppermute | solution.py:593
  282.1 9.3 %attend_back.2 = (bf16[128,1024]{1,0:T(8,128)(2,1)}, bf16[128,1024]{1,0:T(8,128)(2,1)}, bf16[128,1024]{1,0:T(8,128)(2,1)}, bf16[128,1024]{1,0:T(8,128)(2,1)}, bf...) custom-call(s32[1]{0:T(128)} %bitcast.refs_0_.refs_1_, s32[2,1,2]{2,1,0:T(1,128)} %refs_1_.14, ...), custom_call_target="tpu_custom_call" | custom-call | flops 1 | bytes 39600000 | tf_op jit(solution)/shard_map/attend_back/pallas_call | solution.py:86
  295.2 4.5 %collective-permute-done.25.refs_6_.refs_3_ = bf16[128,1024]{1,0:T(8,128)(2,1)S(1)} collective-permute-done((bf16[128,1024]{1,0:T(8,128)(2,1)}, bf16[128,1024]{1,0:T(8,128)(2,1)S(1)}, u32[]{:S(2)}, u32[]{:S(2)}) %collective-permute-start.25) | collective-permute-done | bytes 262176 | tf_op jit(solution)/shard_map/ppermute | solution.py:597
  299.7 7.4 %collective-permute-done.26.refs_7_.refs_4_ = bf16[128,1024]{1,0:T(8,128)(2,1)S(1)} collective-permute-done((bf16[128,1024]{1,0:T(8,128)(2,1)}, bf16[128,1024]{1,0:T(8,128)(2,1)S(1)}, u32[]{:S(2)}, u32[]{:S(2)}) %collective-permute-start.26) | collective-permute-done | bytes 262176 | tf_op jit(solution)/shard_map/ppermute | solution.py:597
  307.1 6.1 %all-to-all-done.3 = bf16[32,48,1024]{2,1,0:T(8,128)(2,1)} async-done(((bf16[32,48,1024]{2,1,0:T(8,128)(2,1)}), bf16[32,48,1024]{2,1,0:T(8,128)(2,1)}, u32[]{:S(2)}, u32[]{:S(2)}) %all-to-all-start.3) | async-done | bytes 3145760 | tf_op jit(solution)/shard_map/all_to_all | solution.py:644
  317.0 8.3 %all-to-all-start.4 = ((bf16[32,48,1024]{2,1,0:T(8,128)(2,1)}), bf16[32,48,1024]{2,1,0:T(8,128)(2,1)}, u32[]{:S(2)}, u32[]{:S(2)}) async-start(bf16[32,48,1024]{2,1,0:T(8,128)(2,1)} %bitcast.25), calls=%async_computation.5 | async-start | bytes 6291456 | tf_op jit(solution)/shard_map/all_to_all | solution.py:644
  330.3 3.9 collective-permute-done.30.refs_6_
  334.2 6.6 %collective-permute-done.29.refs_5_ = bf16[128,1024]{1,0:T(8,128)(2,1)S(1)} collective-permute-done((bf16[128,1024]{1,0:T(8,128)(2,1)S(1)}, bf16[128,1024]{1,0:T(8,128)(2,1)S(1)}, u32[]{:S(2)}, u32[]{:S(2)}) %collective-permute-start.29) | collective-permute-done | bytes 262176 | tf_op jit(solution)/shard_map/ppermute | solution.py:593
  341.6 11.3 %attend_back.3 = (bf16[128,1024]{1,0:T(8,128)(2,1)}, bf16[128,1024]{1,0:T(8,128)(2,1)}, bf16[128,1024]{1,0:T(8,128)(2,1)}, bf16[128,1024]{1,0:T(8,128)(2,1)}, bf...) custom-call(s32[1]{0:T(128)} %bitcast.refs_0_.refs_1_, s32[2,1,2]{2,1,0:T(1,128)} %refs_1_.14, ...), custom_call_target="tpu_custom_call" | custom-call | flops 1 | bytes 39600000 | tf_op jit(solution)/shard_map/attend_back/pallas_call | solution.py:86
  366.2 5.3 %collective-permute-done.36.refs_5_.refs_9_ = bf16[128,1024]{1,0:T(8,128)(2,1)S(1)} collective-permute-done((bf16[128,1024]{1,0:T(8,128)(2,1)}, bf16[128,1024]{1,0:T(8,128)(2,1)S(1)}, u32[]{:S(2)}, u32[]{:S(2)}) %collective-permute-start.36) | collective-permute-done | bytes 262176 | tf_op jit(solution)/shard_map/ppermute | solution.py:597
  390.6 7.1 %collective-permute-done.38.refs_2_ = bf16[448,256]{1,0:T(8,128)(2,1)S(1)} collective-permute-done((bf16[448,256]{1,0:T(8,128)(2,1)S(1)}, bf16[448,256]{1,0:T(8,128)(2,1)S(1)}, u32[]{:S(2)}, u32[]{:S(2)}) %collective-permute-start.38) | collective-permute-done | bytes 229408 | tf_op jit(solution)/shard_map/ppermute | solution.py:632
  (210 shorter events, 149.4 us)
Async XLA Ops:
  7.2 167.6 %all-gather.5.cloned.1.call-start = ((), (), s32[]{:S(2)}) async-start(), calls=%async_computation.9 | async-start | bytes 19464192 | tf_op jit(solution)/shard_map/all_gather | solution.py:720
  7.2 15.1 %collective-permute-start.1 = (bf16[2,128,1024]{2,1,0:T(8,128)(2,1)}, bf16[2,128,1024]{2,1,0:T(8,128)(2,1)S(1)}, u32[]{:S(2)}, u32[]{:S(2)}) collective-permute-start(bf16[2,128,1024]{2,1,0:T(8,128)(2,1)} %refs_4_.2), channel_id=1, source_target_pairs={{0,2},{1,3},{2,0},{3,1},{4,6},{5,7},{6,4},{7,5},{8,10},{9,11},{10,... | collective-permute-start | bytes 1572872 | tf_op jit(solution)/shard_map/ppermute | solution.py:593
  10.9 23.2 %collective-permute-start = (bf16[2,128,1024]{2,1,0:T(8,128)(2,1)}, bf16[2,128,1024]{2,1,0:T(8,128)(2,1)}, u32[]{:S(2)}, u32[]{:S(2)}) collective-permute-start(bf16[2,128,1024]{2,1,0:T(8,128)(2,1)} %refs_4_.2), channel_id=1, source_target_pairs={{0,3},{1,0},{2,1},{3,2},{4,7},{5,4},{6,5},{7,6},{8,11},{9,8},{10,9... | collective-permute-start | bytes 1572872 | tf_op jit(solution)/shard_map/ppermute | solution.py:593
  11.7 23.1 %collective-permute-start.2 = (bf16[2,128,1024]{2,1,0:T(8,128)(2,1)}, bf16[2,128,1024]{2,1,0:T(8,128)(2,1)}, u32[]{:S(2)}, u32[]{:S(2)}) collective-permute-start(bf16[2,128,1024]{2,1,0:T(8,128)(2,1)} %refs_4_.2), channel_id=1, source_target_pairs={{0,1},{1,2},{2,3},{3,0},{4,5},{5,6},{6,7},{7,4},{8,9},{9,10},{10,1... | collective-permute-start | bytes 1572872 | tf_op jit(solution)/shard_map/ppermute | solution.py:593
  39.2 26.2 %collective-permute-start.6 = (bf16[272,512]{1,0:T(8,128)(2,1)}, bf16[272,512]{1,0:T(8,128)(2,1)S(1)}, u32[]{:S(2)}, u32[]{:S(2)}) collective-permute-start(bf16[272,512]{1,0:T(8,128)(2,1)} %get-tuple-element.103), channel_id=1, source_target_pairs={{0,3},{1,0},{2,1},{3,2},{4,7},{5,4},{6,5},{7,6},{8,11},{9,8},{10,9... | collective-permute-start | bytes 835592 | tf_op jit(solution)/shard_map/ppermute | solution.py:593
  40.6 24.9 %collective-permute-start.7 = (bf16[272,512]{1,0:T(8,128)(2,1)}, bf16[272,512]{1,0:T(8,128)(2,1)S(1)}, u32[]{:S(2)}, u32[]{:S(2)}) collective-permute-start(bf16[272,512]{1,0:T(8,128)(2,1)} %get-tuple-element.104), channel_id=1, source_target_pairs={{0,2},{1,3},{2,0},{3,1},{4,6},{5,7},{6,4},{7,5},{8,10},{9,11},{10,... | collective-permute-start | bytes 835592 | tf_op jit(solution)/shard_map/ppermute | solution.py:593
  42.2 23.2 %collective-permute-start.8 = (bf16[272,512]{1,0:T(8,128)(2,1)}, bf16[272,512]{1,0:T(8,128)(2,1)S(1)}, u32[]{:S(2)}, u32[]{:S(2)}) collective-permute-start(bf16[272,512]{1,0:T(8,128)(2,1)} %get-tuple-element.105), channel_id=1, source_target_pairs={{0,1},{1,2},{2,3},{3,0},{4,5},{5,6},{6,7},{7,4},{8,9},{9,10},{10,1... | collective-permute-start | bytes 835592 | tf_op jit(solution)/shard_map/ppermute | solution.py:593
  42.5 22.9 %collective-permute-start.4 = (bf16[128,1024]{1,0:T(8,128)(2,1)}, bf16[128,1024]{1,0:T(8,128)(2,1)S(1)}, u32[]{:S(2)}, u32[]{:S(2)}) collective-permute-start(bf16[128,1024]{1,0:T(8,128)(2,1)} %get-tuple-element.101.refs_3_), channel_id=1, source_target_pairs={{0,2},{1,3},{2,0},{3,1},{4,6},{5,7},{6,4},{7,5},{8,10},{9,11},{10,... | collective-permute-start | bytes 786440 | tf_op jit(solution)/shard_map/ppermute | solution.py:593
  46.3 19.1 %collective-permute-start.3 = (bf16[128,1024]{1,0:T(8,128)(2,1)}, bf16[128,1024]{1,0:T(8,128)(2,1)S(1)}, u32[]{:S(2)}, u32[]{:S(2)}) collective-permute-start(bf16[128,1024]{1,0:T(8,128)(2,1)} %get-tuple-element.101.refs_3_), channel_id=1, source_target_pairs={{0,3},{1,0},{2,1},{3,2},{4,7},{5,4},{6,5},{7,6},{8,11},{9,8},{10,9... | collective-permute-start | bytes 786440 | tf_op jit(solution)/shard_map/ppermute | solution.py:593
  74.7 15.5 %collective-permute-start.18 = (bf16[128,1024]{1,0:T(8,128)(2,1)}, bf16[128,1024]{1,0:T(8,128)(2,1)}, u32[]{:S(2)}, u32[]{:S(2)}) collective-permute-start(bf16[128,1024]{1,0:T(8,128)(2,1)} %get-tuple-element.118), channel_id=1, source_target_pairs={{0,2},{1,3},{2,0},{3,1},{4,6},{5,7},{6,4},{7,5},{8,10},{9,11},{10,... | collective-permute-start | bytes 786440 | tf_op jit(solution)/shard_map/ppermute | solution.py:597
  78.0 13.1 %collective-permute-start.19 = (bf16[128,1024]{1,0:T(8,128)(2,1)}, bf16[128,1024]{1,0:T(8,128)(2,1)}, u32[]{:S(2)}, u32[]{:S(2)}) collective-permute-start(bf16[128,1024]{1,0:T(8,128)(2,1)} %get-tuple-element.119), channel_id=1, source_target_pairs={{0,3},{1,0},{2,1},{3,2},{4,7},{5,4},{6,5},{7,6},{8,11},{9,8},{10,9... | collective-permute-start | bytes 786440 | tf_op jit(solution)/shard_map/ppermute | solution.py:597
  82.7 14.2 %collective-permute-start.12 = (bf16[128,1024]{1,0:T(8,128)(2,1)}, bf16[128,1024]{1,0:T(8,128)(2,1)S(1)}, u32[]{:S(2)}, u32[]{:S(2)}) collective-permute-start(bf16[128,1024]{1,0:T(8,128)(2,1)} %hold.7.refs_3_), channel_id=1, source_target_pairs={{0,1},{1,2},{2,3},{3,0},{4,5},{5,6},{6,7},{7,4},{8,9},{9,10},{10,1... | collective-permute-start | bytes 786440 | tf_op jit(solution)/shard_map/ppermute | solution.py:593
  82.7 18.6 %collective-permute-start.11 = (bf16[128,1024]{1,0:T(8,128)(2,1)}, bf16[128,1024]{1,0:T(8,128)(2,1)S(1)}, u32[]{:S(2)}, u32[]{:S(2)}) collective-permute-start(bf16[128,1024]{1,0:T(8,128)(2,1)} %hold.7.refs_3_), channel_id=1, source_target_pairs={{0,2},{1,3},{2,0},{3,1},{4,6},{5,7},{6,4},{7,5},{8,10},{9,11},{10,... | collective-permute-start | bytes 786440 | tf_op jit(solution)/shard_map/ppermute | solution.py:593
  86.7 14.6 %collective-permute-start.10 = (bf16[128,1024]{1,0:T(8,128)(2,1)}, bf16[128,1024]{1,0:T(8,128)(2,1)S(1)}, u32[]{:S(2)}, u32[]{:S(2)}) collective-permute-start(bf16[128,1024]{1,0:T(8,128)(2,1)} %hold.7.refs_3_), channel_id=1, source_target_pairs={{0,3},{1,0},{2,1},{3,2},{4,7},{5,4},{6,5},{7,6},{8,11},{9,8},{10,9... | collective-permute-start | bytes 786440 | tf_op jit(solution)/shard_map/ppermute | solution.py:593
  106.4 48.9 %all-to-all-start = ((bf16[32,48,1024]{2,1,0:T(8,128)(2,1)}), bf16[32,48,1024]{2,1,0:T(8,128)(2,1)}, u32[]{:S(2)}, u32[]{:S(2)}) async-start(bf16[32,48,1024]{2,1,0:T(8,128)(2,1)} %bitcast.29), calls=%async_computation | async-start | bytes 6291456 | tf_op jit(solution)/shard_map/all_to_all | solution.py:644
  116.1 32.1 %collective-permute-start.17 = (bf16[2,3,512,128]{3,2,1,0:T(8,128)(2,1)}, bf16[2,3,512,128]{3,2,1,0:T(8,128)(2,1)S(1)}, u32[]{:S(2)}, u32[]{:S(2)}) collective-permute-start(bf16[2,3,512,128]{3,2,1,0:T(8,128)(2,1)} %hold.8.refs_5_.refs_4_), channel_id=1, source_target_pairs={{0,1},{1,2},{2,3},{3,0},{4,5},{5,6},{6,7},{7,4},{8,9},{9,10},{10,1... | collective-permute-start | bytes 2359304 | tf_op jit(solution)/shard_map/ppermute | solution.py:593
  116.2 32.1 %collective-permute-start.16 = (bf16[2,3,512,128]{3,2,1,0:T(8,128)(2,1)}, bf16[2,3,512,128]{3,2,1,0:T(8,128)(2,1)}, u32[]{:S(2)}, u32[]{:S(2)}) collective-permute-start(bf16[2,3,512,128]{3,2,1,0:T(8,128)(2,1)} %hold.8.refs_5_.refs_4_), channel_id=1, source_target_pairs={{0,3},{1,0},{2,1},{3,2},{4,7},{5,4},{6,5},{7,6},{8,11},{9,8},{10,9... | collective-permute-start | bytes 2359304 | tf_op jit(solution)/shard_map/ppermute | solution.py:593
  125.9 16.3 %collective-permute-start.13 = (bf16[128,1024]{1,0:T(8,128)(2,1)}, bf16[128,1024]{1,0:T(8,128)(2,1)S(1)}, u32[]{:S(2)}, u32[]{:S(2)}) collective-permute-start(bf16[128,1024]{1,0:T(8,128)(2,1)} %get-tuple-element.111), channel_id=1, source_target_pairs={{0,1},{1,2},{2,3},{3,0},{4,5},{5,6},{6,7},{7,4},{8,9},{9,10},{10,1... | collective-permute-start | bytes 786440 | tf_op jit(solution)/shard_map/ppermute | solution.py:597
  125.9 22.3 %collective-permute-start.14 = (bf16[128,1024]{1,0:T(8,128)(2,1)}, bf16[128,1024]{1,0:T(8,128)(2,1)S(1)}, u32[]{:S(2)}, u32[]{:S(2)}) collective-permute-start(bf16[128,1024]{1,0:T(8,128)(2,1)} %get-tuple-element.112), channel_id=1, source_target_pairs={{0,2},{1,3},{2,0},{3,1},{4,6},{5,7},{6,4},{7,5},{8,10},{9,11},{10,... | collective-permute-start | bytes 786440 | tf_op jit(solution)/shard_map/ppermute | solution.py:597
  127.8 20.4 %collective-permute-start.15 = (bf16[128,1024]{1,0:T(8,128)(2,1)}, bf16[128,1024]{1,0:T(8,128)(2,1)S(1)}, u32[]{:S(2)}, u32[]{:S(2)}) collective-permute-start(bf16[128,1024]{1,0:T(8,128)(2,1)} %get-tuple-element.113), channel_id=1, source_target_pairs={{0,3},{1,0},{2,1},{3,2},{4,7},{5,4},{6,5},{7,6},{8,11},{9,8},{10,9... | collective-permute-start | bytes 786440 | tf_op jit(solution)/shard_map/ppermute | solution.py:597
  155.3 50.2 %all-to-all-start.1 = ((bf16[32,48,1024]{2,1,0:T(8,128)(2,1)}), bf16[32,48,1024]{2,1,0:T(8,128)(2,1)}, u32[]{:S(2)}, u32[]{:S(2)}) async-start(bf16[32,48,1024]{2,1,0:T(8,128)(2,1)} %bitcast.27), calls=%async_computation.1 | async-start | bytes 6291456 | tf_op jit(solution)/shard_map/all_to_all | solution.py:644
  162.7 215.3 %reduce-scatter.3.cloned.1.call-start = ((), (), s32[]{:S(2)}) async-start(), calls=%async_computation.7 | async-start | bytes 8650752 | tf_op jit(solution)/shard_map/reduce_scatter | solution.py:640
  205.5 48.0 %all-to-all-start.2 = ((bf16[32,48,1024]{2,1,0:T(8,128)(2,1)}), bf16[32,48,1024]{2,1,0:T(8,128)(2,1)}, u32[]{:S(2)}, u32[]{:S(2)}) async-start(bf16[32,48,1024]{2,1,0:T(8,128)(2,1)} %bitcast.10), calls=%async_computation.3 | async-start | bytes 6291456 | tf_op jit(solution)/shard_map/all_to_all | solution.py:644
  214.3 201.2 %reduce-scatter.5.cloned.1.call-start = ((), (), s32[]{:S(2)}) async-start(), calls=%async_computation.8 | async-start | bytes 3932160 | tf_op jit(solution)/shard_map/reduce_scatter | solution.py:795
  253.5 59.7 %all-to-all-start.3 = ((bf16[32,48,1024]{2,1,0:T(8,128)(2,1)}), bf16[32,48,1024]{2,1,0:T(8,128)(2,1)}, u32[]{:S(2)}, u32[]{:S(2)}) async-start(bf16[32,48,1024]{2,1,0:T(8,128)(2,1)} %bitcast.26), calls=%async_computation.4 | async-start | bytes 6291456 | tf_op jit(solution)/shard_map/all_to_all | solution.py:644
  265.6 15.7 %collective-permute-start.23 = (bf16[128,1024]{1,0:T(8,128)(2,1)}, bf16[128,1024]{1,0:T(8,128)(2,1)S(1)}, u32[]{:S(2)}, u32[]{:S(2)}) collective-permute-start(bf16[128,1024]{1,0:T(8,128)(2,1)} %get-tuple-element.133.refs_3_), channel_id=1, source_target_pairs={{0,2},{1,3},{2,0},{3,1},{4,6},{5,7},{6,4},{7,5},{8,10},{9,11},{10,... | collective-permute-start | bytes 786440 | tf_op jit(solution)/shard_map/ppermute | solution.py:593
  292.7 14.3 %collective-permute-start.26 = (bf16[128,1024]{1,0:T(8,128)(2,1)}, bf16[128,1024]{1,0:T(8,128)(2,1)S(1)}, u32[]{:S(2)}, u32[]{:S(2)}) collective-permute-start(bf16[128,1024]{1,0:T(8,128)(2,1)} %get-tuple-element.140), channel_id=1, source_target_pairs={{0,2},{1,3},{2,0},{3,1},{4,6},{5,7},{6,4},{7,5},{8,10},{9,11},{10,... | collective-permute-start | bytes 786440 | tf_op jit(solution)/shard_map/ppermute | solution.py:597
  317.0 60.9 %all-to-all-start.4 = ((bf16[32,48,1024]{2,1,0:T(8,128)(2,1)}), bf16[32,48,1024]{2,1,0:T(8,128)(2,1)}, u32[]{:S(2)}, u32[]{:S(2)}) async-start(bf16[32,48,1024]{2,1,0:T(8,128)(2,1)} %bitcast.25), calls=%async_computation.5 | async-start | bytes 6291456 | tf_op jit(solution)/shard_map/all_to_all | solution.py:644
  325.3 105.1 %all-gather.7.cloned.1.call-start = ((), (), s32[]{:S(2)}) async-start(), calls=%async_computation.10 | async-start | bytes 2621440 | tf_op jit(solution)/shard_map/all_gather | solution.py:854
  326.4 14.4 %collective-permute-start.29 = (bf16[128,1024]{1,0:T(8,128)(2,1)S(1)}, bf16[128,1024]{1,0:T(8,128)(2,1)S(1)}, u32[]{:S(2)}, u32[]{:S(2)}) collective-permute-start(bf16[128,1024]{1,0:T(8,128)(2,1)S(1)} %copy-done.11), channel_id=1, source_target_pairs={{0,2},{1,3},{2,0},{3,1},{4,6},{5,7},{6,4},{7,5},{8,10},{9,11},{10,... | collective-permute-start | bytes 786440 | tf_op jit(solution)/shard_map/ppermute | solution.py:593
  355.2 16.3 %collective-permute-start.36 = (bf16[128,1024]{1,0:T(8,128)(2,1)}, bf16[128,1024]{1,0:T(8,128)(2,1)S(1)}, u32[]{:S(2)}, u32[]{:S(2)}) collective-permute-start(bf16[128,1024]{1,0:T(8,128)(2,1)} %get-tuple-element.157), channel_id=1, source_target_pairs={{0,2},{1,3},{2,0},{3,1},{4,6},{5,7},{6,4},{7,5},{8,10},{9,11},{10,... | collective-permute-start | bytes 786440 | tf_op jit(solution)/shard_map/ppermute | solution.py:597
  357.1 17.0 %collective-permute-start.37 = (bf16[128,1024]{1,0:T(8,128)(2,1)}, bf16[128,1024]{1,0:T(8,128)(2,1)}, u32[]{:S(2)}, u32[]{:S(2)}) collective-permute-start(bf16[128,1024]{1,0:T(8,128)(2,1)} %get-tuple-element.158), channel_id=1, source_target_pairs={{0,3},{1,0},{2,1},{3,2},{4,7},{5,4},{6,5},{7,6},{8,11},{9,8},{10,9... | collective-permute-start | bytes 786440 | tf_op jit(solution)/shard_map/ppermute | solution.py:597
  (69 other events, 393.8 us)
Sparse Core Ops, SparseCore 0:
  37.8 80.3 all-gather.4
  205.6 142.2 reduce-scatter.2
  350.4 46.0 reduce-scatter.4
  398.8 31.5 all-gather.6

commit v5 on v4

--- a/solution.py
+++ b/solution.py
@@ -64,9 +64,8 @@
     "join_x": 1.5,
     "join_y": 2.2,
     "block": 4.5,
-    "place": 2.8,
     "tokens": 3.4,
-    "weights": 3.9,
+    "finish": 5.5,
 }
 
 
@@ -589,6 +588,11 @@
     gain_ref[...] = jnp.broadcast_to(total, (ROWS_HERE, 128)).T[0:1]
 
 
+def finish_body(micro, place, order, block_rows, own, got, wq, wk, wv, gain, block_ref, *outs):
+    weights_body(place, own, got, wq, wk, wv, gain, *outs)
+    place_body(micro, place, order, block_rows, block_ref)
+
+
 def from_right(v, k):
     return lax.ppermute(v, "shard", [(i, (i - k) % SHARDS) for i in range(SHARDS)])
 
@@ -847,13 +851,7 @@
         [*mixtures, routed[-1][0], *[left[m][0] for m in range(micro)]],
         after=[sum_y],
     )[0]
-    block_out = run(
-        "place",
-        functools.partial(place_body, micro),
-        [shape(tokens.shape, BF)],
-        [place, order, lax.all_gather(blocks, "shard", axis=0)],
-        smem=(0,),
-    )[0]
+    block_rows = lax.all_gather(blocks, "shard", axis=0)
     o_piece, *pieces = run(
         "split_x",
         split_x_body,
@@ -870,6 +868,7 @@
         [shape((384, 256), BF), shape((1, 256), F32)],
         [place, o_piece, *x_pieces],
         smem=(0,),
+        after=totals[:1],
     )
     grad_tokens = run(
         "tokens",
@@ -884,12 +883,13 @@
         [shape((1536, 256), BF)],
         [place, *pieces],
         smem=(0,),
-        after=[grad_tokens, totals[0]],
+        after=[grad_tokens],
     )[0]
-    grad_query, grad_key, grad_value, grad_out, grad_gain = run(
-        "weights",
-        weights_body,
+    block_out, grad_query, grad_key, grad_value, grad_out, grad_gain = run(
+        "finish",
+        functools.partial(finish_body, micro),
         [
+            shape(tokens.shape, BF),
             shape(w_query.shape, F32),
             shape(w_key.shape, F32),
             shape(w_value.shape, F32),
@@ -898,6 +898,8 @@
         ],
         [
             place,
+            order,
+            block_rows,
             piece,
             swap_core(piece),
             w_query,
@@ -906,7 +908,6 @@
             gain_attn.astype(F32).reshape(-1, 1),
         ],
         smem=(0,),
-        after=[block_out],
     )
 
     return (

time: 454 us -> 451 us (level)
    pallas_call x22 -> x21, Pallas kernels: 88.8 us -> 86.8 us  [run(): pl.pallas_call(whole, out_shape=outs, in_specs=[SMEM if i in smem else VM...]
  transfers between devices with their start and end apart: 57 -> 57, of which waited for: 33 -> 34; matrix products, arithmetic and copies ran while one was open for 1% -> 1% of each run, Pallas kernels for 32% -> 31%
where the time goes in v5:
time: 451 us; the launch traced here: 443 us
  waiting for transfers between devices  156 us (35%)
  Pallas kernels  146 us (32%)
  starting transfers between devices  113 us (25%)
  between operations  14.6 us (3%)
  local copies, waits for them, and re-layouts  12.6 us (3%)
    pallas_call x21, Pallas kernels, run(): pl.pallas_call(whole, out_shape=outs, in_specs=[SMEM if i in smem else VM...  86.8 us
    ppermute x22, waiting for transfers between devices, from_right(): lax.ppermute(v, 'shard', [(i, (i - k) % SHARDS) for i in range(SHARDS)])  75 us
    pallas_call x2, Pallas kernels, expert_call(): pl.pallas_call(functools.partial(expert_body, m, last, len(after)), grid=...  58.9 us
    ppermute x15, waiting for transfers between devices, to_right(): lax.ppermute(v, 'shard', [(i, (i + k) % SHARDS) for i in range(SHARDS)])  45.7 us
    all_to_all x5, starting transfers between devices, exchange(): return lax.all_to_all(v, 'expert', split_axis=0, concat_axis=0, tiled=True)  41.5 us
    ppermute x22, starting transfers between devices, from_right(): lax.ppermute(v, 'shard', [(i, (i - k) % SHARDS) for i in range(SHARDS)])  33.2 us
    ppermute x15, starting transfers between devices, to_right(): lax.ppermute(v, 'shard', [(i, (i + k) % SHARDS) for i in range(SHARDS)])  20 us
    all_to_all x5, waiting for transfers between devices, exchange(): return lax.all_to_all(v, 'expert', split_axis=0, concat_axis=0, tiled=True)  18.1 us
  transfers between devices with their start and end apart: 57, of which 34 were waited for; matrix products, arithmetic and copies ran while one was open for 1% of the time, Pallas kernels for 31%

profile of v5, /device:TPU:1, one launch (start us, length us, event | category | flops | bytes accessed | tf_op | source)
XLA Modules:
  0.0 442.7 jit_solution(13918004532828164971)
XLA Ops:
  22.3 11.8 %collective-permute-done.refs_5_ = bf16[2,128,1024]{2,1,0:T(8,128)(2,1)} collective-permute-done((bf16[2,128,1024]{2,1,0:T(8,128)(2,1)}, bf16[2,128,1024]{2,1,0:T(8,128)(2,1)}, u32[]{:S(2)}, u32[]{:S(2)}) %collective-permute-start) | collective-permute-done | bytes 524320 | tf_op jit(solution)/shard_map/ppermute | solution.py:597
  48.1 17.3 %collective-permute-done.4.refs_5_ = bf16[128,1024]{1,0:T(8,128)(2,1)S(1)} collective-permute-done((bf16[128,1024]{1,0:T(8,128)(2,1)}, bf16[128,1024]{1,0:T(8,128)(2,1)S(1)}, u32[]{:S(2)}, u32[]{:S(2)}) %collective-permute-start.4) | collective-permute-done | bytes 262176 | tf_op jit(solution)/shard_map/ppermute | solution.py:597
  66.9 7.4 %attend.2 = (bf16[128,1024]{1,0:T(8,128)(2,1)}, bf16[128,1024]{1,0:T(8,128)(2,1)}, bf16[128,1024]{1,0:T(8,128)(2,1)}, bf16[128,1024]{1,0:T(8,128)(2,1)}, bf16[12...) custom-call(s32[1]{0:T(128)} %bitcast.refs_0_.refs_1_, ...), custom_call_target="tpu_custom_call" | custom-call | flops 1 | bytes 26280000 | tf_op jit(solution)/shard_map/attend/pallas_call | solution.py:85
  78.0 4.0 collective-permute-done.9.refs_1_
  82.7 3.9 collective-permute-start.11
  91.1 5.8 %collective-permute-done.12.refs_6_.refs_3_.refs_10_ = bf16[128,1024]{1,0:T(8,128)(2,1)S(1)} collective-permute-done((bf16[128,1024]{1,0:T(8,128)(2,1)}, bf16[128,1024]{1,0:T(8,128)(2,1)S(1)}, u32[]{:S(2)}, u32[]{:S(2)}) %collective-permute-start.12) | collective-permute-done | bytes 262176 | tf_op jit(solution)/shard_map/ppermute | solution.py:597
  96.9 4.4 collective-permute-done.11.refs_5_.refs_2_.refs_9_
  102.1 4.3 leave.3
  106.4 9.7 %all-to-all-start = ((bf16[32,48,1024]{2,1,0:T(8,128)(2,1)}), bf16[32,48,1024]{2,1,0:T(8,128)(2,1)}, u32[]{:S(2)}, u32[]{:S(2)}) async-start(bf16[32,48,1024]{2,1,0:T(8,128)(2,1)} %bitcast.29), calls=%async_computation | async-start | bytes 6291456 | tf_op jit(solution)/shard_map/all_to_all | solution.py:648
  118.8 7.0 %attend.3 = (bf16[128,1024]{1,0:T(8,128)(2,1)}, bf16[128,1024]{1,0:T(8,128)(2,1)}, bf16[128,1024]{1,0:T(8,128)(2,1)}, bf16[128,1024]{1,0:T(8,128)(2,1)}, bf16[12...) custom-call(s32[1]{0:T(128)} %bitcast.refs_0_.refs_1_, ...), custom_call_target="tpu_custom_call" | custom-call | flops 1 | bytes 26280000 | tf_op jit(solution)/shard_map/attend/pallas_call | solution.py:85
  128.6 13.6 %collective-permute-done.13.refs_1_ = bf16[128,1024]{1,0:T(8,128)(2,1)S(1)} collective-permute-done((bf16[128,1024]{1,0:T(8,128)(2,1)}, bf16[128,1024]{1,0:T(8,128)(2,1)S(1)}, u32[]{:S(2)}, u32[]{:S(2)}) %collective-permute-start.13) | collective-permute-done | bytes 262176 | tf_op jit(solution)/shard_map/ppermute | solution.py:601
  142.1 6.1 %collective-permute-done.14.refs_2_ = bf16[128,1024]{1,0:T(8,128)(2,1)S(1)} collective-permute-done((bf16[128,1024]{1,0:T(8,128)(2,1)}, bf16[128,1024]{1,0:T(8,128)(2,1)S(1)}, u32[]{:S(2)}, u32[]{:S(2)}) %collective-permute-start.14) | collective-permute-done | bytes 262176 | tf_op jit(solution)/shard_map/ppermute | solution.py:601
  149.2 4.3 leave.2
  155.3 7.4 %all-to-all-start.1 = ((bf16[32,48,1024]{2,1,0:T(8,128)(2,1)}), bf16[32,48,1024]{2,1,0:T(8,128)(2,1)}, u32[]{:S(2)}, u32[]{:S(2)}) async-start(bf16[32,48,1024]{2,1,0:T(8,128)(2,1)} %bitcast.27), calls=%async_computation.1 | async-start | bytes 6291456 | tf_op jit(solution)/shard_map/all_to_all | solution.py:648
  167.0 7.4 %collective-permute-done.21.refs_9_.refs_8_ = bf16[1,3,512,128]{3,2,1,0:T(8,128)(2,1)S(1)} collective-permute-done((bf16[1,3,512,128]{3,2,1,0:T(8,128)(2,1)S(1)}, bf16[1,3,512,128]{3,2,1,0:T(8,128)(2,1)S(1)}, u32[]{:S(2)}, u32[]{:S(2)}) %collective-permute-start.21) | collective-permute-done | bytes 393248 | tf_op jit(solution)/shard_map/ppermute | solution.py:597
  175.5 30.0 %expert.2 = (bf16[32,128,1024]{2,1,0:T(8,128)(2,1)}, bf16[1536,1024]{1,0:T(8,128)(2,1)}, f32[3,1024,512]{2,1,0:T(8,128)}) custom-call(bf16[1536,1024]{1,0:T(8,128)(2,1)} %get-tuple-element.117.refs_0_, s32[1]{0:T(128)} %bitcast.refs_0_.refs_1_, s32[1,32]{1,0:T(1,128)} %bitcast.36, bf16[1536,1024]{1,0:T(8,128)(2,1)} %bitcast.5.refs_3_, ...), custom_call_target="tpu_custom_call" | custom-call | flops 1 | bytes 97200000 | tf_op jit(solution)/shard_map/expert/pallas_call | solution.py:376
  205.5 8.8 %all-to-all-start.2 = ((bf16[32,48,1024]{2,1,0:T(8,128)(2,1)}), bf16[32,48,1024]{2,1,0:T(8,128)(2,1)}, u32[]{:S(2)}, u32[]{:S(2)}) async-start(bf16[32,48,1024]{2,1,0:T(8,128)(2,1)} %bitcast.10), calls=%async_computation.3 | async-start | bytes 6291456 | tf_op jit(solution)/shard_map/all_to_all | solution.py:648
  214.3 29.0 %expert.3 = (bf16[1536,1024]{1,0:T(8,128)(2,1)}, bf16[1536,1024]{1,0:T(8,128)(2,1)}, bf16[4,3,1024,128]{3,2,1,0:T(8,128)(2,1)}) custom-call(s32[1]{0:T(128)} %bitcast.refs_0_.refs_1_, s32[1,32]{1,0:T(1,128)} %bitcast.37, bf16[1536,1024]{1,0:T(8,128)(2,1)} %bitcast.8.refs_2_, bf16[32,2,144,1024]{3,2,1,0:T(8,128)(2,1)} %bitcast.23, ...), custom_call_target="tpu_custom_call" | custom-call | flops 1 | bytes 97200000 | tf_op jit(solution)/shard_map/expert/pallas_call | solution.py:376
  243.3 10.2 %all-to-all-done.2 = bf16[32,48,1024]{2,1,0:T(8,128)(2,1)} async-done(((bf16[32,48,1024]{2,1,0:T(8,128)(2,1)}), bf16[32,48,1024]{2,1,0:T(8,128)(2,1)}, u32[]{:S(2)}, u32[]{:S(2)}) %all-to-all-start.2) | async-done | bytes 3145760 | tf_op jit(solution)/shard_map/all_to_all | solution.py:648
  253.5 7.4 %all-to-all-start.3 = ((bf16[32,48,1024]{2,1,0:T(8,128)(2,1)}), bf16[32,48,1024]{2,1,0:T(8,128)(2,1)}, u32[]{:S(2)}, u32[]{:S(2)}) async-start(bf16[32,48,1024]{2,1,0:T(8,128)(2,1)} %bitcast.26), calls=%async_computation.4 | async-start | bytes 6291456 | tf_op jit(solution)/shard_map/all_to_all | solution.py:648
  269.5 5.3 %collective-permute-done.24.refs_6_ = bf16[128,1024]{1,0:T(8,128)(2,1)S(1)} collective-permute-done((bf16[128,1024]{1,0:T(8,128)(2,1)}, bf16[128,1024]{1,0:T(8,128)(2,1)S(1)}, u32[]{:S(2)}, u32[]{:S(2)}) %collective-permute-start.24) | collective-permute-done | bytes 262176 | tf_op jit(solution)/shard_map/ppermute | solution.py:597
  274.8 6.5 %collective-permute-done.23.refs_5_ = bf16[128,1024]{1,0:T(8,128)(2,1)S(1)} collective-permute-done((bf16[128,1024]{1,0:T(8,128)(2,1)}, bf16[128,1024]{1,0:T(8,128)(2,1)S(1)}, u32[]{:S(2)}, u32[]{:S(2)}) %collective-permute-start.23) | collective-permute-done | bytes 262176 | tf_op jit(solution)/shard_map/ppermute | solution.py:597
  282.1 9.3 %attend_back.2 = (bf16[128,1024]{1,0:T(8,128)(2,1)}, bf16[128,1024]{1,0:T(8,128)(2,1)}, bf16[128,1024]{1,0:T(8,128)(2,1)}, bf16[128,1024]{1,0:T(8,128)(2,1)}, bf...) custom-call(s32[1]{0:T(128)} %bitcast.refs_0_.refs_1_, s32[2,1,2]{2,1,0:T(1,128)} %refs_1_.14, ...), custom_call_target="tpu_custom_call" | custom-call | flops 1 | bytes 39600000 | tf_op jit(solution)/shard_map/attend_back/pallas_call | solution.py:85
  295.2 4.5 %collective-permute-done.25.refs_6_.refs_3_ = bf16[128,1024]{1,0:T(8,128)(2,1)S(1)} collective-permute-done((bf16[128,1024]{1,0:T(8,128)(2,1)}, bf16[128,1024]{1,0:T(8,128)(2,1)S(1)}, u32[]{:S(2)}, u32[]{:S(2)}) %collective-permute-start.25) | collective-permute-done | bytes 262176 | tf_op jit(solution)/shard_map/ppermute | solution.py:601
  299.6 7.4 %collective-permute-done.26.refs_7_.refs_4_ = bf16[128,1024]{1,0:T(8,128)(2,1)S(1)} collective-permute-done((bf16[128,1024]{1,0:T(8,128)(2,1)}, bf16[128,1024]{1,0:T(8,128)(2,1)S(1)}, u32[]{:S(2)}, u32[]{:S(2)}) %collective-permute-start.26) | collective-permute-done | bytes 262176 | tf_op jit(solution)/shard_map/ppermute | solution.py:601
  307.0 6.2 %all-to-all-done.3 = bf16[32,48,1024]{2,1,0:T(8,128)(2,1)} async-done(((bf16[32,48,1024]{2,1,0:T(8,128)(2,1)}), bf16[32,48,1024]{2,1,0:T(8,128)(2,1)}, u32[]{:S(2)}, u32[]{:S(2)}) %all-to-all-start.3) | async-done | bytes 3145760 | tf_op jit(solution)/shard_map/all_to_all | solution.py:648
  317.0 8.3 %all-to-all-start.4 = ((bf16[32,48,1024]{2,1,0:T(8,128)(2,1)}), bf16[32,48,1024]{2,1,0:T(8,128)(2,1)}, u32[]{:S(2)}, u32[]{:S(2)}) async-start(bf16[32,48,1024]{2,1,0:T(8,128)(2,1)} %bitcast.25), calls=%async_computation.5 | async-start | bytes 6291456 | tf_op jit(solution)/shard_map/all_to_all | solution.py:648
  334.2 6.6 %collective-permute-done.29.refs_5_ = bf16[128,1024]{1,0:T(8,128)(2,1)S(1)} collective-permute-done((bf16[128,1024]{1,0:T(8,128)(2,1)S(1)}, bf16[128,1024]{1,0:T(8,128)(2,1)S(1)}, u32[]{:S(2)}, u32[]{:S(2)}) %collective-permute-start.29) | collective-permute-done | bytes 262176 | tf_op jit(solution)/shard_map/ppermute | solution.py:597
  341.6 11.3 %attend_back.3 = (bf16[128,1024]{1,0:T(8,128)(2,1)}, bf16[128,1024]{1,0:T(8,128)(2,1)}, bf16[128,1024]{1,0:T(8,128)(2,1)}, bf16[128,1024]{1,0:T(8,128)(2,1)}, bf...) custom-call(s32[1]{0:T(128)} %bitcast.refs_0_.refs_1_, s32[2,1,2]{2,1,0:T(1,128)} %refs_1_.14, ...), custom_call_target="tpu_custom_call" | custom-call | flops 1 | bytes 39600000 | tf_op jit(solution)/shard_map/attend_back/pallas_call | solution.py:85
  366.2 5.6 %collective-permute-done.36.refs_5_.refs_9_ = bf16[128,1024]{1,0:T(8,128)(2,1)S(1)} collective-permute-done((bf16[128,1024]{1,0:T(8,128)(2,1)}, bf16[128,1024]{1,0:T(8,128)(2,1)S(1)}, u32[]{:S(2)}, u32[]{:S(2)}) %collective-permute-start.36) | collective-permute-done | bytes 262176 | tf_op jit(solution)/shard_map/ppermute | solution.py:601
  390.6 7.1 %collective-permute-done.38.refs_2_ = bf16[448,256]{1,0:T(8,128)(2,1)S(1)} collective-permute-done((bf16[448,256]{1,0:T(8,128)(2,1)S(1)}, bf16[448,256]{1,0:T(8,128)(2,1)S(1)}, u32[]{:S(2)}, u32[]{:S(2)}) %collective-permute-start.38) | collective-permute-done | bytes 229408 | tf_op jit(solution)/shard_map/ppermute | solution.py:636
  430.9 4.8 %finish.1 = (bf16[2,128,1024]{2,1,0:T(8,128)(2,1)}, f32[256,1024]{1,0:T(8,128)}, f32[256,512]{1,0:T(8,128)}, f32[256,512]{1,0:T(8,128)}, f32[256,1024]{1,0:T(8,128)}, /*index=5*/f32[1,256]{1,0:T(1,128)}) custom-call(s32[1]{0:T(128)} %bitcast.refs_0_.refs_1_, s32[2,1,512]{2,1,0:T(1,128)} %refs_1_.15, bf16[4,2,128,1024]{3,2,1,0:T(8,128)(2,1)} %bitcast.30, ...), custom_call_target="tpu_custom_call" | custom-call | flops 1 | bytes 19800000 | tf_op jit(solution)/shard_map/finish/pallas_call | solution.py:85
  (209 shorter events, 145.9 us)
Async XLA Ops:
  7.2 167.6 %all-gather.5.cloned.1.call-start = ((), (), s32[]{:S(2)}) async-start(), calls=%async_computation.9 | async-start | bytes 19464192 | tf_op jit(solution)/shard_map/all_gather | solution.py:724
  7.2 15.1 %collective-permute-start.1 = (bf16[2,128,1024]{2,1,0:T(8,128)(2,1)}, bf16[2,128,1024]{2,1,0:T(8,128)(2,1)S(1)}, u32[]{:S(2)}, u32[]{:S(2)}) collective-permute-start(bf16[2,128,1024]{2,1,0:T(8,128)(2,1)} %refs_4_.1), channel_id=1, source_target_pairs={{0,2},{1,3},{2,0},{3,1},{4,6},{5,7},{6,4},{7,5},{8,10},{9,11},{10,... | collective-permute-start | bytes 1572872 | tf_op jit(solution)/shard_map/ppermute | solution.py:597
  10.9 23.2 %collective-permute-start = (bf16[2,128,1024]{2,1,0:T(8,128)(2,1)}, bf16[2,128,1024]{2,1,0:T(8,128)(2,1)}, u32[]{:S(2)}, u32[]{:S(2)}) collective-permute-start(bf16[2,128,1024]{2,1,0:T(8,128)(2,1)} %refs_4_.1), channel_id=1, source_target_pairs={{0,3},{1,0},{2,1},{3,2},{4,7},{5,4},{6,5},{7,6},{8,11},{9,8},{10,9... | collective-permute-start | bytes 1572872 | tf_op jit(solution)/shard_map/ppermute | solution.py:597
  11.7 23.1 %collective-permute-start.2 = (bf16[2,128,1024]{2,1,0:T(8,128)(2,1)}, bf16[2,128,1024]{2,1,0:T(8,128)(2,1)}, u32[]{:S(2)}, u32[]{:S(2)}) collective-permute-start(bf16[2,128,1024]{2,1,0:T(8,128)(2,1)} %refs_4_.1), channel_id=1, source_target_pairs={{0,1},{1,2},{2,3},{3,0},{4,5},{5,6},{6,7},{7,4},{8,9},{9,10},{10,1... | collective-permute-start | bytes 1572872 | tf_op jit(solution)/shard_map/ppermute | solution.py:597
  39.2 26.2 %collective-permute-start.6 = (bf16[272,512]{1,0:T(8,128)(2,1)}, bf16[272,512]{1,0:T(8,128)(2,1)S(1)}, u32[]{:S(2)}, u32[]{:S(2)}) collective-permute-start(bf16[272,512]{1,0:T(8,128)(2,1)} %get-tuple-element.104), channel_id=1, source_target_pairs={{0,3},{1,0},{2,1},{3,2},{4,7},{5,4},{6,5},{7,6},{8,11},{9,8},{10,9... | collective-permute-start | bytes 835592 | tf_op jit(solution)/shard_map/ppermute | solution.py:597
  40.6 24.9 %collective-permute-start.7 = (bf16[272,512]{1,0:T(8,128)(2,1)}, bf16[272,512]{1,0:T(8,128)(2,1)S(1)}, u32[]{:S(2)}, u32[]{:S(2)}) collective-permute-start(bf16[272,512]{1,0:T(8,128)(2,1)} %get-tuple-element.105), channel_id=1, source_target_pairs={{0,2},{1,3},{2,0},{3,1},{4,6},{5,7},{6,4},{7,5},{8,10},{9,11},{10,... | collective-permute-start | bytes 835592 | tf_op jit(solution)/shard_map/ppermute | solution.py:597
  42.2 23.2 %collective-permute-start.8 = (bf16[272,512]{1,0:T(8,128)(2,1)}, bf16[272,512]{1,0:T(8,128)(2,1)S(1)}, u32[]{:S(2)}, u32[]{:S(2)}) collective-permute-start(bf16[272,512]{1,0:T(8,128)(2,1)} %get-tuple-element.106), channel_id=1, source_target_pairs={{0,1},{1,2},{2,3},{3,0},{4,5},{5,6},{6,7},{7,4},{8,9},{9,10},{10,1... | collective-permute-start | bytes 835592 | tf_op jit(solution)/shard_map/ppermute | solution.py:597
  42.5 22.9 %collective-permute-start.4 = (bf16[128,1024]{1,0:T(8,128)(2,1)}, bf16[128,1024]{1,0:T(8,128)(2,1)S(1)}, u32[]{:S(2)}, u32[]{:S(2)}) collective-permute-start(bf16[128,1024]{1,0:T(8,128)(2,1)} %get-tuple-element.102.refs_3_), channel_id=1, source_target_pairs={{0,2},{1,3},{2,0},{3,1},{4,6},{5,7},{6,4},{7,5},{8,10},{9,11},{10,... | collective-permute-start | bytes 786440 | tf_op jit(solution)/shard_map/ppermute | solution.py:597
  46.3 19.1 %collective-permute-start.3 = (bf16[128,1024]{1,0:T(8,128)(2,1)}, bf16[128,1024]{1,0:T(8,128)(2,1)S(1)}, u32[]{:S(2)}, u32[]{:S(2)}) collective-permute-start(bf16[128,1024]{1,0:T(8,128)(2,1)} %get-tuple-element.102.refs_3_), channel_id=1, source_target_pairs={{0,3},{1,0},{2,1},{3,2},{4,7},{5,4},{6,5},{7,6},{8,11},{9,8},{10,9... | collective-permute-start | bytes 786440 | tf_op jit(solution)/shard_map/ppermute | solution.py:597
  74.7 15.5 %collective-permute-start.18 = (bf16[128,1024]{1,0:T(8,128)(2,1)}, bf16[128,1024]{1,0:T(8,128)(2,1)}, u32[]{:S(2)}, u32[]{:S(2)}) collective-permute-start(bf16[128,1024]{1,0:T(8,128)(2,1)} %get-tuple-element.119), channel_id=1, source_target_pairs={{0,2},{1,3},{2,0},{3,1},{4,6},{5,7},{6,4},{7,5},{8,10},{9,11},{10,... | collective-permute-start | bytes 786440 | tf_op jit(solution)/shard_map/ppermute | solution.py:601
  78.0 13.1 %collective-permute-start.19 = (bf16[128,1024]{1,0:T(8,128)(2,1)}, bf16[128,1024]{1,0:T(8,128)(2,1)}, u32[]{:S(2)}, u32[]{:S(2)}) collective-permute-start(bf16[128,1024]{1,0:T(8,128)(2,1)} %get-tuple-element.120), channel_id=1, source_target_pairs={{0,3},{1,0},{2,1},{3,2},{4,7},{5,4},{6,5},{7,6},{8,11},{9,8},{10,9... | collective-permute-start | bytes 786440 | tf_op jit(solution)/shard_map/ppermute | solution.py:601
  82.7 14.2 %collective-permute-start.12 = (bf16[128,1024]{1,0:T(8,128)(2,1)}, bf16[128,1024]{1,0:T(8,128)(2,1)S(1)}, u32[]{:S(2)}, u32[]{:S(2)}) collective-permute-start(bf16[128,1024]{1,0:T(8,128)(2,1)} %hold.7.refs_3_), channel_id=1, source_target_pairs={{0,1},{1,2},{2,3},{3,0},{4,5},{5,6},{6,7},{7,4},{8,9},{9,10},{10,1... | collective-permute-start | bytes 786440 | tf_op jit(solution)/shard_map/ppermute | solution.py:597
  82.7 18.6 %collective-permute-start.11 = (bf16[128,1024]{1,0:T(8,128)(2,1)}, bf16[128,1024]{1,0:T(8,128)(2,1)S(1)}, u32[]{:S(2)}, u32[]{:S(2)}) collective-permute-start(bf16[128,1024]{1,0:T(8,128)(2,1)} %hold.7.refs_3_), channel_id=1, source_target_pairs={{0,2},{1,3},{2,0},{3,1},{4,6},{5,7},{6,4},{7,5},{8,10},{9,11},{10,... | collective-permute-start | bytes 786440 | tf_op jit(solution)/shard_map/ppermute | solution.py:597
  86.7 14.6 %collective-permute-start.10 = (bf16[128,1024]{1,0:T(8,128)(2,1)}, bf16[128,1024]{1,0:T(8,128)(2,1)S(1)}, u32[]{:S(2)}, u32[]{:S(2)}) collective-permute-start(bf16[128,1024]{1,0:T(8,128)(2,1)} %hold.7.refs_3_), channel_id=1, source_target_pairs={{0,3},{1,0},{2,1},{3,2},{4,7},{5,4},{6,5},{7,6},{8,11},{9,8},{10,9... | collective-permute-start | bytes 786440 | tf_op jit(solution)/shard_map/ppermute | solution.py:597
  106.4 48.9 %all-to-all-start = ((bf16[32,48,1024]{2,1,0:T(8,128)(2,1)}), bf16[32,48,1024]{2,1,0:T(8,128)(2,1)}, u32[]{:S(2)}, u32[]{:S(2)}) async-start(bf16[32,48,1024]{2,1,0:T(8,128)(2,1)} %bitcast.29), calls=%async_computation | async-start | bytes 6291456 | tf_op jit(solution)/shard_map/all_to_all | solution.py:648
  116.1 32.1 %collective-permute-start.17 = (bf16[2,3,512,128]{3,2,1,0:T(8,128)(2,1)}, bf16[2,3,512,128]{3,2,1,0:T(8,128)(2,1)S(1)}, u32[]{:S(2)}, u32[]{:S(2)}) collective-permute-start(bf16[2,3,512,128]{3,2,1,0:T(8,128)(2,1)} %hold.8.refs_5_.refs_4_), channel_id=1, source_target_pairs={{0,1},{1,2},{2,3},{3,0},{4,5},{5,6},{6,7},{7,4},{8,9},{9,10},{10,1... | collective-permute-start | bytes 2359304 | tf_op jit(solution)/shard_map/ppermute | solution.py:597
  116.2 32.1 %collective-permute-start.16 = (bf16[2,3,512,128]{3,2,1,0:T(8,128)(2,1)}, bf16[2,3,512,128]{3,2,1,0:T(8,128)(2,1)}, u32[]{:S(2)}, u32[]{:S(2)}) collective-permute-start(bf16[2,3,512,128]{3,2,1,0:T(8,128)(2,1)} %hold.8.refs_5_.refs_4_), channel_id=1, source_target_pairs={{0,3},{1,0},{2,1},{3,2},{4,7},{5,4},{6,5},{7,6},{8,11},{9,8},{10,9... | collective-permute-start | bytes 2359304 | tf_op jit(solution)/shard_map/ppermute | solution.py:597
  125.9 16.3 %collective-permute-start.13 = (bf16[128,1024]{1,0:T(8,128)(2,1)}, bf16[128,1024]{1,0:T(8,128)(2,1)S(1)}, u32[]{:S(2)}, u32[]{:S(2)}) collective-permute-start(bf16[128,1024]{1,0:T(8,128)(2,1)} %get-tuple-element.112), channel_id=1, source_target_pairs={{0,1},{1,2},{2,3},{3,0},{4,5},{5,6},{6,7},{7,4},{8,9},{9,10},{10,1... | collective-permute-start | bytes 786440 | tf_op jit(solution)/shard_map/ppermute | solution.py:601
  125.9 22.3 %collective-permute-start.14 = (bf16[128,1024]{1,0:T(8,128)(2,1)}, bf16[128,1024]{1,0:T(8,128)(2,1)S(1)}, u32[]{:S(2)}, u32[]{:S(2)}) collective-permute-start(bf16[128,1024]{1,0:T(8,128)(2,1)} %get-tuple-element.113), channel_id=1, source_target_pairs={{0,2},{1,3},{2,0},{3,1},{4,6},{5,7},{6,4},{7,5},{8,10},{9,11},{10,... | collective-permute-start | bytes 786440 | tf_op jit(solution)/shard_map/ppermute | solution.py:601
  127.8 20.4 %collective-permute-start.15 = (bf16[128,1024]{1,0:T(8,128)(2,1)}, bf16[128,1024]{1,0:T(8,128)(2,1)S(1)}, u32[]{:S(2)}, u32[]{:S(2)}) collective-permute-start(bf16[128,1024]{1,0:T(8,128)(2,1)} %get-tuple-element.114), channel_id=1, source_target_pairs={{0,3},{1,0},{2,1},{3,2},{4,7},{5,4},{6,5},{7,6},{8,11},{9,8},{10,9... | collective-permute-start | bytes 786440 | tf_op jit(solution)/shard_map/ppermute | solution.py:601
  155.3 50.2 %all-to-all-start.1 = ((bf16[32,48,1024]{2,1,0:T(8,128)(2,1)}), bf16[32,48,1024]{2,1,0:T(8,128)(2,1)}, u32[]{:S(2)}, u32[]{:S(2)}) async-start(bf16[32,48,1024]{2,1,0:T(8,128)(2,1)} %bitcast.27), calls=%async_computation.1 | async-start | bytes 6291456 | tf_op jit(solution)/shard_map/all_to_all | solution.py:648
  162.7 215.3 %reduce-scatter.3.cloned.1.call-start = ((), (), s32[]{:S(2)}) async-start(), calls=%async_computation.7 | async-start | bytes 8650752 | tf_op jit(solution)/shard_map/reduce_scatter | solution.py:644
  205.5 48.0 %all-to-all-start.2 = ((bf16[32,48,1024]{2,1,0:T(8,128)(2,1)}), bf16[32,48,1024]{2,1,0:T(8,128)(2,1)}, u32[]{:S(2)}, u32[]{:S(2)}) async-start(bf16[32,48,1024]{2,1,0:T(8,128)(2,1)} %bitcast.10), calls=%async_computation.3 | async-start | bytes 6291456 | tf_op jit(solution)/shard_map/all_to_all | solution.py:648
  214.3 191.7 %reduce-scatter.5.cloned.1.call-start = ((), (), s32[]{:S(2)}) async-start(), calls=%async_computation.8 | async-start | bytes 3932160 | tf_op jit(solution)/shard_map/reduce_scatter | solution.py:799
  253.5 59.7 %all-to-all-start.3 = ((bf16[32,48,1024]{2,1,0:T(8,128)(2,1)}), bf16[32,48,1024]{2,1,0:T(8,128)(2,1)}, u32[]{:S(2)}, u32[]{:S(2)}) async-start(bf16[32,48,1024]{2,1,0:T(8,128)(2,1)} %bitcast.26), calls=%async_computation.4 | async-start | bytes 6291456 | tf_op jit(solution)/shard_map/all_to_all | solution.py:648
  265.6 15.7 %collective-permute-start.23 = (bf16[128,1024]{1,0:T(8,128)(2,1)}, bf16[128,1024]{1,0:T(8,128)(2,1)S(1)}, u32[]{:S(2)}, u32[]{:S(2)}) collective-permute-start(bf16[128,1024]{1,0:T(8,128)(2,1)} %get-tuple-element.134.refs_3_), channel_id=1, source_target_pairs={{0,2},{1,3},{2,0},{3,1},{4,6},{5,7},{6,4},{7,5},{8,10},{9,11},{10,... | collective-permute-start | bytes 786440 | tf_op jit(solution)/shard_map/ppermute | solution.py:597
  292.7 14.3 %collective-permute-start.26 = (bf16[128,1024]{1,0:T(8,128)(2,1)}, bf16[128,1024]{1,0:T(8,128)(2,1)S(1)}, u32[]{:S(2)}, u32[]{:S(2)}) collective-permute-start(bf16[128,1024]{1,0:T(8,128)(2,1)} %get-tuple-element.141), channel_id=1, source_target_pairs={{0,2},{1,3},{2,0},{3,1},{4,6},{5,7},{6,4},{7,5},{8,10},{9,11},{10,... | collective-permute-start | bytes 786440 | tf_op jit(solution)/shard_map/ppermute | solution.py:601
  317.0 60.9 %all-to-all-start.4 = ((bf16[32,48,1024]{2,1,0:T(8,128)(2,1)}), bf16[32,48,1024]{2,1,0:T(8,128)(2,1)}, u32[]{:S(2)}, u32[]{:S(2)}) async-start(bf16[32,48,1024]{2,1,0:T(8,128)(2,1)} %bitcast.25), calls=%async_computation.5 | async-start | bytes 6291456 | tf_op jit(solution)/shard_map/all_to_all | solution.py:648
  325.3 105.0 %all-gather.7.cloned.1.call-start = ((), (), s32[]{:S(2)}) async-start(), calls=%async_computation.10 | async-start | bytes 2621440 | tf_op jit(solution)/shard_map/all_gather | solution.py:854
  326.4 14.4 %collective-permute-start.29 = (bf16[128,1024]{1,0:T(8,128)(2,1)S(1)}, bf16[128,1024]{1,0:T(8,128)(2,1)S(1)}, u32[]{:S(2)}, u32[]{:S(2)}) collective-permute-start(bf16[128,1024]{1,0:T(8,128)(2,1)S(1)} %copy-done.11), channel_id=1, source_target_pairs={{0,2},{1,3},{2,0},{3,1},{4,6},{5,7},{6,4},{7,5},{8,10},{9,11},{10,... | collective-permute-start | bytes 786440 | tf_op jit(solution)/shard_map/ppermute | solution.py:597
  355.2 16.5 %collective-permute-start.36 = (bf16[128,1024]{1,0:T(8,128)(2,1)}, bf16[128,1024]{1,0:T(8,128)(2,1)S(1)}, u32[]{:S(2)}, u32[]{:S(2)}) collective-permute-start(bf16[128,1024]{1,0:T(8,128)(2,1)} %get-tuple-element.158), channel_id=1, source_target_pairs={{0,2},{1,3},{2,0},{3,1},{4,6},{5,7},{6,4},{7,5},{8,10},{9,11},{10,... | collective-permute-start | bytes 786440 | tf_op jit(solution)/shard_map/ppermute | solution.py:601
  357.2 17.0 %collective-permute-start.37 = (bf16[128,1024]{1,0:T(8,128)(2,1)}, bf16[128,1024]{1,0:T(8,128)(2,1)}, u32[]{:S(2)}, u32[]{:S(2)}) collective-permute-start(bf16[128,1024]{1,0:T(8,128)(2,1)} %get-tuple-element.159), channel_id=1, source_target_pairs={{0,3},{1,0},{2,1},{3,2},{4,7},{5,4},{6,5},{7,6},{8,11},{9,8},{10,9... | collective-permute-start | bytes 786440 | tf_op jit(solution)/shard_map/ppermute | solution.py:601
  (69 other events, 399.8 us)
Sparse Core Ops, SparseCore 0:
  37.8 80.3 all-gather.4
  205.6 142.0 reduce-scatter.2
  350.2 46.2 reduce-scatter.4
  398.8 31.5 all-gather.6

commit v6 on v5

--- a/solution.py
+++ b/solution.py
@@ -535,7 +535,7 @@
     o_ref[...] = total(slice(256, 384)).astype(BF)
 
 
-def join_x_body(place, o, own, r1, r2, r3, out_ref, gain_ref):
+def join_x_body(place, o, own, r1, r2, r3, out_ref):
     x = x_of(place)
     gain = jnp.zeros((16, 256), F32)
     for k, ref in enumerate((own, r1, r2, r3)):
@@ -543,7 +543,9 @@
         out_ref[pl.ds(pl.multiple_of(s * 64, 64), 64), :] = ref[0:64, :]
         gain += ref[64:80, :].astype(F32)
     out_ref[256:384, :] = o[...]
-    gain_ref[...] = gain[0:1]
+    high = gain.astype(BF).astype(F32)
+    halves = jnp.where(iota((16, 256), 0) < 8, high, gain - high)
+    out_ref[384:400, :] = halves.astype(BF)
 
 
 def join_y_body(place, own, r1, r2, r3, out_ref):
@@ -553,14 +555,18 @@
         out_ref[pl.ds(pl.multiple_of(s * rows, rows), rows), :] = ref[...]
 
 
-def weights_body(place, own, got, wq, wk, wv, gain, q_ref, k_ref, v_ref, o_ref, gain_ref):
+def weights_body(
+    place, own, got, wq, wk, wv, gain, q_ref, k_ref, v_ref, o_ref, gain_ref, gain_ffn_ref
+):
     c = core_of(place)
+    halves = jnp.where(c == 0, own[384:400, :].astype(F32), got[384:400, :].astype(F32))
+    gain_ffn_ref[...] = halves[0:1] + halves[8:9]
     scale = gain[...]
     total = jnp.zeros((ROWS_HERE, 1), F32)
 
     def piece(ref, b):
         return jnp.concatenate(
-            [ref[j * 384 + b * 64 : j * 384 + (b + 1) * 64, :] for j in range(4)], axis=0
+            [ref[j * 400 + b * 64 : j * 400 + (b + 1) * 64, :] for j in range(4)], axis=0
         ).astype(F32)
 
     for b in range(6):
@@ -862,14 +868,14 @@
         after=[blocks],
     )
     x_pieces = scatter_x(pieces)
-    piece, gain_ffn_sum = run(
+    piece = run(
         "join_x",
         join_x_body,
-        [shape((384, 256), BF), shape((1, 256), F32)],
+        [shape((400, 256), BF)],
         [place, o_piece, *x_pieces],
         smem=(0,),
         after=totals[:1],
-    )
+    )[0]
     grad_tokens = run(
         "tokens",
         functools.partial(tokens_body, micro),
@@ -880,12 +886,12 @@
     piece = run(
         "join_y",
         join_y_body,
-        [shape((1536, 256), BF)],
+        [shape((1600, 256), BF)],
         [place, *pieces],
         smem=(0,),
         after=[grad_tokens],
     )[0]
-    block_out, grad_query, grad_key, grad_value, grad_out, grad_gain = run(
+    block_out, grad_query, grad_key, grad_value, grad_out, grad_gain, gain_ffn_sum = run(
         "finish",
         functools.partial(finish_body, micro),
         [
@@ -894,6 +900,7 @@
             shape(w_key.shape, F32),
             shape(w_value.shape, F32),
             shape(w_out.shape, F32),
+            shape((1, ROWS_HERE), F32),
             shape((1, ROWS_HERE), F32),
         ],
         [

time: 451 us -> 452 us (level)
  transfers between devices with their start and end apart: 57 -> 57, of which waited for: 34 -> 32; matrix products, arithmetic and copies ran while one was open for 1% -> 1% of each run, Pallas kernels for 31% -> 31%
where the time goes in v6:
time: 452 us; the launch traced here: 443 us
  waiting for transfers between devices  156 us (35%)
  Pallas kernels  146 us (32%)
  starting transfers between devices  113 us (25%)
  between operations  14.6 us (3%)
  local copies, waits for them, and re-layouts  13 us (3%)
    pallas_call x21, Pallas kernels, run(): pl.pallas_call(whole, out_shape=outs, in_specs=[SMEM if i in smem else VM...  87 us
    ppermute x22, waiting for transfers between devices, from_right(): lax.ppermute(v, 'shard', [(i, (i - k) % SHARDS) for i in range(SHARDS)])  75.1 us
    pallas_call x2, Pallas kernels, expert_call(): pl.pallas_call(functools.partial(expert_body, m, last, len(after)), grid=...  58.9 us
    ppermute x15, waiting for transfers between devices, to_right(): lax.ppermute(v, 'shard', [(i, (i + k) % SHARDS) for i in range(SHARDS)])  45.9 us
    all_to_all x5, starting transfers between devices, exchange(): return lax.all_to_all(v, 'expert', split_axis=0, concat_axis=0, tiled=True)  41.5 us
    ppermute x22, starting transfers between devices, from_right(): lax.ppermute(v, 'shard', [(i, (i - k) % SHARDS) for i in range(SHARDS)])  33.2 us
    ppermute x15, starting transfers between devices, to_right(): lax.ppermute(v, 'shard', [(i, (i + k) % SHARDS) for i in range(SHARDS)])  20 us
    all_to_all x5, waiting for transfers between devices, exchange(): return lax.all_to_all(v, 'expert', split_axis=0, concat_axis=0, tiled=True)  18.1 us
  transfers between devices with their start and end apart: 57, of which 32 were waited for; matrix products, arithmetic and copies ran while one was open for 1% of the time, Pallas kernels for 31%

profile of v6, /device:TPU:1, one launch (start us, length us, event | category | flops | bytes accessed | tf_op | source)
XLA Modules:
  0.0 443.4 jit_solution(17736775180183731330)
XLA Ops:
  22.3 11.8 %collective-permute-done.refs_5_ = bf16[2,128,1024]{2,1,0:T(8,128)(2,1)} collective-permute-done((bf16[2,128,1024]{2,1,0:T(8,128)(2,1)}, bf16[2,128,1024]{2,1,0:T(8,128)(2,1)}, u32[]{:S(2)}, u32[]{:S(2)}) %collective-permute-start) | collective-permute-done | bytes 524320 | tf_op jit(solution)/shard_map/ppermute | solution.py:603
  48.1 17.3 %collective-permute-done.4.refs_5_ = bf16[128,1024]{1,0:T(8,128)(2,1)S(1)} collective-permute-done((bf16[128,1024]{1,0:T(8,128)(2,1)}, bf16[128,1024]{1,0:T(8,128)(2,1)S(1)}, u32[]{:S(2)}, u32[]{:S(2)}) %collective-permute-start.4) | collective-permute-done | bytes 262176 | tf_op jit(solution)/shard_map/ppermute | solution.py:603
  66.9 7.4 %attend.2 = (bf16[128,1024]{1,0:T(8,128)(2,1)}, bf16[128,1024]{1,0:T(8,128)(2,1)}, bf16[128,1024]{1,0:T(8,128)(2,1)}, bf16[128,1024]{1,0:T(8,128)(2,1)}, bf16[12...) custom-call(s32[1]{0:T(128)} %bitcast.refs_0_.refs_1_, ...), custom_call_target="tpu_custom_call" | custom-call | flops 1 | bytes 26280000 | tf_op jit(solution)/shard_map/attend/pallas_call | solution.py:85
  78.0 4.0 collective-permute-done.9.refs_1_
  82.8 3.9 collective-permute-start.11
  91.1 5.8 %collective-permute-done.12.refs_6_.refs_3_.refs_10_ = bf16[128,1024]{1,0:T(8,128)(2,1)S(1)} collective-permute-done((bf16[128,1024]{1,0:T(8,128)(2,1)}, bf16[128,1024]{1,0:T(8,128)(2,1)S(1)}, u32[]{:S(2)}, u32[]{:S(2)}) %collective-permute-start.12) | collective-permute-done | bytes 262176 | tf_op jit(solution)/shard_map/ppermute | solution.py:603
  96.9 4.4 collective-permute-done.11.refs_5_.refs_2_.refs_9_
  102.1 4.3 leave.3
  106.4 9.6 %all-to-all-start = ((bf16[32,48,1024]{2,1,0:T(8,128)(2,1)}), bf16[32,48,1024]{2,1,0:T(8,128)(2,1)}, u32[]{:S(2)}, u32[]{:S(2)}) async-start(bf16[32,48,1024]{2,1,0:T(8,128)(2,1)} %bitcast.29), calls=%async_computation | async-start | bytes 6291456 | tf_op jit(solution)/shard_map/all_to_all | solution.py:654
  118.8 7.1 %attend.3 = (bf16[128,1024]{1,0:T(8,128)(2,1)}, bf16[128,1024]{1,0:T(8,128)(2,1)}, bf16[128,1024]{1,0:T(8,128)(2,1)}, bf16[128,1024]{1,0:T(8,128)(2,1)}, bf16[12...) custom-call(s32[1]{0:T(128)} %bitcast.refs_0_.refs_1_, ...), custom_call_target="tpu_custom_call" | custom-call | flops 1 | bytes 26280000 | tf_op jit(solution)/shard_map/attend/pallas_call | solution.py:85
  128.5 13.5 %collective-permute-done.13.refs_1_ = bf16[128,1024]{1,0:T(8,128)(2,1)S(1)} collective-permute-done((bf16[128,1024]{1,0:T(8,128)(2,1)}, bf16[128,1024]{1,0:T(8,128)(2,1)S(1)}, u32[]{:S(2)}, u32[]{:S(2)}) %collective-permute-start.13) | collective-permute-done | bytes 262176 | tf_op jit(solution)/shard_map/ppermute | solution.py:607
  142.1 6.1 %collective-permute-done.14.refs_2_ = bf16[128,1024]{1,0:T(8,128)(2,1)S(1)} collective-permute-done((bf16[128,1024]{1,0:T(8,128)(2,1)}, bf16[128,1024]{1,0:T(8,128)(2,1)S(1)}, u32[]{:S(2)}, u32[]{:S(2)}) %collective-permute-start.14) | collective-permute-done | bytes 262176 | tf_op jit(solution)/shard_map/ppermute | solution.py:607
  149.2 4.3 leave.2
  155.2 7.4 %all-to-all-start.1 = ((bf16[32,48,1024]{2,1,0:T(8,128)(2,1)}), bf16[32,48,1024]{2,1,0:T(8,128)(2,1)}, u32[]{:S(2)}, u32[]{:S(2)}) async-start(bf16[32,48,1024]{2,1,0:T(8,128)(2,1)} %bitcast.27), calls=%async_computation.1 | async-start | bytes 6291456 | tf_op jit(solution)/shard_map/all_to_all | solution.py:654
  167.0 7.4 %collective-permute-done.21.refs_9_.refs_8_ = bf16[1,3,512,128]{3,2,1,0:T(8,128)(2,1)S(1)} collective-permute-done((bf16[1,3,512,128]{3,2,1,0:T(8,128)(2,1)S(1)}, bf16[1,3,512,128]{3,2,1,0:T(8,128)(2,1)S(1)}, u32[]{:S(2)}, u32[]{:S(2)}) %collective-permute-start.21) | collective-permute-done | bytes 393248 | tf_op jit(solution)/shard_map/ppermute | solution.py:603
  175.5 29.9 %expert.2 = (bf16[32,128,1024]{2,1,0:T(8,128)(2,1)}, bf16[1536,1024]{1,0:T(8,128)(2,1)}, f32[3,1024,512]{2,1,0:T(8,128)}) custom-call(bf16[1536,1024]{1,0:T(8,128)(2,1)} %get-tuple-element.116.refs_0_, s32[1]{0:T(128)} %bitcast.refs_0_.refs_1_, s32[1,32]{1,0:T(1,128)} %bitcast.36, bf16[1536,1024]{1,0:T(8,128)(2,1)} %bitcast.5.refs_3_, ...), custom_call_target="tpu_custom_call" | custom-call | flops 1 | bytes 97200000 | tf_op jit(solution)/shard_map/expert/pallas_call | solution.py:376
  205.4 8.8 %all-to-all-start.2 = ((bf16[32,48,1024]{2,1,0:T(8,128)(2,1)}), bf16[32,48,1024]{2,1,0:T(8,128)(2,1)}, u32[]{:S(2)}, u32[]{:S(2)}) async-start(bf16[32,48,1024]{2,1,0:T(8,128)(2,1)} %bitcast.10), calls=%async_computation.3 | async-start | bytes 6291456 | tf_op jit(solution)/shard_map/all_to_all | solution.py:654
  214.3 29.0 %expert.3 = (bf16[1536,1024]{1,0:T(8,128)(2,1)}, bf16[1536,1024]{1,0:T(8,128)(2,1)}, bf16[4,3,1024,128]{3,2,1,0:T(8,128)(2,1)}) custom-call(s32[1]{0:T(128)} %bitcast.refs_0_.refs_1_, s32[1,32]{1,0:T(1,128)} %bitcast.37, bf16[1536,1024]{1,0:T(8,128)(2,1)} %bitcast.8.refs_2_, bf16[32,2,144,1024]{3,2,1,0:T(8,128)(2,1)} %bitcast.23, ...), custom_call_target="tpu_custom_call" | custom-call | flops 1 | bytes 97200000 | tf_op jit(solution)/shard_map/expert/pallas_call | solution.py:376
  243.3 10.2 %all-to-all-done.2 = bf16[32,48,1024]{2,1,0:T(8,128)(2,1)} async-done(((bf16[32,48,1024]{2,1,0:T(8,128)(2,1)}), bf16[32,48,1024]{2,1,0:T(8,128)(2,1)}, u32[]{:S(2)}, u32[]{:S(2)}) %all-to-all-start.2) | async-done | bytes 3145760 | tf_op jit(solution)/shard_map/all_to_all | solution.py:654
  253.4 7.5 %all-to-all-start.3 = ((bf16[32,48,1024]{2,1,0:T(8,128)(2,1)}), bf16[32,48,1024]{2,1,0:T(8,128)(2,1)}, u32[]{:S(2)}, u32[]{:S(2)}) async-start(bf16[32,48,1024]{2,1,0:T(8,128)(2,1)} %bitcast.26), calls=%async_computation.4 | async-start | bytes 6291456 | tf_op jit(solution)/shard_map/all_to_all | solution.py:654
  269.4 5.3 %collective-permute-done.24.refs_6_ = bf16[128,1024]{1,0:T(8,128)(2,1)S(1)} collective-permute-done((bf16[128,1024]{1,0:T(8,128)(2,1)}, bf16[128,1024]{1,0:T(8,128)(2,1)S(1)}, u32[]{:S(2)}, u32[]{:S(2)}) %collective-permute-start.24) | collective-permute-done | bytes 262176 | tf_op jit(solution)/shard_map/ppermute | solution.py:603
  274.8 6.5 %collective-permute-done.23.refs_5_ = bf16[128,1024]{1,0:T(8,128)(2,1)S(1)} collective-permute-done((bf16[128,1024]{1,0:T(8,128)(2,1)}, bf16[128,1024]{1,0:T(8,128)(2,1)S(1)}, u32[]{:S(2)}, u32[]{:S(2)}) %collective-permute-start.23) | collective-permute-done | bytes 262176 | tf_op jit(solution)/shard_map/ppermute | solution.py:603
  282.0 9.3 %attend_back.2 = (bf16[128,1024]{1,0:T(8,128)(2,1)}, bf16[128,1024]{1,0:T(8,128)(2,1)}, bf16[128,1024]{1,0:T(8,128)(2,1)}, bf16[128,1024]{1,0:T(8,128)(2,1)}, bf...) custom-call(s32[1]{0:T(128)} %bitcast.refs_0_.refs_1_, s32[2,1,2]{2,1,0:T(1,128)} %refs_1_.14, ...), custom_call_target="tpu_custom_call" | custom-call | flops 1 | bytes 39600000 | tf_op jit(solution)/shard_map/attend_back/pallas_call | solution.py:85
  295.1 4.5 %collective-permute-done.25.refs_6_.refs_3_ = bf16[128,1024]{1,0:T(8,128)(2,1)S(1)} collective-permute-done((bf16[128,1024]{1,0:T(8,128)(2,1)}, bf16[128,1024]{1,0:T(8,128)(2,1)S(1)}, u32[]{:S(2)}, u32[]{:S(2)}) %collective-permute-start.25) | collective-permute-done | bytes 262176 | tf_op jit(solution)/shard_map/ppermute | solution.py:607
  299.6 7.3 %collective-permute-done.26.refs_7_.refs_4_ = bf16[128,1024]{1,0:T(8,128)(2,1)S(1)} collective-permute-done((bf16[128,1024]{1,0:T(8,128)(2,1)}, bf16[128,1024]{1,0:T(8,128)(2,1)S(1)}, u32[]{:S(2)}, u32[]{:S(2)}) %collective-permute-start.26) | collective-permute-done | bytes 262176 | tf_op jit(solution)/shard_map/ppermute | solution.py:607
  307.0 6.1 %all-to-all-done.3 = bf16[32,48,1024]{2,1,0:T(8,128)(2,1)} async-done(((bf16[32,48,1024]{2,1,0:T(8,128)(2,1)}), bf16[32,48,1024]{2,1,0:T(8,128)(2,1)}, u32[]{:S(2)}, u32[]{:S(2)}) %all-to-all-start.3) | async-done | bytes 3145760 | tf_op jit(solution)/shard_map/all_to_all | solution.py:654
  316.9 8.3 %all-to-all-start.4 = ((bf16[32,48,1024]{2,1,0:T(8,128)(2,1)}), bf16[32,48,1024]{2,1,0:T(8,128)(2,1)}, u32[]{:S(2)}, u32[]{:S(2)}) async-start(bf16[32,48,1024]{2,1,0:T(8,128)(2,1)} %bitcast.25), calls=%async_computation.5 | async-start | bytes 6291456 | tf_op jit(solution)/shard_map/all_to_all | solution.py:654
  334.1 6.6 %collective-permute-done.29.refs_5_ = bf16[128,1024]{1,0:T(8,128)(2,1)S(1)} collective-permute-done((bf16[128,1024]{1,0:T(8,128)(2,1)S(1)}, bf16[128,1024]{1,0:T(8,128)(2,1)S(1)}, u32[]{:S(2)}, u32[]{:S(2)}) %collective-permute-start.29) | collective-permute-done | bytes 262176 | tf_op jit(solution)/shard_map/ppermute | solution.py:603
  341.5 11.3 %attend_back.3 = (bf16[128,1024]{1,0:T(8,128)(2,1)}, bf16[128,1024]{1,0:T(8,128)(2,1)}, bf16[128,1024]{1,0:T(8,128)(2,1)}, bf16[128,1024]{1,0:T(8,128)(2,1)}, bf...) custom-call(s32[1]{0:T(128)} %bitcast.refs_0_.refs_1_, s32[2,1,2]{2,1,0:T(1,128)} %refs_1_.14, ...), custom_call_target="tpu_custom_call" | custom-call | flops 1 | bytes 39600000 | tf_op jit(solution)/shard_map/attend_back/pallas_call | solution.py:85
  366.2 5.7 %collective-permute-done.36.refs_5_.refs_9_ = bf16[128,1024]{1,0:T(8,128)(2,1)S(1)} collective-permute-done((bf16[128,1024]{1,0:T(8,128)(2,1)}, bf16[128,1024]{1,0:T(8,128)(2,1)S(1)}, u32[]{:S(2)}, u32[]{:S(2)}) %collective-permute-start.36) | collective-permute-done | bytes 262176 | tf_op jit(solution)/shard_map/ppermute | solution.py:607
  390.6 7.1 %collective-permute-done.38.refs_2_ = bf16[448,256]{1,0:T(8,128)(2,1)S(1)} collective-permute-done((bf16[448,256]{1,0:T(8,128)(2,1)S(1)}, bf16[448,256]{1,0:T(8,128)(2,1)S(1)}, u32[]{:S(2)}, u32[]{:S(2)}) %collective-permute-start.38) | collective-permute-done | bytes 229408 | tf_op jit(solution)/shard_map/ppermute | solution.py:642
  431.6 4.8 %finish.1 = (bf16[2,128,1024]{2,1,0:T(8,128)(2,1)}, f32[256,1024]{1,0:T(8,128)}, f32[256,512]{1,0:T(8,128)}, f32[256,512]{1,0:T(8,128)}, f32[256,1024]{1,0:T(8,1...) custom-call(s32[1]{0:T(128)} %bitcast.refs_0_.refs_1_, s32[2,1,512]{2,1,0:T(1,128)} %refs_1_.15, ...), custom_call_target="tpu_custom_call" | custom-call | flops 1 | bytes 19800000 | tf_op jit(solution)/shard_map/finish/pallas_call | solution.py:85
  (209 shorter events, 146.3 us)
Async XLA Ops:
  7.2 167.5 %all-gather.5.cloned.1.call-start = ((), (), s32[]{:S(2)}) async-start(), calls=%async_computation.9 | async-start | bytes 19464192 | tf_op jit(solution)/shard_map/all_gather | solution.py:730
  7.2 15.1 %collective-permute-start.1 = (bf16[2,128,1024]{2,1,0:T(8,128)(2,1)}, bf16[2,128,1024]{2,1,0:T(8,128)(2,1)S(1)}, u32[]{:S(2)}, u32[]{:S(2)}) collective-permute-start(bf16[2,128,1024]{2,1,0:T(8,128)(2,1)} %refs_4_.1), channel_id=1, source_target_pairs={{0,2},{1,3},{2,0},{3,1},{4,6},{5,7},{6,4},{7,5},{8,10},{9,11},{10,... | collective-permute-start | bytes 1572872 | tf_op jit(solution)/shard_map/ppermute | solution.py:603
  10.9 23.2 %collective-permute-start = (bf16[2,128,1024]{2,1,0:T(8,128)(2,1)}, bf16[2,128,1024]{2,1,0:T(8,128)(2,1)}, u32[]{:S(2)}, u32[]{:S(2)}) collective-permute-start(bf16[2,128,1024]{2,1,0:T(8,128)(2,1)} %refs_4_.1), channel_id=1, source_target_pairs={{0,3},{1,0},{2,1},{3,2},{4,7},{5,4},{6,5},{7,6},{8,11},{9,8},{10,9... | collective-permute-start | bytes 1572872 | tf_op jit(solution)/shard_map/ppermute | solution.py:603
  11.7 23.1 %collective-permute-start.2 = (bf16[2,128,1024]{2,1,0:T(8,128)(2,1)}, bf16[2,128,1024]{2,1,0:T(8,128)(2,1)}, u32[]{:S(2)}, u32[]{:S(2)}) collective-permute-start(bf16[2,128,1024]{2,1,0:T(8,128)(2,1)} %refs_4_.1), channel_id=1, source_target_pairs={{0,1},{1,2},{2,3},{3,0},{4,5},{5,6},{6,7},{7,4},{8,9},{9,10},{10,1... | collective-permute-start | bytes 1572872 | tf_op jit(solution)/shard_map/ppermute | solution.py:603
  39.2 26.2 %collective-permute-start.6 = (bf16[272,512]{1,0:T(8,128)(2,1)}, bf16[272,512]{1,0:T(8,128)(2,1)S(1)}, u32[]{:S(2)}, u32[]{:S(2)}) collective-permute-start(bf16[272,512]{1,0:T(8,128)(2,1)} %get-tuple-element.103), channel_id=1, source_target_pairs={{0,3},{1,0},{2,1},{3,2},{4,7},{5,4},{6,5},{7,6},{8,11},{9,8},{10,9... | collective-permute-start | bytes 835592 | tf_op jit(solution)/shard_map/ppermute | solution.py:603
  40.6 24.9 %collective-permute-start.7 = (bf16[272,512]{1,0:T(8,128)(2,1)}, bf16[272,512]{1,0:T(8,128)(2,1)S(1)}, u32[]{:S(2)}, u32[]{:S(2)}) collective-permute-start(bf16[272,512]{1,0:T(8,128)(2,1)} %get-tuple-element.104), channel_id=1, source_target_pairs={{0,2},{1,3},{2,0},{3,1},{4,6},{5,7},{6,4},{7,5},{8,10},{9,11},{10,... | collective-permute-start | bytes 835592 | tf_op jit(solution)/shard_map/ppermute | solution.py:603
  42.2 23.2 %collective-permute-start.8 = (bf16[272,512]{1,0:T(8,128)(2,1)}, bf16[272,512]{1,0:T(8,128)(2,1)S(1)}, u32[]{:S(2)}, u32[]{:S(2)}) collective-permute-start(bf16[272,512]{1,0:T(8,128)(2,1)} %get-tuple-element.105), channel_id=1, source_target_pairs={{0,1},{1,2},{2,3},{3,0},{4,5},{5,6},{6,7},{7,4},{8,9},{9,10},{10,1... | collective-permute-start | bytes 835592 | tf_op jit(solution)/shard_map/ppermute | solution.py:603
  42.5 22.9 %collective-permute-start.4 = (bf16[128,1024]{1,0:T(8,128)(2,1)}, bf16[128,1024]{1,0:T(8,128)(2,1)S(1)}, u32[]{:S(2)}, u32[]{:S(2)}) collective-permute-start(bf16[128,1024]{1,0:T(8,128)(2,1)} %get-tuple-element.101.refs_3_), channel_id=1, source_target_pairs={{0,2},{1,3},{2,0},{3,1},{4,6},{5,7},{6,4},{7,5},{8,10},{9,11},{10,... | collective-permute-start | bytes 786440 | tf_op jit(solution)/shard_map/ppermute | solution.py:603
  46.3 19.1 %collective-permute-start.3 = (bf16[128,1024]{1,0:T(8,128)(2,1)}, bf16[128,1024]{1,0:T(8,128)(2,1)S(1)}, u32[]{:S(2)}, u32[]{:S(2)}) collective-permute-start(bf16[128,1024]{1,0:T(8,128)(2,1)} %get-tuple-element.101.refs_3_), channel_id=1, source_target_pairs={{0,3},{1,0},{2,1},{3,2},{4,7},{5,4},{6,5},{7,6},{8,11},{9,8},{10,9... | collective-permute-start | bytes 786440 | tf_op jit(solution)/shard_map/ppermute | solution.py:603
  74.7 15.4 %collective-permute-start.18 = (bf16[128,1024]{1,0:T(8,128)(2,1)}, bf16[128,1024]{1,0:T(8,128)(2,1)}, u32[]{:S(2)}, u32[]{:S(2)}) collective-permute-start(bf16[128,1024]{1,0:T(8,128)(2,1)} %get-tuple-element.118), channel_id=1, source_target_pairs={{0,2},{1,3},{2,0},{3,1},{4,6},{5,7},{6,4},{7,5},{8,10},{9,11},{10,... | collective-permute-start | bytes 786440 | tf_op jit(solution)/shard_map/ppermute | solution.py:607
  82.8 14.1 %collective-permute-start.12 = (bf16[128,1024]{1,0:T(8,128)(2,1)}, bf16[128,1024]{1,0:T(8,128)(2,1)S(1)}, u32[]{:S(2)}, u32[]{:S(2)}) collective-permute-start(bf16[128,1024]{1,0:T(8,128)(2,1)} %hold.7.refs_3_), channel_id=1, source_target_pairs={{0,1},{1,2},{2,3},{3,0},{4,5},{5,6},{6,7},{7,4},{8,9},{9,10},{10,1... | collective-permute-start | bytes 786440 | tf_op jit(solution)/shard_map/ppermute | solution.py:603
  82.8 18.5 %collective-permute-start.11 = (bf16[128,1024]{1,0:T(8,128)(2,1)}, bf16[128,1024]{1,0:T(8,128)(2,1)S(1)}, u32[]{:S(2)}, u32[]{:S(2)}) collective-permute-start(bf16[128,1024]{1,0:T(8,128)(2,1)} %hold.7.refs_3_), channel_id=1, source_target_pairs={{0,2},{1,3},{2,0},{3,1},{4,6},{5,7},{6,4},{7,5},{8,10},{9,11},{10,... | collective-permute-start | bytes 786440 | tf_op jit(solution)/shard_map/ppermute | solution.py:603
  86.7 14.6 %collective-permute-start.10 = (bf16[128,1024]{1,0:T(8,128)(2,1)}, bf16[128,1024]{1,0:T(8,128)(2,1)S(1)}, u32[]{:S(2)}, u32[]{:S(2)}) collective-permute-start(bf16[128,1024]{1,0:T(8,128)(2,1)} %hold.7.refs_3_), channel_id=1, source_target_pairs={{0,3},{1,0},{2,1},{3,2},{4,7},{5,4},{6,5},{7,6},{8,11},{9,8},{10,9... | collective-permute-start | bytes 786440 | tf_op jit(solution)/shard_map/ppermute | solution.py:603
  106.4 48.9 %all-to-all-start = ((bf16[32,48,1024]{2,1,0:T(8,128)(2,1)}), bf16[32,48,1024]{2,1,0:T(8,128)(2,1)}, u32[]{:S(2)}, u32[]{:S(2)}) async-start(bf16[32,48,1024]{2,1,0:T(8,128)(2,1)} %bitcast.29), calls=%async_computation | async-start | bytes 6291456 | tf_op jit(solution)/shard_map/all_to_all | solution.py:654
  116.0 32.1 %collective-permute-start.17 = (bf16[2,3,512,128]{3,2,1,0:T(8,128)(2,1)}, bf16[2,3,512,128]{3,2,1,0:T(8,128)(2,1)S(1)}, u32[]{:S(2)}, u32[]{:S(2)}) collective-permute-start(bf16[2,3,512,128]{3,2,1,0:T(8,128)(2,1)} %hold.8.refs_5_.refs_4_), channel_id=1, source_target_pairs={{0,1},{1,2},{2,3},{3,0},{4,5},{5,6},{6,7},{7,4},{8,9},{9,10},{10,1... | collective-permute-start | bytes 2359304 | tf_op jit(solution)/shard_map/ppermute | solution.py:603
  116.1 32.1 %collective-permute-start.16 = (bf16[2,3,512,128]{3,2,1,0:T(8,128)(2,1)}, bf16[2,3,512,128]{3,2,1,0:T(8,128)(2,1)}, u32[]{:S(2)}, u32[]{:S(2)}) collective-permute-start(bf16[2,3,512,128]{3,2,1,0:T(8,128)(2,1)} %hold.8.refs_5_.refs_4_), channel_id=1, source_target_pairs={{0,3},{1,0},{2,1},{3,2},{4,7},{5,4},{6,5},{7,6},{8,11},{9,8},{10,9... | collective-permute-start | bytes 2359304 | tf_op jit(solution)/shard_map/ppermute | solution.py:603
  125.8 16.2 %collective-permute-start.13 = (bf16[128,1024]{1,0:T(8,128)(2,1)}, bf16[128,1024]{1,0:T(8,128)(2,1)S(1)}, u32[]{:S(2)}, u32[]{:S(2)}) collective-permute-start(bf16[128,1024]{1,0:T(8,128)(2,1)} %get-tuple-element.111), channel_id=1, source_target_pairs={{0,1},{1,2},{2,3},{3,0},{4,5},{5,6},{6,7},{7,4},{8,9},{9,10},{10,1... | collective-permute-start | bytes 786440 | tf_op jit(solution)/shard_map/ppermute | solution.py:607
  125.9 22.3 %collective-permute-start.14 = (bf16[128,1024]{1,0:T(8,128)(2,1)}, bf16[128,1024]{1,0:T(8,128)(2,1)S(1)}, u32[]{:S(2)}, u32[]{:S(2)}) collective-permute-start(bf16[128,1024]{1,0:T(8,128)(2,1)} %get-tuple-element.112), channel_id=1, source_target_pairs={{0,2},{1,3},{2,0},{3,1},{4,6},{5,7},{6,4},{7,5},{8,10},{9,11},{10,... | collective-permute-start | bytes 786440 | tf_op jit(solution)/shard_map/ppermute | solution.py:607
  127.8 20.4 %collective-permute-start.15 = (bf16[128,1024]{1,0:T(8,128)(2,1)}, bf16[128,1024]{1,0:T(8,128)(2,1)S(1)}, u32[]{:S(2)}, u32[]{:S(2)}) collective-permute-start(bf16[128,1024]{1,0:T(8,128)(2,1)} %get-tuple-element.113), channel_id=1, source_target_pairs={{0,3},{1,0},{2,1},{3,2},{4,7},{5,4},{6,5},{7,6},{8,11},{9,8},{10,9... | collective-permute-start | bytes 786440 | tf_op jit(solution)/shard_map/ppermute | solution.py:607
  155.2 50.2 %all-to-all-start.1 = ((bf16[32,48,1024]{2,1,0:T(8,128)(2,1)}), bf16[32,48,1024]{2,1,0:T(8,128)(2,1)}, u32[]{:S(2)}, u32[]{:S(2)}) async-start(bf16[32,48,1024]{2,1,0:T(8,128)(2,1)} %bitcast.27), calls=%async_computation.1 | async-start | bytes 6291456 | tf_op jit(solution)/shard_map/all_to_all | solution.py:654
  162.6 215.3 %reduce-scatter.3.cloned.1.call-start = ((), (), s32[]{:S(2)}) async-start(), calls=%async_computation.7 | async-start | bytes 8650752 | tf_op jit(solution)/shard_map/reduce_scatter | solution.py:650
  205.4 48.0 %all-to-all-start.2 = ((bf16[32,48,1024]{2,1,0:T(8,128)(2,1)}), bf16[32,48,1024]{2,1,0:T(8,128)(2,1)}, u32[]{:S(2)}, u32[]{:S(2)}) async-start(bf16[32,48,1024]{2,1,0:T(8,128)(2,1)} %bitcast.10), calls=%async_computation.3 | async-start | bytes 6291456 | tf_op jit(solution)/shard_map/all_to_all | solution.py:654
  214.2 191.7 %reduce-scatter.5.cloned.1.call-start = ((), (), s32[]{:S(2)}) async-start(), calls=%async_computation.8 | async-start | bytes 3932160 | tf_op jit(solution)/shard_map/reduce_scatter | solution.py:805
  253.4 59.7 %all-to-all-start.3 = ((bf16[32,48,1024]{2,1,0:T(8,128)(2,1)}), bf16[32,48,1024]{2,1,0:T(8,128)(2,1)}, u32[]{:S(2)}, u32[]{:S(2)}) async-start(bf16[32,48,1024]{2,1,0:T(8,128)(2,1)} %bitcast.26), calls=%async_computation.4 | async-start | bytes 6291456 | tf_op jit(solution)/shard_map/all_to_all | solution.py:654
  265.6 15.7 %collective-permute-start.23 = (bf16[128,1024]{1,0:T(8,128)(2,1)}, bf16[128,1024]{1,0:T(8,128)(2,1)S(1)}, u32[]{:S(2)}, u32[]{:S(2)}) collective-permute-start(bf16[128,1024]{1,0:T(8,128)(2,1)} %get-tuple-element.133.refs_3_), channel_id=1, source_target_pairs={{0,2},{1,3},{2,0},{3,1},{4,6},{5,7},{6,4},{7,5},{8,10},{9,11},{10,... | collective-permute-start | bytes 786440 | tf_op jit(solution)/shard_map/ppermute | solution.py:603
  292.7 14.3 %collective-permute-start.26 = (bf16[128,1024]{1,0:T(8,128)(2,1)}, bf16[128,1024]{1,0:T(8,128)(2,1)S(1)}, u32[]{:S(2)}, u32[]{:S(2)}) collective-permute-start(bf16[128,1024]{1,0:T(8,128)(2,1)} %get-tuple-element.140), channel_id=1, source_target_pairs={{0,2},{1,3},{2,0},{3,1},{4,6},{5,7},{6,4},{7,5},{8,10},{9,11},{10,... | collective-permute-start | bytes 786440 | tf_op jit(solution)/shard_map/ppermute | solution.py:607
  316.9 60.9 %all-to-all-start.4 = ((bf16[32,48,1024]{2,1,0:T(8,128)(2,1)}), bf16[32,48,1024]{2,1,0:T(8,128)(2,1)}, u32[]{:S(2)}, u32[]{:S(2)}) async-start(bf16[32,48,1024]{2,1,0:T(8,128)(2,1)} %bitcast.25), calls=%async_computation.5 | async-start | bytes 6291456 | tf_op jit(solution)/shard_map/all_to_all | solution.py:654
  325.2 105.4 %all-gather.7.cloned.1.call-start = ((), (), s32[]{:S(2)}) async-start(), calls=%async_computation.10 | async-start | bytes 2621440 | tf_op jit(solution)/shard_map/all_gather | solution.py:860
  326.3 14.4 %collective-permute-start.29 = (bf16[128,1024]{1,0:T(8,128)(2,1)S(1)}, bf16[128,1024]{1,0:T(8,128)(2,1)S(1)}, u32[]{:S(2)}, u32[]{:S(2)}) collective-permute-start(bf16[128,1024]{1,0:T(8,128)(2,1)S(1)} %copy-done.11), channel_id=1, source_target_pairs={{0,2},{1,3},{2,0},{3,1},{4,6},{5,7},{6,4},{7,5},{8,10},{9,11},{10,... | collective-permute-start | bytes 786440 | tf_op jit(solution)/shard_map/ppermute | solution.py:603
  355.2 16.7 %collective-permute-start.36 = (bf16[128,1024]{1,0:T(8,128)(2,1)}, bf16[128,1024]{1,0:T(8,128)(2,1)S(1)}, u32[]{:S(2)}, u32[]{:S(2)}) collective-permute-start(bf16[128,1024]{1,0:T(8,128)(2,1)} %get-tuple-element.157), channel_id=1, source_target_pairs={{0,2},{1,3},{2,0},{3,1},{4,6},{5,7},{6,4},{7,5},{8,10},{9,11},{10,... | collective-permute-start | bytes 786440 | tf_op jit(solution)/shard_map/ppermute | solution.py:607
  357.1 17.2 %collective-permute-start.37 = (bf16[128,1024]{1,0:T(8,128)(2,1)}, bf16[128,1024]{1,0:T(8,128)(2,1)}, u32[]{:S(2)}, u32[]{:S(2)}) collective-permute-start(bf16[128,1024]{1,0:T(8,128)(2,1)} %get-tuple-element.158), channel_id=1, source_target_pairs={{0,3},{1,0},{2,1},{3,2},{4,7},{5,4},{6,5},{7,6},{8,11},{9,8},{10,9... | collective-permute-start | bytes 786440 | tf_op jit(solution)/shard_map/ppermute | solution.py:607
  361.1 13.1 %collective-permute-start.32 = (bf16[448,256]{1,0:T(8,128)(2,1)}, bf16[448,256]{1,0:T(8,128)(2,1)S(1)}, u32[]{:S(2)}, u32[]{:S(2)}) collective-permute-start(bf16[448,256]{1,0:T(8,128)(2,1)} %get-tuple-element.153), channel_id=1, source_target_pairs={{0,8},{4,12},{8,16},{12,20},{16,24},{20,28},{24,0},{28,4},{32,40},... | collective-permute-start | bytes 688136 | tf_op jit(solution)/shard_map/ppermute | solution.py:642
  (69 other events, 399.4 us)
Sparse Core Ops, SparseCore 0:
  37.8 80.3 all-gather.4
  205.6 142.2 reduce-scatter.2
  350.4 46.0 reduce-scatter.4
  398.7 31.5 all-gather.6
